TPU v7x, 32 devices: a whole 2x2x4 slice. The times are simulated.
32 devices in a mesh: seq: 2 (over x), ctx: 16 (over z, y, core).
Axes of the slice: x: 2, y: 2, z: 4, core: 2. Of those that a mesh axis runs over, the one named last changes fastest.
Arguments:
- layer_input: bfloat16 [2, 2048, 768], P('seq', 'ctx'), may hold values from -6 to 6
- query_weight: bfloat16 [768, 768], P(('seq', 'ctx')), may hold values from -0.3125 to 0.3125
- query_bias: bfloat16 [768], P(('seq', 'ctx')), may hold values from -3 to 3
- key_weight: bfloat16 [768, 768], P(('seq', 'ctx')), may hold values from -0.3125 to 0.3125
- value_weight: bfloat16 [768, 768], P(('seq', 'ctx')), may hold values from -0.21875 to 0.21875
- value_bias: bfloat16 [768], P(('seq', 'ctx')), may hold values from -3 to 3
- mixer_weight: bfloat16 [768, 768], P(('seq', 'ctx')), may hold values from -1.25 to 1.25
- mixer_bias: bfloat16 [768], P(('seq', 'ctx')), may hold values from -3 to 3
- first_gain: bfloat16 [768], P(('seq', 'ctx')), may hold values from 0.099609375 to 1.8984375
- first_shift: bfloat16 [768], P(('seq', 'ctx')), may hold values from -3 to 3
- inner_weight: bfloat16 [768, 3072], P(('seq', 'ctx')), may hold values from -0.21875 to 0.21875
- inner_bias: bfloat16 [3072], P(('seq', 'ctx')), may hold values from -3 to 3
- outer_weight: bfloat16 [3072, 768], P(('seq', 'ctx')), may hold values from -0.109375 to 0.109375
- outer_bias: bfloat16 [768], P(('seq', 'ctx')), may hold values from -3 to 3
- second_gain: bfloat16 [768], P(('seq', 'ctx')), may hold values from 0.099609375 to 1.8984375
- second_shift: bfloat16 [768], P(('seq', 'ctx')), may hold values from -3 to 3
- head_weight: bfloat16 [768], P(('seq', 'ctx')), may hold values from -0.21875 to 0.21875
- out_cotangent: bfloat16 [2, 2048, 768], P('seq', 'ctx'), may hold values from -6 to 6
- term_cotangent: float32 [2, 2048], P('seq', 'ctx'), may hold values from -6 to 6
Outputs:
- layer_output: bfloat16 [2, 2048, 768], P('seq', 'ctx')
- term_weights: float32 [2, 2048], P('seq', 'ctx')
- input_grad: bfloat16 [2, 2048, 768], P('seq', 'ctx')
- query_weight_grad: float32 [768, 768], P(('seq', 'ctx'))
- query_bias_grad: float32 [768], P(('seq', 'ctx'))
- key_weight_grad: float32 [768, 768], P(('seq', 'ctx'))
- value_weight_grad: float32 [768, 768], P(('seq', 'ctx'))
- value_bias_grad: float32 [768], P(('seq', 'ctx'))
- mixer_weight_grad: float32 [768, 768], P(('seq', 'ctx'))
- mixer_bias_grad: float32 [768], P(('seq', 'ctx'))
- first_gain_grad: float32 [768], P(('seq', 'ctx'))
- first_shift_grad: float32 [768], P(('seq', 'ctx'))
- inner_weight_grad: float32 [768, 3072], P(('seq', 'ctx'))
- inner_bias_grad: float32 [3072], P(('seq', 'ctx'))
- outer_weight_grad: float32 [3072, 768], P(('seq', 'ctx'))
- outer_bias_grad: float32 [768], P(('seq', 'ctx'))
- second_gain_grad: float32 [768], P(('seq', 'ctx'))
- second_shift_grad: float32 [768], P(('seq', 'ctx'))
- head_weight_grad: float32 [768], P(('seq', 'ctx'))
All inputs are finite; a program needn't handle non-finite values.
Results may differ from a plain program's by a relative error of at most 0.025.
Values may be sent and summed in bfloat16 or wider, within the bound.
No kernel may reach another device: no remote copies, remote signals or barrier semaphores. Data moves between devices by JAX's collectives and lax.ppermute only.
A program may use at most 128 MiB of HBM per device.

v0:
```python
import math

import jax
import jax.numpy as jnp
from jax import lax
from jax.sharding import PartitionSpec as P

HEADS = 12
HD = 64


EPSILON = 1e-12
HIGHEST = lax.Precision.HIGHEST
ROOT_HALF = 0.7071067811865476
GAUSS_FACTOR = 0.3989422804014327


def passed_along(block, axis, distance):
    devices = range(lax.axis_size(axis))
    route = [((i - distance) % len(devices), i) for i in devices]
    return lax.ppermute(block, axis, route)


def matmul(left_side, right_side):
    return jnp.dot(left_side, right_side, preferred_element_type=jnp.float32)


def matmul_left(left_side, right_side):
    return lax.dot_general(
        left_side, right_side, (((0,), (0,)), ((), ())), preferred_element_type=jnp.float32
    )


def matmul_right(left_side, right_side):
    return lax.dot_general(
        left_side, right_side, (((1,), (1,)), ((), ())), preferred_element_type=jnp.float32
    )


def norm_forward(residual, norm_gain, norm_shift):
    center = residual - jnp.mean(residual, axis=-1, keepdims=True)
    row_scale = lax.rsqrt(jnp.mean(center * center, axis=-1, keepdims=True) + EPSILON)
    normed = center * row_scale
    return (normed * norm_gain + norm_shift, normed, row_scale)


def norm_backward(grad_out, normed, row_scale, norm_gain):
    grad_normed = grad_out * norm_gain
    grad_residual = row_scale * (
        grad_normed
        - jnp.mean(grad_normed, axis=-1, keepdims=True)
        - normed * jnp.mean(grad_normed * normed, axis=-1, keepdims=True)
    )
    return (grad_residual, jnp.sum(grad_out * normed, axis=0), jnp.sum(grad_out, axis=0))


def gelu_exact(inner_rows):
    return 0.5 * inner_rows * (1.0 + lax.erf(inner_rows * ROOT_HALF))


def gelu_slope(inner_rows):
    return (
        0.5 * (1.0 + lax.erf(inner_rows * ROOT_HALF))
        + inner_rows * jnp.exp(-0.5 * inner_rows * inner_rows) * GAUSS_FACTOR
    )


def soft_plus(logits):
    return jnp.maximum(logits, 0.0) + jnp.log1p(jnp.exp(-jnp.abs(logits)))


def block_grads(queries, grad_context, log_total, row_delta, key_heads, value_heads, scale_factor):
    scores = (
        jnp.einsum("qhd,khd->hqk", queries, key_heads, preferred_element_type=jnp.float32)
        * scale_factor
    )
    prob_rows = jnp.exp(scores - log_total[..., None])
    grad_probs = jnp.einsum(
        "qhd,khd->hqk", grad_context, value_heads, preferred_element_type=jnp.float32
    )
    grad_scores = (prob_rows * (grad_probs - row_delta[..., None]) * scale_factor).astype(
        jnp.bfloat16
    )
    part_queries = jnp.einsum(
        "hqk,khd->qhd", grad_scores, key_heads, preferred_element_type=jnp.float32
    )
    part_keys = jnp.einsum("hqk,qhd->khd", grad_scores, queries, preferred_element_type=jnp.float32)
    part_values = jnp.einsum(
        "hqk,qhd->khd",
        prob_rows.astype(jnp.bfloat16),
        grad_context,
        preferred_element_type=jnp.float32,
    )
    return (part_queries, part_keys, part_values)


def shards(
    layer_input,
    query_weight,
    query_bias,
    key_weight,
    value_weight,
    value_bias,
    mixer_weight,
    mixer_bias,
    first_gain,
    first_shift,
    inner_weight,
    inner_bias,
    outer_weight,
    outer_bias,
    second_gain,
    second_shift,
    head_weight,
    out_cotangent,
    term_cotangent,
):
    (
        full_query,
        full_qbias,
        full_key,
        full_value,
        full_vbias,
        full_mixer,
        full_mbias,
        full_fgain,
        full_fshift,
        full_inner,
        full_ibias,
        full_outer,
        full_obias,
        full_sgain,
        full_sshift,
        full_head,
    ) = (
        lax.all_gather(query_weight, ("seq", "ctx"), axis=0, tiled=True),
        lax.all_gather(query_bias, ("seq", "ctx"), axis=0, tiled=True),
        lax.all_gather(key_weight, ("seq", "ctx"), axis=0, tiled=True),
        lax.all_gather(value_weight, ("seq", "ctx"), axis=0, tiled=True),
        lax.all_gather(value_bias, ("seq", "ctx"), axis=0, tiled=True),
        lax.all_gather(mixer_weight, ("seq", "ctx"), axis=0, tiled=True),
        lax.all_gather(mixer_bias, ("seq", "ctx"), axis=0, tiled=True),
        lax.all_gather(first_gain, ("seq", "ctx"), axis=0, tiled=True),
        lax.all_gather(first_shift, ("seq", "ctx"), axis=0, tiled=True),
        lax.all_gather(inner_weight, ("seq", "ctx"), axis=0, tiled=True),
        lax.all_gather(inner_bias, ("seq", "ctx"), axis=0, tiled=True),
        lax.all_gather(outer_weight, ("seq", "ctx"), axis=0, tiled=True),
        lax.all_gather(outer_bias, ("seq", "ctx"), axis=0, tiled=True),
        lax.all_gather(second_gain, ("seq", "ctx"), axis=0, tiled=True),
        lax.all_gather(second_shift, ("seq", "ctx"), axis=0, tiled=True),
        lax.all_gather(head_weight, ("seq", "ctx"), axis=0, tiled=True),
    )
    inputs = layer_input[0]
    tokens = inputs.shape[0]
    head_count = HEADS
    head_size = HD
    width = head_count * head_size
    scale_factor = 1.0 / math.sqrt(head_size)
    head_shape = (tokens, head_count, head_size)
    queries = (matmul(inputs, full_query) + full_qbias.astype(jnp.float32)).astype(jnp.bfloat16)
    key_rows = matmul(inputs, full_key).astype(jnp.bfloat16)
    value_rows = (matmul(inputs, full_value) + full_vbias.astype(jnp.float32)).astype(jnp.bfloat16)
    query_heads = queries.reshape(head_shape)
    start_sums = (
        jnp.zeros((head_count, tokens, head_size), jnp.float32),
        jnp.full((head_count, tokens), -1e30, jnp.float32),
        jnp.zeros((head_count, tokens), jnp.float32),
    )
    piece_keys = lax.all_gather(key_rows, "ctx", axis=0, tiled=True)
    piece_values = lax.all_gather(value_rows, "ctx", axis=0, tiled=True)
    block_rows = math.gcd(piece_keys.shape[0], tokens)

    def one_block(number, block_state):
        weighted, running, normalizer = block_state
        block_keys = lax.dynamic_slice_in_dim(piece_keys, number * block_rows, block_rows, 0)
        block_values = lax.dynamic_slice_in_dim(piece_values, number * block_rows, block_rows, 0)
        block_keys = block_keys.reshape(block_rows, head_count, head_size)
        block_values = block_values.reshape(block_rows, head_count, head_size)
        scores = (
            jnp.einsum("qhd,khd->hqk", query_heads, block_keys, preferred_element_type=jnp.float32)
            * scale_factor
        )
        newmax = jnp.maximum(running, jnp.max(scores, axis=-1))
        expo_rows = jnp.exp(scores - newmax[..., None])
        factor = jnp.exp(running - newmax)
        normalizer = normalizer * factor + jnp.sum(expo_rows, axis=-1)
        weighted = weighted * factor[..., None] + jnp.einsum(
            "hqk,khd->hqd",
            expo_rows.astype(jnp.bfloat16),
            block_values,
            preferred_element_type=jnp.float32,
        )
        return (weighted, newmax, normalizer)

    weighted, running, normalizer = lax.fori_loop(
        0, piece_keys.shape[0] // block_rows, one_block, start_sums
    )
    log_total = running + jnp.log(normalizer)
    context_exact = jnp.transpose(weighted / normalizer[..., None], (1, 0, 2)).reshape(
        tokens, width
    )
    context = context_exact.astype(jnp.bfloat16)
    attended = matmul(context, full_mixer) + full_mbias.astype(jnp.float32)
    first_rows, first_normed, first_scale = norm_forward(
        inputs.astype(jnp.float32) + attended,
        full_fgain.astype(jnp.float32),
        full_fshift.astype(jnp.float32),
    )
    first_low = first_rows.astype(jnp.bfloat16)
    inner_rows = matmul(first_low, full_inner) + full_ibias.astype(jnp.float32)
    active = gelu_exact(inner_rows).astype(jnp.bfloat16)
    outer_rows = matmul(active, full_outer) + full_obias.astype(jnp.float32)
    final_rows, second_normed, second_scale = norm_forward(
        first_rows + outer_rows, full_sgain.astype(jnp.float32), full_sshift.astype(jnp.float32)
    )
    back_query, back_key, back_value = (full_query, full_key, full_value)
    back_mixer, back_inner, back_outer = (full_mixer, full_inner, full_outer)
    back_fgain, back_sgain, back_head = (full_fgain, full_sgain, full_head)
    head_float = back_head.astype(jnp.float32)
    logits = jnp.dot(final_rows, head_float, precision=HIGHEST)
    term_weights = soft_plus(logits)
    head_slope = term_cotangent[0] * jax.nn.sigmoid(logits)
    grad_final = out_cotangent[0].astype(jnp.float32) + head_slope[:, None] * head_float
    head_grad = jnp.dot(head_slope, final_rows, precision=HIGHEST)
    grad_second, second_gain_grad, second_shift_grad = norm_backward(
        grad_final, second_normed, second_scale, back_sgain.astype(jnp.float32)
    )
    grad_outer = grad_second.astype(jnp.bfloat16)
    outer_bias_grad = jnp.sum(grad_outer.astype(jnp.float32), axis=0)
    outer_weight_grad = matmul_left(active, grad_outer)
    grad_inner = (matmul_right(grad_outer, back_outer) * gelu_slope(inner_rows)).astype(
        jnp.bfloat16
    )
    inner_bias_grad = jnp.sum(grad_inner.astype(jnp.float32), axis=0)
    inner_weight_grad = matmul_left(first_low, grad_inner)
    grad_first = grad_second + matmul_right(grad_inner, back_inner)
    grad_residual, first_gain_grad, first_shift_grad = norm_backward(
        grad_first, first_normed, first_scale, back_fgain.astype(jnp.float32)
    )
    grad_attended = grad_residual.astype(jnp.bfloat16)
    mixer_bias_grad = jnp.sum(grad_attended.astype(jnp.float32), axis=0)
    mixer_weight_grad = matmul_left(context, grad_attended)
    grad_context = matmul_right(grad_attended, back_mixer).astype(jnp.bfloat16)
    row_delta = jnp.transpose(
        jnp.sum((grad_context.astype(jnp.float32) * context_exact).reshape(head_shape), axis=-1)
    )
    cycle_length = lax.axis_size("ctx")
    zero_rows = jnp.zeros((tokens, width), jnp.float32)
    grad_heads = grad_context.reshape(head_shape)

    def key_turn(rotation, cycle_state):
        moving_keys, moving_values, sum_keys, sum_values, sum_queries = cycle_state
        part_queries, part_keys, part_values = block_grads(
            query_heads,
            grad_heads,
            log_total,
            row_delta,
            moving_keys.reshape(head_shape),
            moving_values.reshape(head_shape),
            scale_factor,
        )
        moving_keys, moving_values = passed_along((moving_keys, moving_values), "ctx", 1)
        sum_keys, sum_values = (
            passed_along(
                (sum_keys + part_keys.reshape(tokens, width)).astype(jnp.bfloat16), "ctx", 1
            ).astype(jnp.float32),
            passed_along(
                (sum_values + part_values.reshape(tokens, width)).astype(jnp.bfloat16), "ctx", 1
            ).astype(jnp.float32),
        )
        return (
            moving_keys,
            moving_values,
            sum_keys,
            sum_values,
            sum_queries + part_queries.reshape(tokens, width),
        )

    cycle_state = lax.fori_loop(
        0, cycle_length, key_turn, (key_rows, value_rows, zero_rows, zero_rows, zero_rows)
    )
    sum_keys, sum_values, sum_queries = (cycle_state[2], cycle_state[3], cycle_state[4])
    grad_queries = sum_queries.astype(jnp.bfloat16)
    grad_keys = sum_keys.astype(jnp.bfloat16)
    grad_values = sum_values.astype(jnp.bfloat16)
    query_weight_grad = matmul_left(inputs, grad_queries)
    query_bias_grad = jnp.sum(grad_queries.astype(jnp.float32), axis=0)
    key_weight_grad = matmul_left(inputs, grad_keys)
    value_weight_grad = matmul_left(inputs, grad_values)
    value_bias_grad = jnp.sum(grad_values.astype(jnp.float32), axis=0)
    input_grad = (
        grad_residual
        + matmul_right(grad_queries, back_query)
        + matmul_right(grad_keys, back_key)
        + matmul_right(grad_values, back_value)
    ).astype(jnp.bfloat16)
    owned = (
        lax.psum_scatter(query_weight_grad, ("seq", "ctx"), scatter_dimension=0, tiled=True),
        lax.psum_scatter(query_bias_grad, ("seq", "ctx"), scatter_dimension=0, tiled=True),
        lax.psum_scatter(key_weight_grad, ("seq", "ctx"), scatter_dimension=0, tiled=True),
        lax.psum_scatter(value_weight_grad, ("seq", "ctx"), scatter_dimension=0, tiled=True),
        lax.psum_scatter(value_bias_grad, ("seq", "ctx"), scatter_dimension=0, tiled=True),
        lax.psum_scatter(mixer_weight_grad, ("seq", "ctx"), scatter_dimension=0, tiled=True),
        lax.psum_scatter(mixer_bias_grad, ("seq", "ctx"), scatter_dimension=0, tiled=True),
        lax.psum_scatter(first_gain_grad, ("seq", "ctx"), scatter_dimension=0, tiled=True),
        lax.psum_scatter(first_shift_grad, ("seq", "ctx"), scatter_dimension=0, tiled=True),
        lax.psum_scatter(inner_weight_grad, ("seq", "ctx"), scatter_dimension=0, tiled=True),
        lax.psum_scatter(inner_bias_grad, ("seq", "ctx"), scatter_dimension=0, tiled=True),
        lax.psum_scatter(outer_weight_grad, ("seq", "ctx"), scatter_dimension=0, tiled=True),
        lax.psum_scatter(outer_bias_grad, ("seq", "ctx"), scatter_dimension=0, tiled=True),
        lax.psum_scatter(second_gain_grad, ("seq", "ctx"), scatter_dimension=0, tiled=True),
        lax.psum_scatter(second_shift_grad, ("seq", "ctx"), scatter_dimension=0, tiled=True),
        lax.psum_scatter(head_grad, ("seq", "ctx"), scatter_dimension=0, tiled=True),
    )
    return (
        final_rows.astype(jnp.bfloat16)[None],
        term_weights[None],
        input_grad[None],
        owned[0],
        owned[1],
        owned[2],
        owned[3],
        owned[4],
        owned[5],
        owned[6],
        owned[7],
        owned[8],
        owned[9],
        owned[10],
        owned[11],
        owned[12],
        owned[13],
        owned[14],
        owned[15],
    )


def solution(mesh):
    in_specs = (
        P("seq", "ctx", None),
        P(("seq", "ctx"), None),
        P(("seq", "ctx")),
        P(("seq", "ctx"), None),
        P(("seq", "ctx"), None),
        P(("seq", "ctx")),
        P(("seq", "ctx"), None),
        P(("seq", "ctx")),
        P(("seq", "ctx")),
        P(("seq", "ctx")),
        P(("seq", "ctx"), None),
        P(("seq", "ctx")),
        P(("seq", "ctx"), None),
        P(("seq", "ctx")),
        P(("seq", "ctx")),
        P(("seq", "ctx")),
        P(("seq", "ctx")),
        P("seq", "ctx", None),
        P("seq", "ctx"),
    )
    out_specs = (
        P("seq", "ctx", None),
        P("seq", "ctx"),
        P("seq", "ctx", None),
        P(("seq", "ctx"), None),
        P(("seq", "ctx")),
        P(("seq", "ctx"), None),
        P(("seq", "ctx"), None),
        P(("seq", "ctx")),
        P(("seq", "ctx"), None),
        P(("seq", "ctx")),
        P(("seq", "ctx")),
        P(("seq", "ctx")),
        P(("seq", "ctx"), None),
        P(("seq", "ctx")),
        P(("seq", "ctx"), None),
        P(("seq", "ctx")),
        P(("seq", "ctx")),
        P(("seq", "ctx")),
        P(("seq", "ctx")),
    )
    return jax.shard_map(shards, mesh=mesh, in_specs=in_specs, out_specs=out_specs, check_vma=False)
```

profile of v0, /device:TPU:0, one launch (start us, length us, event | category | flops | bytes accessed | tf_op | source)
XLA Modules:
  0.0 1430.1 jit_solution(3858905203933811925)
XLA Ops:
  9.6 58.3 %all-gather.9.cloned.1.call-done = bf16[768,768]{1,0:T(8,128)(2,1)} async-done(((bf16[24,768]{1,0:T(8,128)(2,1)}), bf16[768,768]{1,0:T(8,128)(2,1)}) %all-gather.9.cloned.1.call-update) | async-done | bytes 1179664 | tf_op jit(solution)/shard_map/all_gather | solution.py:138
  72.8 39.6 %all-reduce.21 = (bf16[768]{0:T(1024)(128)(2,1)S(1)}, bf16[768]{0:T(1024)(128)(2,1)S(1)}, bf16[768]{0:T(1024)(128)(2,1)S(1)}, bf16[768]{0:T(1024)(128)(2,1)S(1)}...) all-reduce(bf16[768]{0:T(1024)(128)(2,1)S(1)} %dynamic-update-slice, ...), channel_id=1, replica_groups=mesh['seq'=2,'ctx'=16] {'seq','ctx'}, use_global_device_ids=true, to_apply=%add.8 | all-reduce | flops 9984 | bytes 39936
  112.4 11.4 all-gather.15.cloned.1.call-done
  134.6 45.2 %all-gather.13.cloned.1.call-done = bf16[768,768]{1,0:T(8,128)(2,1)} async-done(((bf16[24,768]{1,0:T(8,128)(2,1)}), bf16[768,768]{1,0:T(8,128)(2,1)}) %all-gather.13.cloned.1.call-update) | async-done | bytes 1179664 | tf_op jit(solution)/shard_map/all_gather | solution.py:136
  181.5 45.1 %all-gather.11.cloned.1.call-done = bf16[2048,768]{1,0:T(8,128)(2,1)} async-done(((bf16[128,768]{1,0:T(8,128)(2,1)}), bf16[2048,768]{1,0:T(8,128)(2,1)}) %all-gather.11.cloned.1.call-update) | async-done | bytes 3145744 | tf_op jit(solution)/shard_map/all_gather | solution.py:169
  226.6 46.7 %all-gather.17.cloned.1.call-done = bf16[2048,768]{1,0:T(8,128)(2,1)} async-done(((bf16[128,768]{1,0:T(8,128)(2,1)}), bf16[2048,768]{1,0:T(8,128)(2,1)}) %all-gather.17.cloned.1.call-update) | async-done | bytes 3145744 | tf_op jit(solution)/shard_map/all_gather | solution.py:170
  273.3 35.1 %while.37 = (s32[]{:T(128)}, f32[12,128,64]{1,2,0:T(8,128)S(1)}, f32[12,128]{1,0:T(8,128)S(1)}, f32[12,128]{1,0:T(8,128)S(1)}, bf16[2048,768]{1,0:T(8,128)(2,1)}...) while((s32[]{:T(128)}, f32[12,128,64]{1,2,0:T(8,128)S(1)}, ...), condition=%wide.region_3.0_spmd.clone, body=%wide.region_0.0_spmd.clone.sunk | while | flops 51813892 | bytes 5406899 | solution.py:195
  308.7 20.3 %all-gather.19.cloned.1.call-done = bf16[768,768]{1,0:T(8,128)(2,1)} async-done(((bf16[24,768]{1,0:T(8,128)(2,1)}), bf16[768,768]{1,0:T(8,128)(2,1)}) %all-gather.19.cloned.1.call-update) | async-done | bytes 1179664 | tf_op jit(solution)/shard_map/all_gather | solution.py:141
  331.0 63.3 %all-gather.21.cloned.1.call-done = bf16[768,3072]{1,0:T(8,128)(2,1)} async-done(((bf16[24,3072]{1,0:T(8,128)(2,1)}), bf16[768,3072]{1,0:T(8,128)(2,1)}) %all-gather.21.cloned.1.call-update) | async-done | bytes 4718608 | tf_op jit(solution)/shard_map/all_gather | solution.py:145
  397.6 62.0 %all-gather.23.cloned.1.call-done = bf16[3072,768]{1,0:T(8,128)(2,1)} async-done(((bf16[96,768]{1,0:T(8,128)(2,1)}), bf16[3072,768]{1,0:T(8,128)(2,1)}) %all-gather.23.cloned.1.call-update) | async-done | bytes 4718608 | tf_op jit(solution)/shard_map/all_gather | solution.py:147
  474.3 249.9 %while.38 = (s32[]{:T(128)}, bf16[128,768]{0,1:T(8,128)(2,1)}, bf16[128,768]{0,1:T(8,128)(2,1)}, f32[128,768]{0,1:T(8,128)}, f32[128,768]{0,1:T(8,128)S(1)}, /*i...) while((s32[]{:T(128)}, bf16[128,768]{0,1:T(8,128)(2,1)}, ...), condition=%wide.region_14.0_spmd.clone, body=%wide.region_13.0_spmd.clone.sunk | while | flops 128188416 | bytes 14364961 | solution.py:279
  512.3 7.2 collective-permute-done.2
  527.9 7.2 collective-permute-done.2
  543.5 7.2 collective-permute-done.2
  559.0 7.2 collective-permute-done.2
  574.6 7.2 collective-permute-done.2
  590.2 7.2 collective-permute-done.2
  605.8 7.2 collective-permute-done.2
  621.4 7.2 collective-permute-done.2
  637.0 7.2 collective-permute-done.2
  652.5 7.2 collective-permute-done.2
  668.1 7.2 collective-permute-done.2
  683.7 7.2 collective-permute-done.2
  699.3 7.2 collective-permute-done.2
  714.9 7.2 collective-permute-done.2
  758.8 38.3 %all-reduce.20 = (f32[768]{0:T(1024)S(1)}, f32[768]{0:T(1024)S(1)}, f32[768]{0:T(1024)S(1)}, f32[768]{0:T(1024)S(1)}, f32[768]{0:T(1024)S(1)}, /*index=5*/f32[30...) all-reduce(f32[768]{0:T(1024)S(1)} %convert_reduce_fusion.4, ...), channel_id=3, replica_groups=mesh['seq'=2,'ctx'=16] {'seq','ctx'}, use_global_device_ids=true, to_apply=%region_17.0.clone | all-reduce | flops 9984 | bytes 79872
  807.3 20.1 %reduce-scatter.19.cloned.1.call-done = f32[24,768]{1,0:T(8,128)} async-done(((f32[768,768]{1,0:T(8,128)}), f32[24,768]{1,0:T(8,128)}) %reduce-scatter.19.cloned.1.call-update) | async-done | bytes 73744
  827.3 104.6 %reduce-scatter.21.cloned.1.call-done = f32[24,768]{1,0:T(8,128)} async-done(((f32[768,768]{1,0:T(8,128)}), f32[24,768]{1,0:T(8,128)}) %reduce-scatter.21.cloned.1.call-update) | async-done | bytes 73744
  931.9 103.9 %reduce-scatter.23.cloned.1.call-done = f32[24,768]{1,0:T(8,128)} async-done(((f32[768,768]{1,0:T(8,128)}), f32[24,768]{1,0:T(8,128)}) %reduce-scatter.23.cloned.1.call-update) | async-done | bytes 73744
  1035.9 104.6 %reduce-scatter.13.cloned.1.call-done = f32[24,768]{1,0:T(8,128)} async-done(((f32[768,768]{1,0:T(8,128)}), f32[24,768]{1,0:T(8,128)}) %reduce-scatter.13.cloned.1.call-update) | async-done | bytes 73744 | tf_op jit(solution)/shard_map/reduce_scatter | solution.py:303
  1140.5 141.0 %reduce-scatter.15.cloned.1.call-done = f32[24,3072]{1,0:T(8,128)} async-done(((f32[768,3072]{1,0:T(8,128)}), f32[24,3072]{1,0:T(8,128)}) %reduce-scatter.15.cloned.1.call-update) | async-done | bytes 294928 | tf_op jit(solution)/shard_map/reduce_scatter | solution.py:307
  1281.5 142.1 %reduce-scatter.17.cloned.1.call-done = f32[96,768]{1,0:T(8,128)} async-done(((f32[3072,768]{1,0:T(8,128)}), f32[96,768]{1,0:T(8,128)}) %reduce-scatter.17.cloned.1.call-update) | async-done | bytes 294928 | tf_op jit(solution)/shard_map/reduce_scatter | solution.py:309
  (690 shorter events, 265.8 us)
Async XLA Ops:
  7.3 60.6 %all-gather.9.cloned.1.call-start = ((), (), s32[]{:S(2)}) async-start(), calls=%async_computation.6 | async-start | bytes 1216512 | tf_op jit(solution)/shard_map/all_gather | solution.py:138
  8.0 115.8 %all-gather.15.cloned.1.call-start = ((), (), s32[]{:S(2)}) async-start(), calls=%async_computation.9 | async-start | bytes 1216512 | tf_op jit(solution)/shard_map/all_gather | solution.py:139
  8.8 171.0 %all-gather.13.cloned.1.call-start = ((), (), s32[]{:S(2)}) async-start(), calls=%async_computation.8 | async-start | bytes 1216512 | tf_op jit(solution)/shard_map/all_gather | solution.py:136
  9.5 217.0 %all-gather.11.cloned.1.call-start = ((), (), s32[]{:S(2)}) async-start(), calls=%async_computation.7 | async-start | bytes 3342336 | tf_op jit(solution)/shard_map/all_gather | solution.py:169
  70.3 203.0 %all-gather.17.cloned.1.call-start = ((), (), s32[]{:S(2)}) async-start(), calls=%async_computation.10 | async-start | bytes 3342336 | tf_op jit(solution)/shard_map/all_gather | solution.py:170
  126.1 202.9 %all-gather.19.cloned.1.call-start = ((), (), s32[]{:S(2)}) async-start(), calls=%async_computation.11 | async-start | bytes 1216512 | tf_op jit(solution)/shard_map/all_gather | solution.py:141
  126.7 267.7 %all-gather.21.cloned.1.call-start = ((), (), s32[]{:S(2)}) async-start(), calls=%async_computation.12 | async-start | bytes 4866048 | tf_op jit(solution)/shard_map/all_gather | solution.py:145
  127.4 332.2 %all-gather.23.cloned.1.call-start = ((), (), s32[]{:S(2)}) async-start(), calls=%async_computation.13 | async-start | bytes 4866048 | tf_op jit(solution)/shard_map/all_gather | solution.py:147
  128.2 699.2 %reduce-scatter.19.cloned.1.call-start = ((), (), s32[]{:S(2)}) async-start(), calls=%async_computation.17 | async-start | bytes 2433024
  475.2 15.2 %collective-permute-start = (bf16[128,768]{0,1:T(8,128)(2,1)S(1)}, bf16[128,768]{0,1:T(8,128)(2,1)}, u32[]{:S(2)}, u32[]{:S(2)}) collective-permute-start(bf16[128,768]{0,1:T(8,128)(2,1)S(1)} %copy.116), channel_id=1, source_target_pairs={{15,0},{0,1},{1,2},{2,3},{3,4},{4,5},{5,6},{6,7},{7,8},{8,9},{9,10... | collective-permute-start | bytes 589832 | tf_op jit(solution)/shard_map/while/body/eval_jaxpr/ppermute | solution.py:21
  476.4 14.0 collective-permute-start.1
  491.4 14.6 %collective-permute-start = (bf16[128,768]{0,1:T(8,128)(2,1)S(1)}, bf16[128,768]{0,1:T(8,128)(2,1)}, u32[]{:S(2)}, u32[]{:S(2)}) collective-permute-start(bf16[128,768]{0,1:T(8,128)(2,1)S(1)} %copy.116), channel_id=1, source_target_pairs={{15,0},{0,1},{1,2},{2,3},{3,4},{4,5},{5,6},{6,7},{7,8},{8,9},{9,10... | collective-permute-start | bytes 589832 | tf_op jit(solution)/shard_map/while/body/eval_jaxpr/ppermute | solution.py:21
  492.3 13.7 collective-permute-start.1
  507.0 14.6 %collective-permute-start = (bf16[128,768]{0,1:T(8,128)(2,1)S(1)}, bf16[128,768]{0,1:T(8,128)(2,1)}, u32[]{:S(2)}, u32[]{:S(2)}) collective-permute-start(bf16[128,768]{0,1:T(8,128)(2,1)S(1)} %copy.116), channel_id=1, source_target_pairs={{15,0},{0,1},{1,2},{2,3},{3,4},{4,5},{5,6},{6,7},{7,8},{8,9},{9,10... | collective-permute-start | bytes 589832 | tf_op jit(solution)/shard_map/while/body/eval_jaxpr/ppermute | solution.py:21
  522.6 14.6 %collective-permute-start = (bf16[128,768]{0,1:T(8,128)(2,1)S(1)}, bf16[128,768]{0,1:T(8,128)(2,1)}, u32[]{:S(2)}, u32[]{:S(2)}) collective-permute-start(bf16[128,768]{0,1:T(8,128)(2,1)S(1)} %copy.116), channel_id=1, source_target_pairs={{15,0},{0,1},{1,2},{2,3},{3,4},{4,5},{5,6},{6,7},{7,8},{8,9},{9,10... | collective-permute-start | bytes 589832 | tf_op jit(solution)/shard_map/while/body/eval_jaxpr/ppermute | solution.py:21
  538.2 14.6 %collective-permute-start = (bf16[128,768]{0,1:T(8,128)(2,1)S(1)}, bf16[128,768]{0,1:T(8,128)(2,1)}, u32[]{:S(2)}, u32[]{:S(2)}) collective-permute-start(bf16[128,768]{0,1:T(8,128)(2,1)S(1)} %copy.116), channel_id=1, source_target_pairs={{15,0},{0,1},{1,2},{2,3},{3,4},{4,5},{5,6},{6,7},{7,8},{8,9},{9,10... | collective-permute-start | bytes 589832 | tf_op jit(solution)/shard_map/while/body/eval_jaxpr/ppermute | solution.py:21
  553.7 14.6 %collective-permute-start = (bf16[128,768]{0,1:T(8,128)(2,1)S(1)}, bf16[128,768]{0,1:T(8,128)(2,1)}, u32[]{:S(2)}, u32[]{:S(2)}) collective-permute-start(bf16[128,768]{0,1:T(8,128)(2,1)S(1)} %copy.116), channel_id=1, source_target_pairs={{15,0},{0,1},{1,2},{2,3},{3,4},{4,5},{5,6},{6,7},{7,8},{8,9},{9,10... | collective-permute-start | bytes 589832 | tf_op jit(solution)/shard_map/while/body/eval_jaxpr/ppermute | solution.py:21
  569.3 14.6 %collective-permute-start = (bf16[128,768]{0,1:T(8,128)(2,1)S(1)}, bf16[128,768]{0,1:T(8,128)(2,1)}, u32[]{:S(2)}, u32[]{:S(2)}) collective-permute-start(bf16[128,768]{0,1:T(8,128)(2,1)S(1)} %copy.116), channel_id=1, source_target_pairs={{15,0},{0,1},{1,2},{2,3},{3,4},{4,5},{5,6},{6,7},{7,8},{8,9},{9,10... | collective-permute-start | bytes 589832 | tf_op jit(solution)/shard_map/while/body/eval_jaxpr/ppermute | solution.py:21
  584.9 14.6 %collective-permute-start = (bf16[128,768]{0,1:T(8,128)(2,1)S(1)}, bf16[128,768]{0,1:T(8,128)(2,1)}, u32[]{:S(2)}, u32[]{:S(2)}) collective-permute-start(bf16[128,768]{0,1:T(8,128)(2,1)S(1)} %copy.116), channel_id=1, source_target_pairs={{15,0},{0,1},{1,2},{2,3},{3,4},{4,5},{5,6},{6,7},{7,8},{8,9},{9,10... | collective-permute-start | bytes 589832 | tf_op jit(solution)/shard_map/while/body/eval_jaxpr/ppermute | solution.py:21
  600.5 14.6 %collective-permute-start = (bf16[128,768]{0,1:T(8,128)(2,1)S(1)}, bf16[128,768]{0,1:T(8,128)(2,1)}, u32[]{:S(2)}, u32[]{:S(2)}) collective-permute-start(bf16[128,768]{0,1:T(8,128)(2,1)S(1)} %copy.116), channel_id=1, source_target_pairs={{15,0},{0,1},{1,2},{2,3},{3,4},{4,5},{5,6},{6,7},{7,8},{8,9},{9,10... | collective-permute-start | bytes 589832 | tf_op jit(solution)/shard_map/while/body/eval_jaxpr/ppermute | solution.py:21
  616.1 14.6 %collective-permute-start = (bf16[128,768]{0,1:T(8,128)(2,1)S(1)}, bf16[128,768]{0,1:T(8,128)(2,1)}, u32[]{:S(2)}, u32[]{:S(2)}) collective-permute-start(bf16[128,768]{0,1:T(8,128)(2,1)S(1)} %copy.116), channel_id=1, source_target_pairs={{15,0},{0,1},{1,2},{2,3},{3,4},{4,5},{5,6},{6,7},{7,8},{8,9},{9,10... | collective-permute-start | bytes 589832 | tf_op jit(solution)/shard_map/while/body/eval_jaxpr/ppermute | solution.py:21
  631.7 14.6 %collective-permute-start = (bf16[128,768]{0,1:T(8,128)(2,1)S(1)}, bf16[128,768]{0,1:T(8,128)(2,1)}, u32[]{:S(2)}, u32[]{:S(2)}) collective-permute-start(bf16[128,768]{0,1:T(8,128)(2,1)S(1)} %copy.116), channel_id=1, source_target_pairs={{15,0},{0,1},{1,2},{2,3},{3,4},{4,5},{5,6},{6,7},{7,8},{8,9},{9,10... | collective-permute-start | bytes 589832 | tf_op jit(solution)/shard_map/while/body/eval_jaxpr/ppermute | solution.py:21
  647.2 14.6 %collective-permute-start = (bf16[128,768]{0,1:T(8,128)(2,1)S(1)}, bf16[128,768]{0,1:T(8,128)(2,1)}, u32[]{:S(2)}, u32[]{:S(2)}) collective-permute-start(bf16[128,768]{0,1:T(8,128)(2,1)S(1)} %copy.116), channel_id=1, source_target_pairs={{15,0},{0,1},{1,2},{2,3},{3,4},{4,5},{5,6},{6,7},{7,8},{8,9},{9,10... | collective-permute-start | bytes 589832 | tf_op jit(solution)/shard_map/while/body/eval_jaxpr/ppermute | solution.py:21
  662.8 14.6 %collective-permute-start = (bf16[128,768]{0,1:T(8,128)(2,1)S(1)}, bf16[128,768]{0,1:T(8,128)(2,1)}, u32[]{:S(2)}, u32[]{:S(2)}) collective-permute-start(bf16[128,768]{0,1:T(8,128)(2,1)S(1)} %copy.116), channel_id=1, source_target_pairs={{15,0},{0,1},{1,2},{2,3},{3,4},{4,5},{5,6},{6,7},{7,8},{8,9},{9,10... | collective-permute-start | bytes 589832 | tf_op jit(solution)/shard_map/while/body/eval_jaxpr/ppermute | solution.py:21
  678.4 14.6 %collective-permute-start = (bf16[128,768]{0,1:T(8,128)(2,1)S(1)}, bf16[128,768]{0,1:T(8,128)(2,1)}, u32[]{:S(2)}, u32[]{:S(2)}) collective-permute-start(bf16[128,768]{0,1:T(8,128)(2,1)S(1)} %copy.116), channel_id=1, source_target_pairs={{15,0},{0,1},{1,2},{2,3},{3,4},{4,5},{5,6},{6,7},{7,8},{8,9},{9,10... | collective-permute-start | bytes 589832 | tf_op jit(solution)/shard_map/while/body/eval_jaxpr/ppermute | solution.py:21
  694.0 14.6 %collective-permute-start = (bf16[128,768]{0,1:T(8,128)(2,1)S(1)}, bf16[128,768]{0,1:T(8,128)(2,1)}, u32[]{:S(2)}, u32[]{:S(2)}) collective-permute-start(bf16[128,768]{0,1:T(8,128)(2,1)S(1)} %copy.116), channel_id=1, source_target_pairs={{15,0},{0,1},{1,2},{2,3},{3,4},{4,5},{5,6},{6,7},{7,8},{8,9},{9,10... | collective-permute-start | bytes 589832 | tf_op jit(solution)/shard_map/while/body/eval_jaxpr/ppermute | solution.py:21
  709.6 14.6 %collective-permute-start = (bf16[128,768]{0,1:T(8,128)(2,1)S(1)}, bf16[128,768]{0,1:T(8,128)(2,1)}, u32[]{:S(2)}, u32[]{:S(2)}) collective-permute-start(bf16[128,768]{0,1:T(8,128)(2,1)S(1)} %copy.116), channel_id=1, source_target_pairs={{15,0},{0,1},{1,2},{2,3},{3,4},{4,5},{5,6},{6,7},{7,8},{8,9},{9,10... | collective-permute-start | bytes 589832 | tf_op jit(solution)/shard_map/while/body/eval_jaxpr/ppermute | solution.py:21
  730.1 201.8 %reduce-scatter.21.cloned.1.call-start = ((), (), s32[]{:S(2)}) async-start(), calls=%async_computation.18 | async-start | bytes 2433024
  736.1 299.7 %reduce-scatter.23.cloned.1.call-start = ((), (), s32[]{:S(2)}) async-start(), calls=%async_computation.19 | async-start | bytes 2433024
  741.5 399.0 %reduce-scatter.13.cloned.1.call-start = ((), (), s32[]{:S(2)}) async-start(), calls=%async_computation.14 | async-start | bytes 2433024 | tf_op jit(solution)/shard_map/reduce_scatter | solution.py:303
  744.4 537.1 %reduce-scatter.15.cloned.1.call-start = ((), (), s32[]{:S(2)}) async-start(), calls=%async_computation.15 | async-start | bytes 9732096 | tf_op jit(solution)/shard_map/reduce_scatter | solution.py:307
  750.7 672.9 %reduce-scatter.17.cloned.1.call-start = ((), (), s32[]{:S(2)}) async-start(), calls=%async_computation.16 | async-start | bytes 9732096 | tf_op jit(solution)/shard_map/reduce_scatter | solution.py:309
  (105 other events, 1713.7 us)
Sparse Core Ops, SparseCore 0:
  11.0 56.7 all-gather.8
  70.8 52.9 all-gather.14
  126.7 52.9 all-gather.12
  182.4 44.0 all-gather.10
  229.3 43.9 all-gather.16
  276.1 52.9 all-gather.18
  331.9 62.3 all-gather.20
  397.3 62.3 all-gather.22
  730.2 97.0 reduce-scatter.18
  833.9 98.0 reduce-scatter.20
  937.8 98.0 reduce-scatter.22
  1042.4 97.9 reduce-scatter.12
  1146.9 134.5 reduce-scatter.14
  1288.8 134.7 reduce-scatter.16
where the time goes:
time: 1430 us
  waiting for transfers between devices  1110 us (78%)
  matrix products  90.8 us (6%)
  local copies, waits for them, and re-layouts  79.6 us (6%)
  blocking collectives  77.9 us (5%)
  other arithmetic  52 us (4%)
  between operations  14.6 us (1%)
    unnamed x17, waiting for transfers between devices  233 us
    reduce_scatter x1, waiting for transfers between devices, shards(): lax.psum_scatter(outer_weight_grad, ('seq', 'ctx'), scatter_dimension=0,...  142 us
    reduce_scatter x1, waiting for transfers between devices, shards(): lax.psum_scatter(inner_weight_grad, ('seq', 'ctx'), scatter_dimension=0,...  141 us
    ppermute x64, waiting for transfers between devices, passed_along(): return lax.ppermute(block, axis, route)  133 us
    reduce_scatter x1, waiting for transfers between devices, shards(): lax.psum_scatter(mixer_weight_grad, ('seq', 'ctx'), scatter_dimension=0,...  105 us
    unnamed x2, blocking collectives  77.9 us
    all_gather x1, waiting for transfers between devices, shards(): lax.all_gather(inner_weight, ('seq', 'ctx'), axis=0, tiled=True)  63.3 us
    all_gather x1, waiting for transfers between devices, shards(): lax.all_gather(outer_weight, ('seq', 'ctx'), axis=0, tiled=True)  62 us
  transfers between devices with their start and end apart: 78, of which 46 were waited for; matrix products, arithmetic and copies ran while one was open for 13% of the time, Pallas kernels for 0%

commit v1 on v0

v1 whole, which is shorter than its diff:
```python
import functools
import math

import jax
import jax.numpy as jnp
from jax import lax
from jax.experimental import pallas as pl
from jax.experimental.pallas import tpu as pltpu
from jax.sharding import PartitionSpec as P

HEADS = 12
HD = 64
WIDTH = HEADS * HD
HALF = WIDTH // 2
NH = HEADS // 2
EPSILON = 1e-12
ROOT_HALF = 0.7071067811865476
GAUSS_FACTOR = 0.3989422804014327
F32 = jnp.float32
BF16 = jnp.bfloat16
AUX = 128


def mm(a, b):
    return lax.dot_general(a, b, (((1,), (0,)), ((), ())), preferred_element_type=F32)


def mm_t(a, b):
    return lax.dot_general(a, b, (((1,), (1,)), ((), ())), preferred_element_type=F32)


def t_mm(a, b):
    return lax.dot_general(a, b, (((0,), (0,)), ((), ())), preferred_element_type=F32)


def swap_ctx(value, bit):
    n = lax.axis_size("ctx")
    return lax.ppermute(value, "ctx", [(i, i ^ bit) for i in range(n)])


def swap_core(value):
    return swap_ctx(value, 1)


def swap_y(value):
    return swap_ctx(value, 2)


def swap_x(value):
    return lax.ppermute(value, "seq", [(0, 1), (1, 0)])


def shift_z(value, k):
    n = lax.axis_size("ctx")
    return lax.ppermute(value, "ctx", [(i, (i + 4 * k) % n) for i in range(n)])


def pair(bit, own, other, axis=0):
    first = jnp.where(bit == 0, own, other)
    second = jnp.where(bit == 0, other, own)
    return jnp.stack([first, second], axis=axis)


def pick(value, index, axis):
    return lax.dynamic_index_in_dim(value, index, axis, keepdims=False)


def gather_chips(block, x, y, z):
    zs = lax.axis_size("ctx") // 4
    rows, cols = block.shape
    along = jnp.zeros((zs, rows, cols), block.dtype)
    for k in range(zs):
        piece = block if k == 0 else shift_z(block, k)
        along = lax.dynamic_update_slice(along, piece[None], ((z - k) % zs, 0, 0))
    both = pair(y, along, swap_y(along), axis=1)
    full = pair(x, both, swap_x(both), axis=0)
    return full.reshape(4 * zs * rows, cols)


def scatter_chips(part, x, y, z):
    zs = lax.axis_size("ctx") // 4
    cols = part.shape[1]
    part = part.reshape(2, -1, cols)
    got = swap_x(pick(part, 1 - x, 0).astype(BF16))
    part = pick(part, x, 0) + got.astype(F32)
    part = part.reshape(zs, 2, -1, cols)
    got = swap_y(pick(part, 1 - y, 1).astype(BF16))
    part = pick(part, y, 1) + got.astype(F32)
    total = pick(part, z, 0)
    for k in range(1, zs):
        total = total + shift_z(pick(part, (z + k) % zs, 0).astype(BF16), k).astype(F32)
    return total


def attend_kernel(q_ref, kv_ref, o_ref, lse_ref, m_s, l_s, acc_s):
    step = pl.program_id(0)

    @pl.when(step == 0)
    def _():
        m_s[...] = jnp.full(m_s.shape, -1e30, F32)
        l_s[...] = jnp.zeros(l_s.shape, F32)
        acc_s[...] = jnp.zeros(acc_s.shape, F32)

    for h in range(NH):
        lo = h * HD
        qh = q_ref[:, lo : lo + HD]
        kh = kv_ref[:, lo : lo + HD]
        vh = kv_ref[:, HALF + lo : HALF + lo + HD]
        s = mm_t(kh, qh)
        before = m_s[h : h + 1, :]
        top = jnp.maximum(before, jnp.max(s, axis=0, keepdims=True))
        p = jnp.exp(s - top)
        factor = jnp.exp(before - top)
        m_s[h : h + 1, :] = top
        l_s[h : h + 1, :] = l_s[h : h + 1, :] * factor + jnp.sum(p, axis=0, keepdims=True)
        acc_s[lo : lo + HD, :] = acc_s[lo : lo + HD, :] * factor + t_mm(vh, p.astype(BF16))

    @pl.when(step == pl.num_programs(0) - 1)
    def _():
        lse_ref[...] = m_s[...] + jnp.log(l_s[...])
        for h in range(NH):
            lo = h * HD
            o_ref[lo : lo + HD, :] = acc_s[lo : lo + HD, :] / l_s[h : h + 1, :]


def attend(q, kv):
    tokens = q.shape[0]
    keys = kv.shape[0]
    block = math.gcd(keys, 1024)
    return pl.pallas_call(
        attend_kernel,
        grid=(keys // block,),
        in_specs=[
            pl.BlockSpec((tokens, HALF), lambda i: (0, 0)),
            pl.BlockSpec((block, WIDTH), lambda i: (i, 0)),
        ],
        out_specs=[
            pl.BlockSpec((HALF, tokens), lambda i: (0, 0)),
            pl.BlockSpec((8, tokens), lambda i: (0, 0)),
        ],
        out_shape=[
            jax.ShapeDtypeStruct((HALF, tokens), F32),
            jax.ShapeDtypeStruct((8, tokens), F32),
        ],
        scratch_shapes=[
            pltpu.VMEM((8, tokens), F32),
            pltpu.VMEM((8, tokens), F32),
            pltpu.VMEM((HALF, tokens), F32),
        ],
        compiler_params=pltpu.CompilerParams(vmem_limit_bytes=40 * 2**20),
        cost_estimate=pl.CostEstimate(
            flops=4 * tokens * keys * HALF,
            bytes_accessed=2 * keys * WIDTH,
            transcendentals=tokens * keys * NH,
        ),
    )(q, kv)


def attend_back_kernel(q_ref, g_ref, o_ref, lse_ref, kv_ref, dq_ref, dkv_ref, delta_s, acc_s):
    step = pl.program_id(0)

    @pl.when(step == 0)
    def _():
        acc_s[...] = jnp.zeros(acc_s.shape, F32)
        prod = jnp.transpose(g_ref[...].astype(F32)) * o_ref[...]
        for h in range(NH):
            delta_s[h : h + 1, :] = jnp.sum(prod[h * HD : (h + 1) * HD, :], axis=0, keepdims=True)

    held = []
    for h in range(NH):
        lo = h * HD
        qh = q_ref[:, lo : lo + HD]
        gh = g_ref[:, lo : lo + HD]
        kh = kv_ref[:, lo : lo + HD]
        vh = kv_ref[:, HALF + lo : HALF + lo + HD]
        p = jnp.exp(mm_t(kh, qh) - lse_ref[h : h + 1, :])
        dp = mm_t(vh, gh)
        ds = (p * (dp - delta_s[h : h + 1, :])).astype(BF16)
        acc_s[lo : lo + HD, :] += t_mm(kh, ds)
        held.append((mm(ds, qh).astype(BF16), mm(p.astype(BF16), gh).astype(BF16)))
        if h % 2 == 1:
            (dk0, dv0), (dk1, dv1) = held
            held = []
            at = lo - HD
            dkv_ref[:, at : at + 2 * HD] = jnp.concatenate([dk0, dk1], axis=1)
            dkv_ref[:, HALF + at : HALF + at + 2 * HD] = jnp.concatenate([dv0, dv1], axis=1)

    @pl.when(step == pl.num_programs(0) - 1)
    def _():
        dq_ref[...] = jnp.transpose(acc_s[...] * 0.125).astype(BF16)


def attend_back(q, g, o, lse, kv):
    tokens = q.shape[0]
    keys = kv.shape[0]
    block = math.gcd(keys, 1024)
    whole = lambda i: (0, 0)
    return pl.pallas_call(
        attend_back_kernel,
        grid=(keys // block,),
        in_specs=[
            pl.BlockSpec((tokens, HALF), whole),
            pl.BlockSpec((tokens, HALF), whole),
            pl.BlockSpec((HALF, tokens), whole),
            pl.BlockSpec((8, tokens), whole),
            pl.BlockSpec((block, WIDTH), lambda i: (i, 0)),
        ],
        out_specs=[
            pl.BlockSpec((tokens, HALF), whole),
            pl.BlockSpec((block, WIDTH), lambda i: (i, 0)),
        ],
        out_shape=[
            jax.ShapeDtypeStruct((tokens, HALF), BF16),
            jax.ShapeDtypeStruct((keys, WIDTH), BF16),
        ],
        scratch_shapes=[
            pltpu.VMEM((8, tokens), F32),
            pltpu.VMEM((HALF, tokens), F32),
        ],
        compiler_params=pltpu.CompilerParams(vmem_limit_bytes=48 * 2**20),
        cost_estimate=pl.CostEstimate(
            flops=10 * tokens * keys * HALF,
            bytes_accessed=4 * keys * WIDTH,
            transcendentals=tokens * keys * NH,
        ),
    )(q, g, o, lse, kv)


def norm_forward(residual, gain, shift):
    center = residual - jnp.mean(residual, axis=-1, keepdims=True)
    scale = lax.rsqrt(jnp.mean(center * center, axis=-1, keepdims=True) + EPSILON)
    normed = center * scale
    return normed * gain + shift, normed, scale


def norm_backward(grad_out, normed, scale, gain):
    grad_normed = grad_out * gain
    return scale * (
        grad_normed
        - jnp.mean(grad_normed, axis=-1, keepdims=True)
        - normed * jnp.mean(grad_normed * normed, axis=-1, keepdims=True)
    )


def gelu_pair(u):
    cdf = 0.5 * (1.0 + lax.erf(u * ROOT_HALF))
    return u * cdf, cdf + u * jnp.exp(-0.5 * u * u) * GAUSS_FACTOR


def soft_plus(logits):
    return jnp.maximum(logits, 0.0) + jnp.log1p(jnp.exp(-jnp.abs(logits)))


def shards(
    layer_input,
    query_weight,
    query_bias,
    key_weight,
    value_weight,
    value_bias,
    mixer_weight,
    mixer_bias,
    first_gain,
    first_shift,
    inner_weight,
    inner_bias,
    outer_weight,
    outer_bias,
    second_gain,
    second_shift,
    head_weight,
    out_cotangent,
    term_cotangent,
):
    n = lax.axis_size("ctx")
    zs = n // 4
    chips = n
    x = lax.axis_index("seq")
    at = lax.axis_index("ctx")
    z, y, core = at // 4, (at // 2) % 2, at % 2
    inputs = layer_input[0]
    tokens = inputs.shape[0]
    rows = query_weight.shape[0]
    hidden = outer_weight.shape[0]
    ff = inner_weight.shape[1]

    def pair_core(own, other, axis=0):
        return pair(core, own, other, axis)

    inputs2 = pair_core(inputs, swap_core(inputs)).reshape(2 * tokens, WIDTH)

    vectors = jnp.stack(
        [
            query_bias,
            value_bias,
            mixer_bias,
            first_gain,
            first_shift,
            outer_bias,
            second_gain,
            second_shift,
            head_weight,
        ],
        axis=1,
    )
    aux = jnp.concatenate([vectors, inner_bias.reshape(rows, hidden // rows)], axis=1)
    aux = jnp.pad(aux, ((0, 0), (0, AUX - aux.shape[1])))
    qkv = jnp.stack([query_weight, key_weight, value_weight]).reshape(3, rows, 2, HALF)

    def qkv_of(side):
        part = jnp.transpose(pick(qkv, side, 2), (1, 0, 2)).reshape(rows, 3 * HALF)
        return jnp.concatenate([part, aux], axis=1)

    qkv_block = pair_core(qkv_of(core), swap_core(qkv_of(1 - core)))
    qkv_full = gather_chips(qkv_block.reshape(2 * rows, 3 * HALF + AUX), x, y, z)
    w_qkv = qkv_full[:, : 3 * HALF]
    aux_full = qkv_full[:, 3 * HALF :]

    inner_split = inner_weight.reshape(rows, chips, 2, hidden)

    def inner_of(side):
        return pick(inner_split, side, 2).reshape(rows, ff // 2)

    inner_block = pair_core(inner_of(core), swap_core(inner_of(1 - core)))
    w_inner = gather_chips(inner_block.reshape(2 * rows, ff // 2), x, y, z)
    w_outer = gather_chips(outer_weight, x, y, z)
    mixer_half = gather_chips(mixer_weight, x, y, z).reshape(chips, rows, WIDTH)
    w_mixer = pair_core(mixer_half, swap_core(mixer_half), axis=1).reshape(WIDTH, WIDTH)

    vecs = jnp.transpose(aux_full[:, :16].astype(F32))
    q_bias = lax.dynamic_slice_in_dim(vecs[0], core * HALF, HALF, 0)
    v_bias = lax.dynamic_slice_in_dim(vecs[1], core * HALF, HALF, 0)
    m_bias, f_gain, f_shift = vecs[2], vecs[3], vecs[4]
    o_bias, s_gain, s_shift, head = vecs[5], vecs[6], vecs[7], vecs[8]
    i_bias = aux_full[:, 9 : 9 + hidden // rows].reshape(chips, 2, hidden)
    i_bias = pick(i_bias, core, 1).reshape(ff // 2).astype(F32)

    bias = jnp.concatenate([q_bias, jnp.zeros((HALF,), F32), v_bias])
    projected = (mm(inputs2, w_qkv) + bias).astype(BF16)
    q_scaled = projected[:, :HALF] * BF16(0.125)
    kv_own = projected[:, HALF:]
    kv_z = jnp.concatenate([kv_own] + [shift_z(kv_own, k) for k in range(1, zs)], axis=0)
    kv = jnp.concatenate([kv_z, swap_y(kv_z)], axis=0)
    o_exact, lse = attend(q_scaled, kv)
    context2 = jnp.transpose(o_exact).astype(BF16).reshape(2, tokens, HALF)
    got = swap_core(pick(context2, 1 - core, 0))
    context = pair_core(pick(context2, core, 0), got, axis=1).reshape(tokens, WIDTH)

    attended = mm(context, w_mixer) + m_bias
    first_rows, first_normed, first_scale = norm_forward(
        inputs.astype(F32) + attended, f_gain, f_shift
    )
    first_low = first_rows.astype(BF16)
    first2 = pair_core(first_low, swap_core(first_low)).reshape(2 * tokens, WIDTH)

    def sum_core(part):
        part = part.reshape(2, tokens, WIDTH)
        return pick(part, core, 0) + swap_core(pick(part, 1 - core, 0))

    inner_rows = mm(first2, w_inner) + i_bias
    act, slope = gelu_pair(inner_rows)
    active = act.astype(BF16)
    outer_rows = sum_core(mm(active, w_outer)) + o_bias
    final_rows, second_normed, second_scale = norm_forward(
        first_rows + outer_rows, s_gain, s_shift
    )
    logits = jnp.sum(final_rows * head, axis=-1)
    term_weights = soft_plus(logits)
    head_slope = term_cotangent[0] * jax.nn.sigmoid(logits)
    grad_final = out_cotangent[0].astype(F32) + head_slope[:, None] * head
    head_grad = jnp.sum(head_slope[:, None] * final_rows, axis=0)
    grad_second = norm_backward(grad_final, second_normed, second_scale, s_gain)
    second_gain_grad = jnp.sum(grad_final * second_normed, axis=0)
    second_shift_grad = jnp.sum(grad_final, axis=0)
    grad_outer = grad_second.astype(BF16)
    outer_bias_grad = jnp.sum(grad_outer.astype(F32), axis=0)
    grad_outer2 = pair_core(grad_outer, swap_core(grad_outer)).reshape(2 * tokens, WIDTH)
    grad_inner = (mm_t(grad_outer2, w_outer) * slope).astype(BF16)
    inner_bias_grad = jnp.sum(grad_inner.astype(F32), axis=0)
    grad_first = grad_second + sum_core(mm_t(grad_inner, w_inner))
    g_outer = scatter_chips(t_mm(active, grad_outer2), x, y, z)
    g_inner = scatter_chips(t_mm(first2, grad_inner), x, y, z)

    grad_residual = norm_backward(grad_first, first_normed, first_scale, f_gain)
    first_gain_grad = jnp.sum(grad_first * first_normed, axis=0)
    first_shift_grad = jnp.sum(grad_first, axis=0)
    grad_attended = grad_residual.astype(BF16)
    mixer_bias_grad = jnp.sum(grad_attended.astype(F32), axis=0)
    g_mixer = t_mm(context, grad_attended).reshape(chips, 2, rows, WIDTH)
    g_mixer = pick(g_mixer, core, 1) + swap_core(pick(g_mixer, 1 - core, 1).astype(BF16)).astype(
        F32
    )
    g_mixer = scatter_chips(g_mixer.reshape(chips * rows, WIDTH), x, y, z)

    grad_context = mm_t(grad_attended, w_mixer).astype(BF16).reshape(tokens, 2, HALF)
    got = swap_core(pick(grad_context, 1 - core, 1))
    grad_context2 = pair_core(pick(grad_context, core, 1), got).reshape(2 * tokens, HALF)

    grad_q, dkv = attend_back(q_scaled, grad_context2, o_exact, lse, kv)
    dkv = dkv.reshape(2, zs, 2 * tokens, WIDTH)
    dkv = dkv[0].astype(F32) + swap_y(dkv[1]).astype(F32)
    total = dkv[0]
    for k in range(1, zs):
        total = total + shift_z(dkv[k].astype(BF16), zs - k).astype(F32)
    grad_kv = total.astype(BF16)
    grad_qkv = jnp.concatenate([grad_q, grad_kv], axis=1)
    input_part = sum_core(mm_t(grad_qkv, w_qkv))
    input_grad = (grad_residual + input_part).astype(BF16)

    sums = jnp.sum(grad_qkv.astype(F32), axis=0)
    zero = jnp.zeros((2, HALF), F32)
    small = jnp.stack(
        [
            lax.dynamic_update_slice(zero, sums[None, :HALF], (core, 0)).reshape(WIDTH),
            lax.dynamic_update_slice(zero, sums[None, 2 * HALF :], (core, 0)).reshape(WIDTH),
            mixer_bias_grad,
            first_gain_grad,
            first_shift_grad,
            outer_bias_grad,
            second_gain_grad,
            second_shift_grad,
            head_grad,
        ],
        axis=1,
    )
    inner_small = lax.dynamic_update_slice(
        jnp.zeros((chips, 2, hidden), F32),
        inner_bias_grad.reshape(chips, 1, hidden),
        (0, core, 0),
    ).reshape(WIDTH, hidden // rows)
    small = jnp.concatenate([small, inner_small], axis=1)
    small = jnp.pad(small, ((0, 0), (0, AUX - small.shape[1])))
    g_qkv = scatter_chips(jnp.concatenate([t_mm(inputs2, grad_qkv), small], axis=1), x, y, z)

    g_all = jnp.concatenate([g_qkv, g_inner], axis=1).reshape(2, rows, -1)
    own, got = pick(g_all, core, 0), swap_core(pick(g_all, 1 - core, 0))
    wide = 3 * HALF
    small = own[:, wide : wide + AUX] + got[:, wide : wide + AUX]
    g_qkv = pair_core(own[:, :wide], got[:, :wide]).reshape(2, rows, 3, HALF)
    g_qkv = jnp.transpose(g_qkv, (2, 1, 0, 3)).reshape(3, rows, WIDTH)
    g_inner = pair_core(
        own[:, wide + AUX :].reshape(rows, chips, hidden),
        got[:, wide + AUX :].reshape(rows, chips, hidden),
        axis=2,
    ).reshape(rows, ff)
    g_ibias = small[:, 9 : 9 + hidden // rows].reshape(hidden)
    sm = jnp.transpose(small[:, :9])
    return (
        final_rows.astype(BF16)[None],
        term_weights[None],
        input_grad[None],
        g_qkv[0],
        sm[0],
        g_qkv[1],
        g_qkv[2],
        sm[1],
        g_mixer,
        sm[2],
        sm[3],
        sm[4],
        g_inner,
        g_ibias,
        g_outer,
        sm[5],
        sm[6],
        sm[7],
        sm[8],
    )


def solution(mesh):
    both = ("seq", "ctx")
    tok, mat, vec = P("seq", "ctx", None), P(both, None), P(both)
    term = P("seq", "ctx")
    in_specs = (
        tok, mat, vec, mat, mat, vec, mat, vec, vec, vec,
        mat, vec, mat, vec, vec, vec, vec, tok, term,
    )
    out_specs = (
        tok, term, tok, mat, vec, mat, mat, vec, mat, vec,
        vec, vec, mat, vec, mat, vec, vec, vec, vec,
    )
    return jax.shard_map(
        shards, mesh=mesh, in_specs=in_specs, out_specs=out_specs, check_vma=False
    )
```

time: 1430 us -> 413 us (0.29)
  waiting for transfers between devices: 1110 us -> 190 us
  blocking collectives: 77.9 us -> 0 us
  starting transfers between devices: 7.36 us -> 81.3 us
  matrix products: 90.8 us -> 17.3 us
  Pallas kernels: 0 us -> 27.9 us
  local copies, waits for them, and re-layouts: 79.6 us -> 56.1 us
  other arithmetic: 52 us -> 32.8 us
    reduce_scatter x3 -> x0, waiting for transfers between devices: 388 us -> none  [the longest x1 142 us: shards(): lax.psum_scatter(outer_weight_grad, ('seq', 'ctx'), scatter_dimension=0,...]
    all_gather x8 -> x0, waiting for transfers between devices: 352 us -> none  [the longest x1 63.3 us: shards(): lax.all_gather(inner_weight, ('seq', 'ctx'), axis=0, tiled=True)]
    unnamed x17 -> x0, waiting for transfers between devices: 233 us -> none
    unnamed x2 -> x0, blocking collectives: 77.9 us -> none
    ppermute x64 -> x61, starting transfers between devices: 6.4 us -> 81.3 us  [the longest x30 61 us: shift_z(): return lax.ppermute(value, 'ctx', [(i, (i + 4 * k) % n) for i in range(n)])]
    dot_general x132 -> x12, matrix products: 90.8 us -> 17.3 us  [the longest x4 8.09 us: mm_t(): lax.dot_general(a, b, (((1,), (1,)), ((), ())), preferred_element_type=F32)]
    ppermute x64 -> x61, waiting for transfers between devices: 133 us -> 190 us  [the longest x30 88.4 us: shift_z(): return lax.ppermute(value, 'ctx', [(i, (i + 4 * k) % n) for i in range(n)])]
    convert_element_type x74 -> x5, other arithmetic: 43.7 us -> 1.54 us  [the longest x1 1.18 us: shards(): active = act.astype(BF16)]
  transfers between devices with their start and end apart: 78 -> 61, of which waited for: 46 -> 23; matrix products, arithmetic and copies ran while one was open for 13% -> 18% of each run, Pallas kernels for 0% -> 7%
where the time goes in v1:
time: 413 us; the launch traced here: 408 us
  waiting for transfers between devices  190 us (46%)
  starting transfers between devices  81.3 us (20%)
  local copies, waits for them, and re-layouts  56.1 us (14%)
  other arithmetic  32.8 us (8%)
  Pallas kernels  27.9 us (7%)
  matrix products  17.3 us (4%)
    ppermute x30, waiting for transfers between devices, shift_z(): return lax.ppermute(value, 'ctx', [(i, (i + 4 * k) % n) for i in range(n)])  88.4 us
    ppermute x30, starting transfers between devices, shift_z(): return lax.ppermute(value, 'ctx', [(i, (i + 4 * k) % n) for i in range(n)])  61 us
    ppermute x8, waiting for transfers between devices, swap_x(): return lax.ppermute(value, 'seq', [(0, 1), (1, 0)])  51.9 us
    ppermute x23, waiting for transfers between devices, swap_ctx(): return lax.ppermute(value, 'ctx', [(i, i ^ bit) for i in range(n)])  49.3 us
    pallas_call x1, Pallas kernels, attend_back(): pl.pallas_call(attend_back_kernel, grid=(keys // block,), in_specs=[pl.Bl...  18.9 us
    another operation x33, other arithmetic, pair(): return jnp.stack([first, second], axis=axis)  11 us
    ppermute x23, starting transfers between devices, swap_ctx(): return lax.ppermute(value, 'ctx', [(i, i ^ bit) for i in range(n)])  10.4 us
    ppermute x8, starting transfers between devices, swap_x(): return lax.ppermute(value, 'seq', [(0, 1), (1, 0)])  9.93 us
  transfers between devices with their start and end apart: 61, of which 23 were waited for; matrix products, arithmetic and copies ran while one was open for 18% of the time, Pallas kernels for 7%

profile of v1, /device:TPU:0, one launch (start us, length us, event | category | flops | bytes accessed | tf_op | source)
XLA Modules:
  0.0 407.7 jit_solution(5857433811273001632)
XLA Ops:
  0.7 3.1 collective-permute-start.12
  32.3 7.2 %collective-permute-done.2 = bf16[48,1280]{1,0:T(8,128)(2,1)S(1)} collective-permute-done((bf16[48,1280]{1,0:T(8,128)(2,1)S(1)}, bf16[48,1280]{1,0:T(8,128)(2,1)S(1)}, u32[]{:S(2)}, u32[]{:S(2)}) %collective-permute-start.2) | collective-permute-done | bytes 122912 | tf_op jit(solution)/shard_map/ppermute | solution.py:55
  41.1 4.9 %collective-permute-start.21 = (bf16[48,1536]{1,0:T(8,128)(2,1)S(1)}, bf16[48,1536]{1,0:T(8,128)(2,1)S(1)}, u32[]{:S(2)}, u32[]{:S(2)}) collective-permute-start(bf16[48,1536]{1,0:T(8,128)(2,1)S(1)} %bitcast.462), channel_id=1, source_target_pairs={{0,8},{1,9},{2,10},{3,11},{4,12},{5,13},{6,14},{7,15},{8,0},{9,1},... | collective-permute-start | bytes 442376 | tf_op jit(solution)/shard_map/ppermute | solution.py:55
  49.9 7.6 %collective-permute-done.20 = bf16[48,1536]{1,0:T(8,128)(2,1)S(1)} collective-permute-done((bf16[48,1536]{1,0:T(8,128)(2,1)S(1)}, bf16[48,1536]{1,0:T(8,128)(2,1)S(1)}, u32[]{:S(2)}, u32[]{:S(2)}) %collective-permute-start.20) | collective-permute-done | bytes 147488 | tf_op jit(solution)/shard_map/ppermute | solution.py:55
  59.4 13.7 %collective-permute-done.5 = bf16[4,48,1280]{2,1,0:T(8,128)(2,1)S(1)} collective-permute-done((bf16[4,48,1280]{2,1,0:T(8,128)(2,1)S(1)}, bf16[4,48,1280]{2,1,0:T(8,128)(2,1)S(1)}, u32[]{:S(2)}, u32[]{:S(2)}) %collective-permute-start.5) | collective-permute-done | bytes 491552 | tf_op jit(solution)/shard_map/ppermute | solution.py:38
  77.2 20.8 %collective-permute-done.6 = bf16[4,2,48,1280]{3,2,0,1:T(8,128)(2,1)S(1)} collective-permute-done((bf16[4,2,48,1280]{3,2,0,1:T(8,128)(2,1)S(1)}, bf16[4,2,48,1280]{3,2,0,1:T(8,128)(2,1)S(1)}, u32[]{:S(2)}, u32[]{:S(2)}) %collective-permute-start.6) | collective-permute-done | bytes 983072 | tf_op jit(solution)/shard_map/ppermute | solution.py:50
  105.7 8.7 %collective-permute-done.9 = bf16[256,768]{1,0:T(8,128)(2,1)S(1)} collective-permute-done((bf16[256,768]{1,0:T(8,128)(2,1)S(1)}, bf16[256,768]{1,0:T(8,128)(2,1)S(1)}, u32[]{:S(2)}, u32[]{:S(2)}) %collective-permute-start.9) | collective-permute-done | bytes 393248 | tf_op jit(solution)/shard_map/ppermute | solution.py:55
  114.3 19.5 %collective-permute-done.8 = bf16[256,768]{1,0:T(8,128)(2,1)S(1)} collective-permute-done((bf16[256,768]{1,0:T(8,128)(2,1)S(1)}, bf16[256,768]{1,0:T(8,128)(2,1)S(1)}, u32[]{:S(2)}, u32[]{:S(2)}) %collective-permute-start.8) | collective-permute-done | bytes 393248 | tf_op jit(solution)/shard_map/ppermute | solution.py:55
  145.5 21.1 %collective-permute-done.10 = bf16[1024,768]{1,0:T(8,128)(2,1)} collective-permute-done((bf16[1024,768]{1,0:T(8,128)(2,1)}, bf16[1024,768]{1,0:T(8,128)(2,1)}, u32[]{:S(2)}, u32[]{:S(2)}) %collective-permute-start.10) | collective-permute-done | bytes 1572896 | tf_op jit(solution)/shard_map/ppermute | solution.py:38
  168.1 9.0 %shard_map.330 = (f32[384,256]{1,0:T(8,128)S(1)}, f32[8,256]{1,0:T(8,128)S(1)}) custom-call(bf16[256,384]{1,0:T(8,128)(2,1)S(1)} %slice_multiply_fusion.q_ref, bf16[2048,768]{1,0:T(8,128)(2,1)S(1)} %constant_dynamic-update-slice_fusion.3.kv_ref), custom_call_target="tpu_custom_call" | custom-call | flops 805306368 | bytes 3145728 | tf_op jit(solution)/shard_map/pallas_call | solution.py:130
  178.2 2.8 select_bitcast_fusion.3
  207.0 4.1 %convert_reduce_fusion = (f32[1536]{0:T(1024)}, bf16[256,1536]{1,0:T(8,128)(2,1)}) fusion(f32[256,1536]{1,0:T(8,128)} %get-tuple-element.137, bf16[256,768]{1,0:T(8,128)(2,1)S(1)} %bitcast.449, bf16[1536,768]{1,0:T(8,128)(2,1)S(1)} %bitcast.436), kind=kOutput, calls=%fused_computation.28 | convolution fusion | flops 608696832 | bytes 5117952 | tf_op jit(solution)/shard_map/dot_general | solution.py:29
  216.1 2.8 fusion.87
  231.6 18.9 %shard_map.331 = (bf16[256,384]{1,0:T(8,128)(2,1)S(1)}, bf16[2048,768]{1,0:T(8,128)(2,1)S(1)}) custom-call(bf16[256,384]{1,0:T(8,128)(2,1)S(1)} %slice_multiply_fusion.q_ref, bf16[256,384]{1,0:T(8,128)(2,1)S(1)} %bitcast.411, f32[384,256]{1,0:T(8,128)S(1)} %get-tuple-element.23.o_ref, f32[8,256]{1,0:T(8,128)S(1)} %get-tuple-element.24.lse_ref, ...), custom_call_target="tpu_custom_call" | custom-call | flops 2013265920 | bytes 6291456 | tf_op jit(solution)/shard_map/pallas_call | solution.py:198
  253.3 22.5 %collective-permute-done.44 = bf16[384,1536]{1,0:T(8,128)(2,1)} collective-permute-done((bf16[384,1536]{1,0:T(8,128)(2,1)}, bf16[384,1536]{1,0:T(8,128)(2,1)}, u32[]{:S(2)}, u32[]{:S(2)}) %collective-permute-start.44) | collective-permute-done | bytes 1179680 | tf_op jit(solution)/shard_map/ppermute | solution.py:50
  277.4 3.8 collective-permute-done.51
  283.9 6.4 %collective-permute-done.52 = bf16[4,24,768]{2,1,0:T(8,128)(2,1)S(1)} collective-permute-done((bf16[4,24,768]{2,1,0:T(8,128)(2,1)S(1)}, bf16[4,24,768]{2,1,0:T(8,128)(2,1)S(1)}, u32[]{:S(2)}, u32[]{:S(2)}) %collective-permute-start.52) | collective-permute-done | bytes 147488 | tf_op jit(solution)/shard_map/ppermute | solution.py:38
  290.4 4.9 %collective-permute-start.53 = (bf16[24,768]{1,0:T(8,128)(2,1)S(1)}, bf16[24,768]{1,0:T(8,128)(2,1)S(1)}, u32[]{:S(2)}, u32[]{:S(2)}) collective-permute-start(bf16[24,768]{1,0:T(8,128)(2,1)S(1)} %get-tuple-element.110), channel_id=1, source_target_pairs={{0,4},{1,5},{2,6},{3,7},{4,8},{5,9},{6,10},{7,11},{8,12},{9,13},{1... | collective-permute-start | bytes 110600 | tf_op jit(solution)/shard_map/ppermute | solution.py:55
  295.9 2.5 collective-permute-start.37
  300.8 2.9 collective-permute-start.55
  303.7 3.6 collective-permute-start.54
  308.2 13.9 %collective-permute-done.55 = bf16[24,768]{1,0:T(8,128)(2,1)S(1)} collective-permute-done((bf16[24,768]{1,0:T(8,128)(2,1)S(1)}, bf16[24,768]{1,0:T(8,128)(2,1)S(1)}, u32[]{:S(2)}, u32[]{:S(2)}) %collective-permute-start.55) | collective-permute-done | bytes 36896 | tf_op jit(solution)/shard_map/ppermute | solution.py:55
  322.9 12.5 %collective-permute-done.54 = bf16[24,768]{1,0:T(8,128)(2,1)S(1)} collective-permute-done((bf16[24,768]{1,0:T(8,128)(2,1)S(1)}, bf16[24,768]{1,0:T(8,128)(2,1)S(1)}, u32[]{:S(2)}, u32[]{:S(2)}) %collective-permute-start.54) | collective-permute-done | bytes 36896 | tf_op jit(solution)/shard_map/ppermute | solution.py:55
  341.6 4.2 %concatenate.40 = f32[768,13]{1,0:T(8,128)} concatenate(f32[768,1]{1,0:T(8,128)} %bitcast.451, f32[768,1]{1,0:T(8,128)} %bitcast.452, f32[768,1]{1,0:T(8,128)} %stack.290, f32[768,1]{1,0:T(8,128)} %stack.291, f32[768,1]{1,0:T(8,128)} %stack.292, f32[768,1]{1,0:T(8,128)} %stack.293, f32[768,1]{1,0:T(8,128)} %stack.294, f32[768,1]{1,0:T(8,128)} %stack.295, f32[768,1]{1,0:T(8,128)} %stack.296, ...), dimensions={1} | concatenate | bytes 79872 | tf_op jit(solution)/shard_map/concatenate | solution.py:431
  345.8 2.6 select_maximum_fusion
  351.0 11.4 %collective-permute-start.46 = (bf16[48,1536]{1,0:T(8,128)(2,1)S(1)}, bf16[48,1536]{1,0:T(8,128)(2,1)S(1)}, u32[]{:S(2)}, u32[]{:S(2)}) collective-permute-start(bf16[48,1536]{1,0:T(8,128)(2,1)S(1)} %get-tuple-element.77), channel_id=1, source_target_pairs={{0,4},{1,5},{2,6},{3,7},{4,8},{5,9},{6,10},{7,11},{8,12},{9,13},{1... | collective-permute-start | bytes 442376 | tf_op jit(solution)/shard_map/ppermute | solution.py:55
  365.1 4.8 %collective-permute-done.39 = bf16[384,1280]{1,0:T(8,128)(2,1)S(1)} collective-permute-done((bf16[384,1280]{1,0:T(8,128)(2,1)S(1)}, bf16[384,1280]{1,0:T(8,128)(2,1)S(1)}, u32[]{:S(2)}, u32[]{:S(2)}) %collective-permute-start.39) | collective-permute-done | bytes 983072 | tf_op jit(solution)/shard_map/ppermute | solution.py:50
  371.6 3.8 collective-permute-start.60
  375.5 4.6 %collective-permute-done.40 = bf16[4,48,1280]{2,1,0:T(8,128)(2,1)S(1)} collective-permute-done((bf16[4,48,1280]{2,1,0:T(8,128)(2,1)S(1)}, bf16[4,48,1280]{2,1,0:T(8,128)(2,1)S(1)}, u32[]{:S(2)}, u32[]{:S(2)}) %collective-permute-start.40) | collective-permute-done | bytes 491552 | tf_op jit(solution)/shard_map/ppermute | solution.py:38
  380.4 4.8 %collective-permute-start.43 = (bf16[48,1280]{1,0:T(8,128)(2,1)S(1)}, bf16[48,1280]{1,0:T(8,128)(2,1)S(1)}, u32[]{:S(2)}, u32[]{:S(2)}) collective-permute-start(bf16[48,1280]{1,0:T(8,128)(2,1)S(1)} %get-tuple-element.87), channel_id=1, source_target_pairs={{0,12},{1,13},{2,14},{3,15},{4,0},{5,1},{6,2},{7,3},{8,4},{9,5},{1... | collective-permute-start | bytes 368648 | tf_op jit(solution)/shard_map/ppermute | solution.py:55
  386.4 2.7 collective-permute-done.41
  389.2 9.4 %collective-permute-done.42 = bf16[48,1280]{1,0:T(8,128)(2,1)S(1)} collective-permute-done((bf16[48,1280]{1,0:T(8,128)(2,1)S(1)}, bf16[48,1280]{1,0:T(8,128)(2,1)S(1)}, u32[]{:S(2)}, u32[]{:S(2)}) %collective-permute-start.42) | collective-permute-done | bytes 122912 | tf_op jit(solution)/shard_map/ppermute | solution.py:55
  (434 shorter events, 139.6 us)
Async XLA Ops:
  0.7 22.3 %collective-permute-start.12 = (bf16[24,768]{1,0:T(8,128)(2,1)}, bf16[24,768]{1,0:T(8,128)(2,1)S(1)}, u32[]{:S(2)}, u32[]{:S(2)}) collective-permute-start(bf16[24,768]{1,0:T(8,128)(2,1)} %param.25), channel_id=1, source_target_pairs={{0,4},{1,5},{2,6},{3,7},{4,8},{5,9},{6,10},{7,11},{8,12},{9,13},{1... | collective-permute-start | bytes 110600 | tf_op jit(solution)/shard_map/ppermute | solution.py:55
  3.8 19.6 %collective-permute-start.14 = (bf16[24,768]{1,0:T(8,128)(2,1)}, bf16[24,768]{1,0:T(8,128)(2,1)S(1)}, u32[]{:S(2)}, u32[]{:S(2)}) collective-permute-start(bf16[24,768]{1,0:T(8,128)(2,1)} %param.25), channel_id=1, source_target_pairs={{0,12},{1,13},{2,14},{3,15},{4,0},{5,1},{6,2},{7,3},{8,4},{9,5},{1... | collective-permute-start | bytes 110600 | tf_op jit(solution)/shard_map/ppermute | solution.py:55
  6.8 19.9 %collective-permute-start.25 = (bf16[96,768]{1,0:T(8,128)(2,1)}, bf16[96,768]{1,0:T(8,128)(2,1)S(1)}, u32[]{:S(2)}, u32[]{:S(2)}) collective-permute-start(bf16[96,768]{1,0:T(8,128)(2,1)} %param.31), channel_id=1, source_target_pairs={{0,4},{1,5},{2,6},{3,7},{4,8},{5,9},{6,10},{7,11},{8,12},{9,13},{1... | collective-permute-start | bytes 442376 | tf_op jit(solution)/shard_map/ppermute | solution.py:55
  8.4 22.4 %collective-permute-start.27 = (bf16[96,768]{1,0:T(8,128)(2,1)}, bf16[96,768]{1,0:T(8,128)(2,1)S(1)}, u32[]{:S(2)}, u32[]{:S(2)}) collective-permute-start(bf16[96,768]{1,0:T(8,128)(2,1)} %param.31), channel_id=1, source_target_pairs={{0,12},{1,13},{2,14},{3,15},{4,0},{5,1},{6,2},{7,3},{8,4},{9,5},{1... | collective-permute-start | bytes 442376 | tf_op jit(solution)/shard_map/ppermute | solution.py:55
  24.6 23.6 %collective-permute-start = (bf16[128,768]{1,0:T(8,128)(2,1)S(1)}, bf16[128,768]{1,0:T(8,128)(2,1)S(1)}, u32[]{:S(2)}, u32[]{:S(2)}) collective-permute-start(bf16[128,768]{1,0:T(8,128)(2,1)S(1)} %bitcast.454), channel_id=1, source_target_pairs={{0,1},{1,0},{2,3},{3,2},{4,5},{5,4},{6,7},{7,6},{8,9},{9,8},{10,11... | collective-permute-start | bytes 589832 | tf_op jit(solution)/shard_map/ppermute | solution.py:38
  24.9 23.2 %collective-permute-start.15 = (bf16[4,24,768]{2,1,0:T(8,128)(2,1)S(1)}, bf16[4,24,768]{2,1,0:T(8,128)(2,1)S(1)}, u32[]{:S(2)}, u32[]{:S(2)}) collective-permute-start(bf16[4,24,768]{2,1,0:T(8,128)(2,1)S(1)} %bitcast_dynamic-update-slice_fusion.12), channel_id=1, source_target_pairs={{0,2},{1,3},{2,0},{3,1},{4,6},{5,7},{6,4},{7,5},{8,10},{9,11},{10,... | collective-permute-start | bytes 442376 | tf_op jit(solution)/shard_map/ppermute | solution.py:38
  39.5 35.3 %collective-permute-start.22 = (bf16[48,1536]{1,0:T(8,128)(2,1)S(1)}, bf16[48,1536]{1,0:T(8,128)(2,1)S(1)}, u32[]{:S(2)}, u32[]{:S(2)}) collective-permute-start(bf16[48,1536]{1,0:T(8,128)(2,1)S(1)} %bitcast.461), channel_id=1, source_target_pairs={{0,12},{1,13},{2,14},{3,15},{4,0},{5,1},{6,2},{7,3},{8,4},{9,5},{1... | collective-permute-start | bytes 442376 | tf_op jit(solution)/shard_map/ppermute | solution.py:55
  48.1 27.3 %collective-permute-start.28 = (bf16[4,96,768]{2,1,0:T(8,128)(2,1)S(1)}, bf16[4,96,768]{2,1,0:T(8,128)(2,1)S(1)}, u32[]{:S(2)}, u32[]{:S(2)}) collective-permute-start(bf16[4,96,768]{2,1,0:T(8,128)(2,1)S(1)} %bitcast_dynamic-update-slice_fusion), channel_id=1, source_target_pairs={{0,2},{1,3},{2,0},{3,1},{4,6},{5,7},{6,4},{7,5},{8,10},{9,11},{10,... | collective-permute-start | bytes 1769480 | tf_op jit(solution)/shard_map/ppermute | solution.py:38
  48.3 27.0 %collective-permute-start.16 = (bf16[4,2,24,768]{3,2,1,0:T(8,128)(2,1)S(1)}, bf16[4,2,24,768]{3,2,1,0:T(8,128)(2,1)S(1)}, u32[]{:S(2)}, u32[]{:S(2)}) collective-permute-start(bf16[4,2,24,768]{3,2,1,0:T(8,128)(2,1)S(1)} %pad_maximum_fusion.15), channel_id=1, source_target_pairs={{0,16},{16,0},{1,17},{17,1},{2,18},{18,2},{3,19},{19,3},{4,20},{20... | collective-permute-start | bytes 884744 | tf_op jit(solution)/shard_map/ppermute | solution.py:50
  73.3 24.8 %collective-permute-start.6 = (bf16[4,2,48,1280]{3,2,0,1:T(8,128)(2,1)S(1)}, bf16[4,2,48,1280]{3,2,0,1:T(8,128)(2,1)S(1)}, u32[]{:S(2)}, u32[]{:S(2)}) collective-permute-start(bf16[4,2,48,1280]{3,2,0,1:T(8,128)(2,1)S(1)} %pad_maximum_fusion.7), channel_id=1, source_target_pairs={{0,16},{16,0},{1,17},{17,1},{2,18},{18,2},{3,19},{19,3},{4,20},{20... | collective-permute-start | bytes 2949128 | tf_op jit(solution)/shard_map/ppermute | solution.py:50
  74.9 29.9 %collective-permute-start.23 = (bf16[4,48,1536]{2,1,0:T(8,128)(2,1)S(1)}, bf16[4,48,1536]{2,1,0:T(8,128)(2,1)S(1)}, u32[]{:S(2)}, u32[]{:S(2)}) collective-permute-start(bf16[4,48,1536]{2,1,0:T(8,128)(2,1)S(1)} %bitcast_dynamic-update-slice_fusion.4), channel_id=1, source_target_pairs={{0,2},{1,3},{2,0},{3,1},{4,6},{5,7},{6,4},{7,5},{8,10},{9,11},{10,... | collective-permute-start | bytes 1769480 | tf_op jit(solution)/shard_map/ppermute | solution.py:38
  75.3 63.5 %collective-permute-start.17 = (bf16[16,24,768]{2,1,0:T(8,128)(2,1)S(1)}, bf16[16,24,768]{2,1,0:T(8,128)(2,1)S(1)}, u32[]{:S(2)}, u32[]{:S(2)}) collective-permute-start(bf16[16,24,768]{2,1,0:T(8,128)(2,1)S(1)} %bitcast.434), channel_id=1, source_target_pairs={{0,1},{1,0},{2,3},{3,2},{4,5},{5,4},{6,7},{7,6},{8,9},{9,8},{10,11... | collective-permute-start | bytes 1769480 | tf_op jit(solution)/shard_map/ppermute | solution.py:38
  76.6 64.4 %collective-permute-start.29 = (bf16[4,2,96,768]{3,2,1,0:T(8,128)(2,1)}, bf16[4,2,96,768]{3,2,1,0:T(8,128)(2,1)}, u32[]{:S(2)}, u32[]{:S(2)}) collective-permute-start(bf16[4,2,96,768]{3,2,1,0:T(8,128)(2,1)} %pad_maximum_fusion.6), channel_id=1, source_target_pairs={{0,16},{16,0},{1,17},{17,1},{2,18},{18,2},{3,19},{19,3},{4,20},{20... | collective-permute-start | bytes 3538952 | tf_op jit(solution)/shard_map/ppermute | solution.py:50
  104.8 29.1 %collective-permute-start.8 = (bf16[256,768]{1,0:T(8,128)(2,1)S(1)}, bf16[256,768]{1,0:T(8,128)(2,1)S(1)}, u32[]{:S(2)}, u32[]{:S(2)}) collective-permute-start(bf16[256,768]{1,0:T(8,128)(2,1)S(1)} %get-tuple-element.93), channel_id=1, source_target_pairs={{0,8},{1,9},{2,10},{3,11},{4,12},{5,13},{6,14},{7,15},{8,0},{9,1},... | collective-permute-start | bytes 1179656 | tf_op jit(solution)/shard_map/ppermute | solution.py:55
  104.8 29.1 %collective-permute-start.7 = (bf16[256,768]{1,0:T(8,128)(2,1)S(1)}, bf16[256,768]{1,0:T(8,128)(2,1)S(1)}, u32[]{:S(2)}, u32[]{:S(2)}) collective-permute-start(bf16[256,768]{1,0:T(8,128)(2,1)S(1)} %get-tuple-element.93), channel_id=1, source_target_pairs={{0,4},{1,5},{2,6},{3,7},{4,8},{5,9},{6,10},{7,11},{8,12},{9,13},{1... | collective-permute-start | bytes 1179656 | tf_op jit(solution)/shard_map/ppermute | solution.py:55
  135.2 31.4 %collective-permute-start.10 = (bf16[1024,768]{1,0:T(8,128)(2,1)}, bf16[1024,768]{1,0:T(8,128)(2,1)}, u32[]{:S(2)}, u32[]{:S(2)}) collective-permute-start(bf16[1024,768]{1,0:T(8,128)(2,1)} %pad_maximum_fusion.3), channel_id=1, source_target_pairs={{0,2},{1,3},{2,0},{3,1},{4,6},{5,7},{6,4},{7,5},{8,10},{9,11},{10,... | collective-permute-start | bytes 4718600 | tf_op jit(solution)/shard_map/ppermute | solution.py:38
  137.3 40.1 %collective-permute-start.24 = (bf16[4,2,48,1536]{3,2,1,0:T(8,128)(2,1)}, bf16[4,2,48,1536]{3,2,1,0:T(8,128)(2,1)}, u32[]{:S(2)}, u32[]{:S(2)}) collective-permute-start(bf16[4,2,48,1536]{3,2,1,0:T(8,128)(2,1)} %pad_maximum_fusion.5), channel_id=1, source_target_pairs={{0,16},{16,0},{1,17},{17,1},{2,18},{18,2},{3,19},{19,3},{4,20},{20... | collective-permute-start | bytes 3538952 | tf_op jit(solution)/shard_map/ppermute | solution.py:50
  221.3 61.0 %collective-permute-start.56 = (bf16[768,768]{1,0:T(8,128)(2,1)}, bf16[768,768]{1,0:T(8,128)(2,1)}, u32[]{:S(2)}, u32[]{:S(2)}) collective-permute-start(bf16[768,768]{1,0:T(8,128)(2,1)} %fusion.15), channel_id=1, source_target_pairs={{0,16},{16,0},{1,17},{17,1},{2,18},{18,2},{3,19},{19,3},{4,20},{20... | collective-permute-start | bytes 3538952 | tf_op jit(solution)/shard_map/ppermute | solution.py:50
  224.9 50.8 %collective-permute-start.44 = (bf16[384,1536]{1,0:T(8,128)(2,1)}, bf16[384,1536]{1,0:T(8,128)(2,1)}, u32[]{:S(2)}, u32[]{:S(2)}) collective-permute-start(bf16[384,1536]{1,0:T(8,128)(2,1)} %fusion.14), channel_id=1, source_target_pairs={{0,16},{16,0},{1,17},{17,1},{2,18},{18,2},{3,19},{19,3},{4,20},{20... | collective-permute-start | bytes 3538952 | tf_op jit(solution)/shard_map/ppermute | solution.py:50
  231.0 20.9 %collective-permute-start.50 = (bf16[16,24,768]{2,1,0:T(8,128)(2,1)S(1)}, bf16[16,24,768]{2,1,0:T(8,128)(2,1)S(1)}, u32[]{:S(2)}, u32[]{:S(2)}) collective-permute-start(bf16[16,24,768]{2,1,0:T(8,128)(2,1)S(1)} %fusion.24), channel_id=1, source_target_pairs={{0,1},{1,0},{2,3},{3,2},{4,5},{5,4},{6,7},{7,6},{8,9},{9,8},{10,11... | collective-permute-start | bytes 1769480 | tf_op jit(solution)/shard_map/ppermute | solution.py:38
  250.8 44.5 %collective-permute-start.34 = (bf16[4,256,768]{2,1,0:T(8,128)(2,1)S(1)}, bf16[4,256,768]{2,1,0:T(8,128)(2,1)S(1)}, u32[]{:S(2)}, u32[]{:S(2)}) collective-permute-start(bf16[4,256,768]{2,1,0:T(8,128)(2,1)S(1)} %bitcast.453), channel_id=1, source_target_pairs={{0,2},{1,3},{2,0},{3,1},{4,6},{5,7},{6,4},{7,5},{8,10},{9,11},{10,... | collective-permute-start | bytes 4718600 | tf_op jit(solution)/shard_map/ppermute | solution.py:38
  252.1 29.1 %collective-permute-start.51 = (bf16[192,768]{1,0:T(8,128)(2,1)S(1)}, bf16[192,768]{1,0:T(8,128)(2,1)S(1)}, u32[]{:S(2)}, u32[]{:S(2)}) collective-permute-start(bf16[192,768]{1,0:T(8,128)(2,1)S(1)} %fusion.37), channel_id=1, source_target_pairs={{0,16},{16,0},{1,17},{17,1},{2,18},{18,2},{3,19},{19,3},{4,20},{20... | collective-permute-start | bytes 884744 | tf_op jit(solution)/shard_map/ppermute | solution.py:50
  295.9 40.9 %collective-permute-start.35 = (bf16[256,768]{1,0:T(8,128)(2,1)S(1)}, bf16[256,768]{1,0:T(8,128)(2,1)S(1)}, u32[]{:S(2)}, u32[]{:S(2)}) collective-permute-start(bf16[256,768]{1,0:T(8,128)(2,1)S(1)} %get-tuple-element.71), channel_id=1, source_target_pairs={{0,12},{1,13},{2,14},{3,15},{4,0},{5,1},{6,2},{7,3},{8,4},{9,5},{1... | collective-permute-start | bytes 1179656 | tf_op jit(solution)/shard_map/ppermute | solution.py:55
  295.9 40.9 %collective-permute-start.37 = (bf16[256,768]{1,0:T(8,128)(2,1)S(1)}, bf16[256,768]{1,0:T(8,128)(2,1)S(1)}, u32[]{:S(2)}, u32[]{:S(2)}) collective-permute-start(bf16[256,768]{1,0:T(8,128)(2,1)S(1)} %get-tuple-element.72), channel_id=1, source_target_pairs={{0,4},{1,5},{2,6},{3,7},{4,8},{5,9},{6,10},{7,11},{8,12},{9,13},{1... | collective-permute-start | bytes 1179656 | tf_op jit(solution)/shard_map/ppermute | solution.py:55
  298.5 38.3 %collective-permute-start.36 = (bf16[256,768]{1,0:T(8,128)(2,1)S(1)}, bf16[256,768]{1,0:T(8,128)(2,1)S(1)}, u32[]{:S(2)}, u32[]{:S(2)}) collective-permute-start(bf16[256,768]{1,0:T(8,128)(2,1)S(1)} %get-tuple-element.73), channel_id=1, source_target_pairs={{0,8},{1,9},{2,10},{3,11},{4,12},{5,13},{6,14},{7,15},{8,0},{9,1},... | collective-permute-start | bytes 1179656 | tf_op jit(solution)/shard_map/ppermute | solution.py:55
  300.8 21.3 %collective-permute-start.55 = (bf16[24,768]{1,0:T(8,128)(2,1)S(1)}, bf16[24,768]{1,0:T(8,128)(2,1)S(1)}, u32[]{:S(2)}, u32[]{:S(2)}) collective-permute-start(bf16[24,768]{1,0:T(8,128)(2,1)S(1)} %get-tuple-element.111), channel_id=1, source_target_pairs={{0,12},{1,13},{2,14},{3,15},{4,0},{5,1},{6,2},{7,3},{8,4},{9,5},{1... | collective-permute-start | bytes 110600 | tf_op jit(solution)/shard_map/ppermute | solution.py:55
  303.7 31.7 %collective-permute-start.54 = (bf16[24,768]{1,0:T(8,128)(2,1)S(1)}, bf16[24,768]{1,0:T(8,128)(2,1)S(1)}, u32[]{:S(2)}, u32[]{:S(2)}) collective-permute-start(bf16[24,768]{1,0:T(8,128)(2,1)S(1)} %get-tuple-element.112), channel_id=1, source_target_pairs={{0,8},{1,9},{2,10},{3,11},{4,12},{5,13},{6,14},{7,15},{8,0},{9,1},... | collective-permute-start | bytes 110600 | tf_op jit(solution)/shard_map/ppermute | solution.py:55
  322.1 41.8 %collective-permute-start.57 = (bf16[4,96,768]{2,1,0:T(8,128)(2,1)}, bf16[4,96,768]{2,1,0:T(8,128)(2,1)}, u32[]{:S(2)}, u32[]{:S(2)}) collective-permute-start(bf16[4,96,768]{2,1,0:T(8,128)(2,1)} %fusion.25), channel_id=1, source_target_pairs={{0,2},{1,3},{2,0},{3,1},{4,6},{5,7},{6,4},{7,5},{8,10},{9,11},{10,... | collective-permute-start | bytes 1769480 | tf_op jit(solution)/shard_map/ppermute | solution.py:38
  348.5 21.4 %collective-permute-start.39 = (bf16[384,1280]{1,0:T(8,128)(2,1)S(1)}, bf16[384,1280]{1,0:T(8,128)(2,1)S(1)}, u32[]{:S(2)}, u32[]{:S(2)}) collective-permute-start(bf16[384,1280]{1,0:T(8,128)(2,1)S(1)} %fusion.16), channel_id=1, source_target_pairs={{0,16},{16,0},{1,17},{17,1},{2,18},{18,2},{3,19},{19,3},{4,20},{20... | collective-permute-start | bytes 2949128 | tf_op jit(solution)/shard_map/ppermute | solution.py:50
  351.0 20.7 %collective-permute-start.46 = (bf16[48,1536]{1,0:T(8,128)(2,1)S(1)}, bf16[48,1536]{1,0:T(8,128)(2,1)S(1)}, u32[]{:S(2)}, u32[]{:S(2)}) collective-permute-start(bf16[48,1536]{1,0:T(8,128)(2,1)S(1)} %get-tuple-element.77), channel_id=1, source_target_pairs={{0,4},{1,5},{2,6},{3,7},{4,8},{5,9},{6,10},{7,11},{8,12},{9,13},{1... | collective-permute-start | bytes 442376 | tf_op jit(solution)/shard_map/ppermute | solution.py:55
  371.6 27.3 %collective-permute-start.58 = (bf16[96,768]{1,0:T(8,128)(2,1)S(1)}, bf16[96,768]{1,0:T(8,128)(2,1)S(1)}, u32[]{:S(2)}, u32[]{:S(2)}) collective-permute-start(bf16[96,768]{1,0:T(8,128)(2,1)S(1)} %get-tuple-element.74), channel_id=1, source_target_pairs={{0,4},{1,5},{2,6},{3,7},{4,8},{5,9},{6,10},{7,11},{8,12},{9,13},{1... | collective-permute-start | bytes 442376 | tf_op jit(solution)/shard_map/ppermute | solution.py:55
  371.6 27.2 %collective-permute-start.60 = (bf16[96,768]{1,0:T(8,128)(2,1)S(1)}, bf16[96,768]{1,0:T(8,128)(2,1)S(1)}, u32[]{:S(2)}, u32[]{:S(2)}) collective-permute-start(bf16[96,768]{1,0:T(8,128)(2,1)S(1)} %get-tuple-element.75), channel_id=1, source_target_pairs={{0,12},{1,13},{2,14},{3,15},{4,0},{5,1},{6,2},{7,3},{8,4},{9,5},{1... | collective-permute-start | bytes 442376 | tf_op jit(solution)/shard_map/ppermute | solution.py:55
  (89 other events, 779.3 us)

commit v2 on v1

v2 whole, which is shorter than its diff:
```python
import functools
import math

import jax
import jax.numpy as jnp
from jax import lax
from jax.experimental import pallas as pl
from jax.experimental.pallas import tpu as pltpu
from jax.sharding import PartitionSpec as P

HEADS = 12
HD = 64
WIDTH = HEADS * HD
HALF = WIDTH // 2
NH = HEADS // 2
EPSILON = 1e-12
ROOT_HALF = 0.7071067811865476
GAUSS_FACTOR = 0.3989422804014327
F32 = jnp.float32
BF16 = jnp.bfloat16
AUX = 128


def mm(a, b):
    return lax.dot_general(a, b, (((1,), (0,)), ((), ())), preferred_element_type=F32)


def mm_t(a, b):
    return lax.dot_general(a, b, (((1,), (1,)), ((), ())), preferred_element_type=F32)


def t_mm(a, b):
    return lax.dot_general(a, b, (((0,), (0,)), ((), ())), preferred_element_type=F32)


def swap_ctx(value, bit):
    n = lax.axis_size("ctx")
    return lax.ppermute(value, "ctx", [(i, i ^ bit) for i in range(n)])


def swap_core(value):
    return swap_ctx(value, 1)


def swap_y(value):
    return swap_ctx(value, 2)


def swap_x(value):
    return lax.ppermute(value, "seq", [(0, 1), (1, 0)])


def shift_z(value, k):
    n = lax.axis_size("ctx")
    return lax.ppermute(value, "ctx", [(i, (i + 4 * k) % n) for i in range(n)])


def pick(value, index, axis):
    return lax.dynamic_index_in_dim(value, index, axis, keepdims=False)


def place():
    at = lax.axis_index("ctx")
    return lax.axis_index("seq"), at // 4, (at // 2) % 2, at % 2


def routes(order, x, z, y, zs, sign):
    out = []
    for outer in range(2):
        for inner in range(2):
            for k in range(zs):
                xr, yr = (outer, inner) if order == "x" else (inner, outer)
                there = (z + sign * k + zs) % zs
                out.append((outer, inner, k, ((x ^ xr) * zs + there) * 2 + (y ^ yr)))
    return out


def assemble(own, other, order):
    x, z, y, _ = place()
    zs, rows, cols = own.shape[1:]
    if rows % 16:
        full = jnp.stack([own, other])
        full = jnp.concatenate([full[:, :, :1], jnp.flip(full[:, :, 1:], 2)], axis=2)
        full = lax.dynamic_slice_in_dim(jnp.concatenate([full, full], axis=2), zs - z, zs, 2)
        bits = (x, y) if order == "x" else (y, x)
        for axis, bit in enumerate(bits):
            full = jnp.where(bit == 0, full, jnp.flip(full, axis))
        if order == "y":
            full = jnp.swapaxes(full, 0, 1)
        return jnp.swapaxes(full, 1, 2).reshape(4 * zs * rows, cols)

    def body(at_ref, own_ref, other_ref, out_ref, sems):
        copies = []
        for outer, inner, k, chip in routes(order, at_ref[0], at_ref[1], at_ref[2], zs, -1):
            source = (own_ref, other_ref)[outer]
            copies.append(
                pltpu.make_async_copy(
                    source.at[inner, k],
                    out_ref.at[pl.ds(pl.multiple_of(chip * rows, 16), rows)],
                    sems.at[(outer * 2 + inner) * zs + k],
                )
            )
        for copy in copies:
            copy.start()
        for copy in copies:
            copy.wait()

    return pl.pallas_call(
        body,
        in_specs=[
            pl.BlockSpec(memory_space=pltpu.SMEM),
            pl.BlockSpec(memory_space=pl.ANY),
            pl.BlockSpec(memory_space=pl.ANY),
        ],
        out_specs=pl.BlockSpec(memory_space=pl.ANY),
        out_shape=jax.ShapeDtypeStruct((4 * zs * rows, cols), own.dtype),
        scratch_shapes=[pltpu.SemaphoreType.DMA((4 * zs,))],
        name="assemble",
    )(jnp.stack([x, z, y]).astype(jnp.int32), own, other)


def split(part, order):
    x, z, y, _ = place()
    zs = lax.axis_size("ctx") // 4
    rows, cols = part.shape[0] // (4 * zs), part.shape[1]
    if rows % 16:
        full = jnp.swapaxes(part.reshape(2, zs, 2, rows, cols), 1, 2)
        full = lax.dynamic_slice_in_dim(jnp.concatenate([full, full], axis=2), z, zs, 2)
        for axis, bit in enumerate((x, y)):
            full = jnp.where(bit == 0, full, jnp.flip(full, axis))
        if order == "y":
            full = jnp.swapaxes(full, 0, 1)
        return full[0], full[1]

    def body(at_ref, part_ref, keep_ref, send_ref, sems):
        copies = []
        for outer, inner, k, chip in routes(order, at_ref[0], at_ref[1], at_ref[2], zs, 1):
            target = (keep_ref, send_ref)[outer]
            copies.append(
                pltpu.make_async_copy(
                    part_ref.at[pl.ds(pl.multiple_of(chip * rows, 16), rows)],
                    target.at[inner, k],
                    sems.at[(outer * 2 + inner) * zs + k],
                )
            )
        for copy in copies:
            copy.start()
        for copy in copies:
            copy.wait()

    return pl.pallas_call(
        body,
        in_specs=[
            pl.BlockSpec(memory_space=pltpu.SMEM),
            pl.BlockSpec(memory_space=pl.ANY),
        ],
        out_specs=[pl.BlockSpec(memory_space=pl.ANY)] * 2,
        out_shape=[jax.ShapeDtypeStruct((2, zs, rows, cols), part.dtype)] * 2,
        scratch_shapes=[pltpu.SemaphoreType.DMA((4 * zs,))],
        name="split",
    )(jnp.stack([x, z, y]).astype(jnp.int32), part)


def z_groups():
    n = lax.axis_size("ctx")
    return [[i + 4 * j for j in range(n // 4)] for i in range(4)]


def turned(blocks, start, forward):
    zs = blocks.shape[0]
    if not forward:
        blocks, start = jnp.flip(blocks, 0), zs - 1 - start
    return lax.dynamic_slice_in_dim(jnp.concatenate([blocks, blocks]), start, zs, 0)


def along_z(block):
    zs = lax.axis_size("ctx") // 4
    if zs > 4:
        every = lax.all_gather(block, "ctx", axis_index_groups=z_groups())
        return turned(every, lax.axis_index("ctx") // 4, False)
    return jnp.stack([block] + [shift_z(block, k) for k in range(1, zs)])


def fan_out(along, order):
    first, last = (swap_y, swap_x) if order == "x" else (swap_x, swap_y)
    own = jnp.stack([along, first(along)])
    return assemble(own, last(own), order)


def fan_in(part, order):
    keep, send = split(part, order)
    first, last = (swap_x, swap_y) if order == "x" else (swap_y, swap_x)
    got = first(send)
    away = last(keep[1] + got[1])
    return keep[0] + got[0] + away


def sum_z(along):
    zs = lax.axis_size("ctx") // 4
    if zs > 4:
        every = turned(along, (zs - lax.axis_index("ctx") // 4) % zs, True)
        every = lax.all_to_all(every, "ctx", 0, 0, axis_index_groups=z_groups())
        return jnp.sum(every.astype(F32), axis=0)
    total = along[0].astype(F32)
    for k in range(1, zs):
        total = total + shift_z(along[k], k).astype(F32)
    return total


def attend_kernel(
    xo_ref, xc_ref, w_ref, bias_ref, q_ref, kvo_ref, kvc_ref, o_ref, ctx_ref, lse_ref, m_s, l_s, acc_s
):
    step = pl.program_id(0)
    tokens = q_ref.shape[0] // 2
    wide = HALF + AUX

    @pl.when(step == 0)
    def _():
        for i, x_ref in enumerate((xo_ref, xc_ref)):
            rows = mm(x_ref[0:tokens, :], w_ref[:, :HALF]) + bias_ref[0:1, :HALF]
            q_ref[i * tokens : (i + 1) * tokens, :] = rows.astype(BF16) * BF16(0.125)
        m_s[...] = jnp.full(m_s.shape, -1e30, F32)
        l_s[...] = jnp.zeros(l_s.shape, F32)
        acc_s[...] = jnp.zeros(acc_s.shape, F32)

    for x_ref, kv_ref in ((xo_ref, kvo_ref), (xc_ref, kvc_ref)):
        kv_ref[...] = (mm(x_ref[...], w_ref[:, wide:]) + bias_ref[0:1, wide:]).astype(BF16)
        for h in range(NH):
            lo = h * HD
            qh = q_ref[:, lo : lo + HD]
            kh = kv_ref[:, lo : lo + HD]
            vh = kv_ref[:, HALF + lo : HALF + lo + HD]
            s = mm_t(kh, qh)
            before = m_s[h : h + 1, :]
            top = jnp.maximum(before, jnp.max(s, axis=0, keepdims=True))
            p = jnp.exp(s - top)
            factor = jnp.exp(before - top)
            m_s[h : h + 1, :] = top
            l_s[h : h + 1, :] = l_s[h : h + 1, :] * factor + jnp.sum(p, axis=0, keepdims=True)
            acc_s[lo : lo + HD, :] = acc_s[lo : lo + HD, :] * factor + t_mm(vh, p.astype(BF16))

    @pl.when(step == pl.num_programs(0) - 1)
    def _():
        lse_ref[...] = m_s[...] + jnp.log(l_s[...])
        for h in range(NH):
            lo = h * HD
            o_ref[lo : lo + HD, :] = acc_s[lo : lo + HD, :] / l_s[h : h + 1, :]
        ctx_ref[...] = jnp.transpose(o_ref[...]).astype(BF16)


def whole_spec(*shape):
    return pl.BlockSpec(shape, lambda i: (0,) * len(shape))


def attend(xo, xc, w, bias, tokens):
    keys = xo.shape[0]
    block = math.gcd(keys, 1024)
    rows = pl.BlockSpec((block, WIDTH), lambda i: (i, 0))
    return pl.pallas_call(
        attend_kernel,
        grid=(keys // block,),
        in_specs=[rows, rows, whole_spec(*w.shape), whole_spec(*bias.shape)],
        out_specs=[
            whole_spec(2 * tokens, HALF),
            rows,
            rows,
            whole_spec(HALF, 2 * tokens),
            whole_spec(2 * tokens, HALF),
            whole_spec(8, 2 * tokens),
        ],
        out_shape=[
            jax.ShapeDtypeStruct((2 * tokens, HALF), BF16),
            jax.ShapeDtypeStruct((keys, WIDTH), BF16),
            jax.ShapeDtypeStruct((keys, WIDTH), BF16),
            jax.ShapeDtypeStruct((HALF, 2 * tokens), F32),
            jax.ShapeDtypeStruct((2 * tokens, HALF), BF16),
            jax.ShapeDtypeStruct((8, 2 * tokens), F32),
        ],
        scratch_shapes=[
            pltpu.VMEM((8, 2 * tokens), F32),
            pltpu.VMEM((8, 2 * tokens), F32),
            pltpu.VMEM((HALF, 2 * tokens), F32),
        ],
        compiler_params=pltpu.CompilerParams(vmem_limit_bytes=40 * 2**20),
        cost_estimate=pl.CostEstimate(
            flops=16 * tokens * keys * HALF + 4 * keys * WIDTH * WIDTH,
            bytes_accessed=8 * keys * WIDTH,
            transcendentals=4 * tokens * keys * NH,
        ),
        name="attend",
    )(xo, xc, w, bias)


def attend_back_kernel(
    q_ref, go_ref, gc_ref, o_ref, lse_ref, kvo_ref, kvc_ref, dq_ref, do_ref, dc_ref, g_s, delta_s, acc_s
):
    step = pl.program_id(0)
    tokens = go_ref.shape[0]

    @pl.when(step == 0)
    def _():
        acc_s[...] = jnp.zeros(acc_s.shape, F32)
        g_s[:tokens, :] = go_ref[...]
        g_s[tokens:, :] = gc_ref[...]
        prod = jnp.transpose(g_s[...].astype(F32)) * o_ref[...]
        for h in range(NH):
            delta_s[h : h + 1, :] = jnp.sum(prod[h * HD : (h + 1) * HD, :], axis=0, keepdims=True)

    for kv_ref, out_ref in ((kvo_ref, do_ref), (kvc_ref, dc_ref)):
        held = []
        for h in range(NH):
            lo = h * HD
            qh = q_ref[:, lo : lo + HD]
            gh = g_s[:, lo : lo + HD]
            kh = kv_ref[:, lo : lo + HD]
            vh = kv_ref[:, HALF + lo : HALF + lo + HD]
            p = jnp.exp(mm_t(kh, qh) - lse_ref[h : h + 1, :])
            dp = mm_t(vh, gh)
            ds = (p * (dp - delta_s[h : h + 1, :])).astype(BF16)
            acc_s[lo : lo + HD, :] += t_mm(kh, ds)
            held.append((mm(ds, qh).astype(BF16), mm(p.astype(BF16), gh).astype(BF16)))
            if h % 2 == 1:
                (dk0, dv0), (dk1, dv1) = held
                held = []
                at = lo - HD
                out_ref[:, at : at + 2 * HD] = jnp.concatenate([dk0, dk1], axis=1)
                out_ref[:, HALF + at : HALF + at + 2 * HD] = jnp.concatenate([dv0, dv1], axis=1)

    @pl.when(step == pl.num_programs(0) - 1)
    def _():
        dq_ref[...] = jnp.transpose(acc_s[...] * 0.125).astype(BF16)


def attend_back(q, go, gc, o, lse, kvo, kvc):
    tokens = go.shape[0]
    keys = kvo.shape[0]
    block = math.gcd(keys, 1024)
    rows = pl.BlockSpec((block, WIDTH), lambda i: (i, 0))
    return pl.pallas_call(
        attend_back_kernel,
        grid=(keys // block,),
        in_specs=[
            whole_spec(2 * tokens, HALF),
            whole_spec(tokens, HALF),
            whole_spec(tokens, HALF),
            whole_spec(HALF, 2 * tokens),
            whole_spec(8, 2 * tokens),
            rows,
            rows,
        ],
        out_specs=[whole_spec(2 * tokens, HALF), rows, rows],
        out_shape=[
            jax.ShapeDtypeStruct((2 * tokens, HALF), BF16),
            jax.ShapeDtypeStruct((keys, WIDTH), BF16),
            jax.ShapeDtypeStruct((keys, WIDTH), BF16),
        ],
        scratch_shapes=[
            pltpu.VMEM((2 * tokens, HALF), BF16),
            pltpu.VMEM((8, 2 * tokens), F32),
            pltpu.VMEM((HALF, 2 * tokens), F32),
        ],
        compiler_params=pltpu.CompilerParams(vmem_limit_bytes=48 * 2**20),
        cost_estimate=pl.CostEstimate(
            flops=40 * tokens * keys * HALF,
            bytes_accessed=8 * keys * WIDTH,
            transcendentals=4 * tokens * keys * NH,
        ),
        name="attend_back",
    )(q, go, gc, o, lse, kvo, kvc)


def norm_forward(residual, gain, shift):
    center = residual - jnp.mean(residual, axis=-1, keepdims=True)
    scale = lax.rsqrt(jnp.mean(center * center, axis=-1, keepdims=True) + EPSILON)
    normed = center * scale
    return normed * gain + shift, normed, scale


def norm_backward(grad_out, normed, scale, gain):
    grad_normed = grad_out * gain
    return scale * (
        grad_normed
        - jnp.mean(grad_normed, axis=-1, keepdims=True)
        - normed * jnp.mean(grad_normed * normed, axis=-1, keepdims=True)
    )


def gelu_pair(u):
    cdf = 0.5 * (1.0 + lax.erf(u * ROOT_HALF))
    return u * cdf, cdf + u * jnp.exp(-0.5 * u * u) * GAUSS_FACTOR


def soft_plus(logits):
    return jnp.maximum(logits, 0.0) + jnp.log1p(jnp.exp(-jnp.abs(logits)))


def shards(
    layer_input,
    query_weight,
    query_bias,
    key_weight,
    value_weight,
    value_bias,
    mixer_weight,
    mixer_bias,
    first_gain,
    first_shift,
    inner_weight,
    inner_bias,
    outer_weight,
    outer_bias,
    second_gain,
    second_shift,
    head_weight,
    out_cotangent,
    term_cotangent,
):
    x, z, y, core = place()
    chips = lax.axis_size("ctx")
    zs = chips // 4
    inputs = layer_input[0]
    tokens = inputs.shape[0]
    rows = query_weight.shape[0]
    hidden = outer_weight.shape[0]
    ff = inner_weight.shape[1]
    wide = HALF + AUX
    cut = (3 * HALF + AUX) // 2

    def in_order(own, other, axis):
        first = jnp.where(core == 0, own, other)
        second = jnp.where(core == 0, other, own)
        return jnp.stack([first, second], axis=axis)

    vectors = jnp.stack(
        [
            query_bias,
            value_bias,
            mixer_bias,
            first_gain,
            first_shift,
            outer_bias,
            second_gain,
            second_shift,
            head_weight,
        ],
        axis=1,
    )
    aux = jnp.concatenate([vectors, inner_bias.reshape(rows, hidden // rows)], axis=1)
    aux = jnp.pad(aux, ((0, 0), (0, AUX - aux.shape[1])))
    three = (query_weight, key_weight, value_weight)
    inner_split = inner_weight.reshape(rows, chips, 2, hidden)

    def side_of(side):
        q, k, v = (lax.dynamic_slice_in_dim(w, side * HALF, HALF, 1) for w in three)
        return jnp.concatenate([q, aux, k, v], axis=1)

    qkv_block = in_order(side_of(core), swap_core(side_of(1 - core)), 0).reshape(2 * rows, -1)
    x_along = along_z(inputs)
    qkv_along = along_z(qkv_block)
    xo = jnp.concatenate([x_along, swap_y(x_along)]).reshape(2 * zs * tokens, WIDTH)
    xc = swap_core(xo)
    w_qkv = jnp.concatenate(
        [fan_out(qkv_along[:, :, :cut], "x"), fan_out(qkv_along[:, :, cut:], "y")], axis=1
    )

    inner_block = in_order(
        pick(inner_split, core, 2).reshape(rows, ff // 2),
        swap_core(pick(inner_split, 1 - core, 2).reshape(rows, ff // 2)),
        0,
    ).reshape(2 * rows, ff // 2)
    w_mixer_half = fan_out(along_z(mixer_weight), "x").reshape(chips, rows, WIDTH)
    w_mixer = in_order(w_mixer_half, swap_core(w_mixer_half), 1).reshape(WIDTH, WIDTH)
    w_inner = fan_out(along_z(inner_block), "x")
    w_outer = fan_out(along_z(outer_weight), "y")

    aux_full = w_qkv[:, HALF:wide]
    vecs = jnp.transpose(aux_full[:, :16].astype(F32))
    halves = lax.dynamic_slice_in_dim(vecs[:2], core * HALF, HALF, 1)
    bias = jnp.concatenate(
        [halves[:1], jnp.zeros((1, AUX + HALF), F32), halves[1:]], axis=1
    )
    m_bias, f_gain, f_shift = vecs[2], vecs[3], vecs[4]
    o_bias, s_gain, s_shift, head = vecs[5], vecs[6], vecs[7], vecs[8]
    i_bias = aux_full[:, 9 : 9 + hidden // rows].reshape(chips, 2, hidden)
    i_bias = pick(i_bias, core, 1).reshape(ff // 2).astype(F32)

    q_scaled, kvo, kvc, o_exact, context2, lse = attend(xo, xc, w_qkv, bias, tokens)
    got = swap_core(context2[tokens:])
    context = in_order(context2[:tokens], got, 1).reshape(tokens, WIDTH)

    attended = mm(context, w_mixer) + m_bias
    first_rows, first_normed, first_scale = norm_forward(
        inputs.astype(F32) + attended, f_gain, f_shift
    )
    first_low = first_rows.astype(BF16)
    first2 = jnp.concatenate([first_low, swap_core(first_low)])

    def sum_core(part):
        return part[:tokens] + swap_core(part[tokens:])

    inner_rows = mm(first2, w_inner) + i_bias
    act, slope = gelu_pair(inner_rows)
    active = act.astype(BF16)
    outer_rows = sum_core(mm(active, w_outer)) + o_bias
    final_rows, second_normed, second_scale = norm_forward(
        first_rows + outer_rows, s_gain, s_shift
    )
    logits = jnp.sum(final_rows * head, axis=-1)
    term_weights = soft_plus(logits)
    head_slope = term_cotangent[0] * jax.nn.sigmoid(logits)
    grad_final = out_cotangent[0].astype(F32) + head_slope[:, None] * head
    head_grad = jnp.sum(head_slope[:, None] * final_rows, axis=0)
    grad_second = norm_backward(grad_final, second_normed, second_scale, s_gain)
    second_gain_grad = jnp.sum(grad_final * second_normed, axis=0)
    second_shift_grad = jnp.sum(grad_final, axis=0)
    grad_outer = grad_second.astype(BF16)
    outer_bias_grad = jnp.sum(grad_outer.astype(F32), axis=0)
    grad_outer2 = jnp.concatenate([grad_outer, swap_core(grad_outer)])
    g_outer = fan_in(t_mm(active, grad_outer2).astype(BF16), "y")
    grad_inner = (mm_t(grad_outer2, w_outer) * slope).astype(BF16)
    inner_bias_grad = jnp.sum(grad_inner.astype(F32), axis=0)
    grad_first = grad_second + sum_core(mm_t(grad_inner, w_inner))
    g_inner = fan_in(t_mm(first2, grad_inner).astype(BF16), "x")

    grad_residual = norm_backward(grad_first, first_normed, first_scale, f_gain)
    first_gain_grad = jnp.sum(grad_first * first_normed, axis=0)
    first_shift_grad = jnp.sum(grad_first, axis=0)
    grad_attended = grad_residual.astype(BF16)
    mixer_bias_grad = jnp.sum(grad_attended.astype(F32), axis=0)
    grad_context = mm_t(grad_attended, w_mixer).astype(BF16).reshape(tokens, 2, HALF)
    got = swap_core(pick(grad_context, 1 - core, 1))
    grad_q, dkvo, dkvc = attend_back(
        q_scaled, pick(grad_context, core, 1), got, o_exact, lse, kvo, kvc
    )

    g_mixer = t_mm(context, grad_attended).astype(BF16).reshape(chips, 2, rows, WIDTH)
    g_mixer = pick(g_mixer, core, 1) + swap_core(pick(g_mixer, 1 - core, 1))
    g_mixer = fan_in(g_mixer.reshape(chips * rows, WIDTH), "x")

    w_kv = w_qkv[:, wide:]
    away = swap_core(mm_t(dkvc, w_kv).astype(BF16))
    part = (mm_t(dkvo, w_kv) + away.astype(F32)).astype(BF16).reshape(2, zs, tokens, WIDTH)
    part = part[0] + swap_y(part[1])
    total = sum_z(jnp.concatenate([part[:1], jnp.flip(part[1:], 0)]))
    input_grad = (
        grad_residual + sum_core(mm_t(grad_q, w_qkv[:, :HALF])) + total
    ).astype(BF16)

    zero = jnp.zeros((2, HALF), F32)
    q_sum = jnp.sum(grad_q.astype(F32), axis=0)
    v_sum = jnp.sum(dkvo[:, HALF:].astype(F32), axis=0) + jnp.sum(
        dkvc[:, HALF:].astype(F32), axis=0
    )
    small = jnp.stack(
        [
            lax.dynamic_update_slice(zero, q_sum[None], (core, 0)).reshape(WIDTH),
            lax.dynamic_update_slice(zero, v_sum[None], (core, 0)).reshape(WIDTH),
            mixer_bias_grad,
            first_gain_grad,
            first_shift_grad,
            outer_bias_grad,
            second_gain_grad,
            second_shift_grad,
            head_grad,
        ],
        axis=1,
    )
    inner_small = lax.dynamic_update_slice(
        jnp.zeros((chips, 2, hidden), F32),
        inner_bias_grad.reshape(chips, 1, hidden),
        (0, core, 0),
    ).reshape(WIDTH, hidden // rows)
    small = jnp.concatenate([small, inner_small], axis=1)
    small = jnp.pad(small, ((0, 0), (0, AUX - small.shape[1])))
    x_two = jnp.concatenate([inputs, xc[:tokens]])
    g_kv = t_mm(xo, dkvo) + t_mm(xc, dkvc)
    g_qkv = jnp.concatenate([t_mm(x_two, grad_q), small, g_kv], axis=1).astype(BF16)
    g_qkv = jnp.concatenate([fan_in(g_qkv[:, :cut], "x"), fan_in(g_qkv[:, cut:], "y")], axis=2)
    g_qkv = sum_z(g_qkv)
    g_outer = sum_z(g_outer)
    g_inner = sum_z(g_inner)
    g_mixer = sum_z(g_mixer)

    g_all = jnp.concatenate([g_qkv, g_inner], axis=1).reshape(2, rows, -1)
    own, got = pick(g_all, core, 0), swap_core(pick(g_all, 1 - core, 0))
    small = own[:, HALF:wide] + got[:, HALF:wide]

    def columns(lo):
        return in_order(own[:, lo : lo + HALF], got[:, lo : lo + HALF], 1).reshape(rows, WIDTH)

    g_inner = in_order(
        own[:, 2 * cut :].reshape(rows, chips, hidden),
        got[:, 2 * cut :].reshape(rows, chips, hidden),
        2,
    ).reshape(rows, ff)
    g_ibias = small[:, 9 : 9 + hidden // rows].reshape(hidden)
    sm = jnp.transpose(small[:, :9])
    return (
        final_rows.astype(BF16)[None],
        term_weights[None],
        input_grad[None],
        columns(0),
        sm[0],
        columns(wide),
        columns(wide + HALF),
        sm[1],
        g_mixer,
        sm[2],
        sm[3],
        sm[4],
        g_inner,
        g_ibias,
        g_outer,
        sm[5],
        sm[6],
        sm[7],
        sm[8],
    )


def solution(mesh):
    both = ("seq", "ctx")
    tok, mat, vec = P("seq", "ctx", None), P(both, None), P(both)
    term = P("seq", "ctx")
    in_specs = (
        tok, mat, vec, mat, mat, vec, mat, vec, vec, vec,
        mat, vec, mat, vec, vec, vec, vec, tok, term,
    )
    out_specs = (
        tok, term, tok, mat, vec, mat, mat, vec, mat, vec,
        vec, vec, mat, vec, mat, vec, vec, vec, vec,
    )
    return jax.shard_map(
        shards, mesh=mesh, in_specs=in_specs, out_specs=out_specs, check_vma=False
    )
```

time: 413 us -> 755 us (1.83)
  Pallas kernels: 27.9 us -> 442 us
  waiting for transfers between devices: 190 us -> 122 us
  starting transfers between devices: 81.3 us -> 69.3 us
  matrix products: 17.3 us -> 27.7 us
    pallas_call x2 -> x10, Pallas kernels: 27.9 us -> 442 us  [the longest x4 210 us: split(): pl.pallas_call(body, in_specs=[pl.BlockSpec(memory_space=pltpu.SMEM), pl....]
    ppermute x8 -> x10, waiting for transfers between devices: 51.9 us -> 12.1 us  [swap_x(): return lax.ppermute(value, 'seq', [(0, 1), (1, 0)])]
    ppermute x30, waiting for transfers between devices: 88.4 us -> 53.7 us  [shift_z(): return lax.ppermute(value, 'ctx', [(i, (i + 4 * k) % n) for i in range(n)])]
    ppermute x30, starting transfers between devices: 61 us -> 37.7 us  [shift_z(): return lax.ppermute(value, 'ctx', [(i, (i + 4 * k) % n) for i in range(n)])]
    ppermute x23 -> x26, starting transfers between devices: 10.4 us -> 19.1 us  [swap_ctx(): return lax.ppermute(value, 'ctx', [(i, i ^ bit) for i in range(n)])]
    ppermute x23 -> x26, waiting for transfers between devices: 49.3 us -> 56.1 us  [swap_ctx(): return lax.ppermute(value, 'ctx', [(i, i ^ bit) for i in range(n)])]
  transfers between devices with their start and end apart: 61 -> 66, of which waited for: 23 -> 22; matrix products, arithmetic and copies ran while one was open for 18% -> 13% of each run, Pallas kernels for 7% -> 59%
where the time goes in v2:
time: 755 us; the launch traced here: 750 us
  Pallas kernels  442 us (59%)
  waiting for transfers between devices  122 us (16%)
  starting transfers between devices  69.3 us (9%)
  local copies, waits for them, and re-layouts  51.6 us (7%)
  other arithmetic  34.7 us (5%)
  matrix products  27.7 us (4%)
    pallas_call x4, Pallas kernels, split(): pl.pallas_call(body, in_specs=[pl.BlockSpec(memory_space=pltpu.SMEM), pl....  210 us
    pallas_call x4, Pallas kernels, assemble(): pl.pallas_call(body, in_specs=[pl.BlockSpec(memory_space=pltpu.SMEM), pl....  210 us
    ppermute x26, waiting for transfers between devices, swap_ctx(): return lax.ppermute(value, 'ctx', [(i, i ^ bit) for i in range(n)])  56.1 us
    ppermute x30, waiting for transfers between devices, shift_z(): return lax.ppermute(value, 'ctx', [(i, (i + 4 * k) % n) for i in range(n)])  53.7 us
    ppermute x30, starting transfers between devices, shift_z(): return lax.ppermute(value, 'ctx', [(i, (i + 4 * k) % n) for i in range(n)])  37.7 us
    ppermute x26, starting transfers between devices, swap_ctx(): return lax.ppermute(value, 'ctx', [(i, i ^ bit) for i in range(n)])  19.1 us
  transfers between devices with their start and end apart: 66, of which 22 were waited for; matrix products, arithmetic and copies ran while one was open for 13% of the time, Pallas kernels for 59%

profile of v2, /device:TPU:0, one launch (start us, length us, event | category | flops | bytes accessed | tf_op | source)
XLA Modules:
  0.0 749.5 jit_solution(5234869078199354685)
XLA Ops:
  0.7 5.1 collective-permute-start.16
  6.8 2.8 collective-permute-start.29
  40.2 10.1 %collective-permute-done.7 = bf16[48,1280]{1,0:T(8,128)(2,1)S(1)} collective-permute-done((bf16[48,1280]{1,0:T(8,128)(2,1)S(1)}, bf16[48,1280]{1,0:T(8,128)(2,1)S(1)}, u32[]{:S(2)}, u32[]{:S(2)}) %collective-permute-start.7) | collective-permute-done | bytes 122912 | tf_op jit(solution)/shard_map/ppermute | solution.py:55
  50.3 2.9 collective-permute-start.24
  53.2 3.3 collective-permute-start.23
  62.3 8.9 %collective-permute-done.23 = bf16[48,1536]{1,0:T(8,128)(2,1)S(1)} collective-permute-done((bf16[48,1536]{1,0:T(8,128)(2,1)S(1)}, bf16[48,1536]{1,0:T(8,128)(2,1)S(1)}, u32[]{:S(2)}, u32[]{:S(2)}) %collective-permute-start.23) | collective-permute-done | bytes 147488 | tf_op jit(solution)/shard_map/ppermute | solution.py:55
  78.9 4.0 collective-permute-done.18
  85.7 7.8 %collective-permute-done.3 = bf16[4,128,768]{2,1,0:T(8,128)(2,1)} collective-permute-done((bf16[4,128,768]{2,1,0:T(8,128)(2,1)}, bf16[4,128,768]{2,1,0:T(8,128)(2,1)}, u32[]{:S(2)}, u32[]{:S(2)}) %collective-permute-start.3) | collective-permute-done | bytes 786464 | tf_op jit(solution)/shard_map/ppermute | solution.py:38
  97.7 8.5 %collective-permute-done.25 = bf16[4,48,1536]{2,1,0:T(8,128)(2,1)} collective-permute-done((bf16[4,48,1536]{2,1,0:T(8,128)(2,1)}, bf16[4,48,1536]{2,1,0:T(8,128)(2,1)}, u32[]{:S(2)}, u32[]{:S(2)}) %collective-permute-start.25) | collective-permute-done | bytes 589856 | tf_op jit(solution)/shard_map/ppermute | solution.py:38
  110.4 31.7 %assemble.4 = bf16[768,640]{1,0:T(8,128)(2,1)} custom-call(s32[3]{0:T(128)} %pad_add_fusion.at_ref, bf16[2,4,48,640]{3,2,1,0:T(8,128)(2,1)} %pad_maximum_fusion.9.own_ref, bf16[2,4,48,640]{3,2,1,0:T(8,128)(2,1)} %collective-permute-done.10.other_ref), custom_call_target="tpu_custom_call" | custom-call | tf_op jit(solution)/shard_map/assemble/pallas_call | solution.py:108
  143.2 31.7 %assemble.5 = bf16[768,640]{1,0:T(8,128)(2,1)} custom-call(s32[3]{0:T(128)} %pad_add_fusion.at_ref, bf16[2,4,48,640]{3,2,1,0:T(8,128)(2,1)} %pad_maximum_fusion.10.own_ref, bf16[2,4,48,640]{3,2,1,0:T(8,128)(2,1)} %collective-permute-done.12.other_ref), custom_call_target="tpu_custom_call" | custom-call | tf_op jit(solution)/shard_map/assemble/pallas_call | solution.py:108
  178.7 10.2 %attend.1 = (bf16[256,384]{1,0:T(8,128)(2,1)S(1)}, bf16[1024,768]{1,0:T(8,128)(2,1)S(1)}, bf16[1024,768]{1,0:T(8,128)(2,1)S(1)}, f32[384,256]{1,0:T(8,128)S(1)},...) custom-call(bf16[1024,768]{1,0:T(8,128)(2,1)S(1)} %bitcast.284, bf16[1024,768]{1,0:T(8,128)(2,1)S(1)} %collective-permute-done.4.xc_ref, ...), custom_call_target="tpu_custom_call" | custom-call | flops 3221225472 | bytes 6291456 | tf_op jit(solution)/shard_map/attend/pallas_call | solution.py:259
  195.8 73.4 %assemble.7 = bf16[1536,768]{1,0:T(8,128)(2,1)} custom-call(s32[3]{0:T(128)} %pad_add_fusion.at_ref, bf16[2,4,96,768]{3,2,1,0:T(8,128)(2,1)} %pad_maximum_fusion.3.own_ref, bf16[2,4,96,768]{3,2,1,0:T(8,128)(2,1)} %collective-permute-done.31.other_ref), custom_call_target="tpu_custom_call" | custom-call | tf_op jit(solution)/shard_map/assemble/pallas_call | solution.py:108
  269.2 73.4 %assemble.6 = bf16[768,1536]{1,0:T(8,128)(2,1)} custom-call(s32[3]{0:T(128)} %pad_add_fusion.at_ref, bf16[2,4,48,1536]{3,2,1,0:T(8,128)(2,1)} %pad_maximum_fusion.2.own_ref, bf16[2,4,48,1536]{3,2,1,0:T(8,128)(2,1)} %collective-permute-done.26.other_ref), custom_call_target="tpu_custom_call" | custom-call | tf_op jit(solution)/shard_map/assemble/pallas_call | solution.py:108
  342.7 3.8 multiply_convert_fusion
  360.2 4.1 convert_reduce_fusion
  369.1 73.4 %split.6 = (bf16[2,4,48,1536]{3,2,1,0:T(8,128)(2,1)}, bf16[2,4,48,1536]{3,2,1,0:T(8,128)(2,1)}) custom-call(s32[3]{0:T(128)} %pad_add_fusion.at_ref, bf16[768,1536]{1,0:T(8,128)(2,1)} %convolution_convert_fusion.1.part_ref), custom_call_target="tpu_custom_call" | custom-call | tf_op jit(solution)/shard_map/split/pallas_call | solution.py:151
  448.9 3.3 convolution_convert_fusion.part_ref
  452.3 73.5 %split.7 = (bf16[2,4,96,768]{3,2,1,0:T(8,128)(2,1)}, bf16[2,4,96,768]{3,2,1,0:T(8,128)(2,1)}) custom-call(s32[3]{0:T(128)} %pad_add_fusion.at_ref, bf16[1536,768]{1,0:T(8,128)(2,1)} %convolution_convert_fusion.part_ref), custom_call_target="tpu_custom_call" | custom-call | tf_op jit(solution)/shard_map/split/pallas_call | solution.py:151
  536.1 10.7 %attend_back.1 = (bf16[256,384]{1,0:T(8,128)(2,1)S(1)}, bf16[1024,768]{1,0:T(8,128)(2,1)S(1)}, bf16[1024,768]{1,0:T(8,128)(2,1)S(1)}) custom-call(bf16[256,384]{1,0:T(8,128)(2,1)S(1)} %get-tuple-element.37.q_ref, bf16[128,384]{1,0:T(8,128)(2,1)S(1)} %bitcast.282, bf16[128,384]{1,0:T(8,128)(2,1)S(1)} %collective-permute-done.35.gc_ref, ...), custom_call_target="tpu_custom_call" | custom-call | flops 2013265920 | bytes 6291456 | tf_op jit(solution)/shard_map/attend_back/pallas_call | solution.py:339
  556.8 2.7 concatenate.60
  561.5 31.8 %split.4 = (bf16[2,4,48,640]{3,2,1,0:T(8,128)(2,1)}, bf16[2,4,48,640]{3,2,1,0:T(8,128)(2,1)}) custom-call(s32[3]{0:T(128)} %pad_add_fusion.at_ref, bf16[768,640]{1,0:T(8,128)(2,1)} %get-tuple-element.89.part_ref), custom_call_target="tpu_custom_call" | custom-call | tf_op jit(solution)/shard_map/split/pallas_call | solution.py:151
  593.9 31.7 %split.5 = (bf16[2,4,48,640]{3,2,1,0:T(8,128)(2,1)}, bf16[2,4,48,640]{3,2,1,0:T(8,128)(2,1)}) custom-call(s32[3]{0:T(128)} %pad_add_fusion.at_ref, bf16[768,640]{1,0:T(8,128)(2,1)} %get-tuple-element.90.part_ref), custom_call_target="tpu_custom_call" | custom-call | tf_op jit(solution)/shard_map/split/pallas_call | solution.py:151
  630.5 8.8 %collective-permute-done.44 = bf16[2,4,48,640]{3,2,1,0:T(8,128)(2,1)S(1)} collective-permute-done((bf16[2,4,48,640]{3,2,1,0:T(8,128)(2,1)}, bf16[2,4,48,640]{3,2,1,0:T(8,128)(2,1)S(1)}, u32[]{:S(2)}, u32[]{:S(2)}) %collective-permute-start.44) | collective-permute-done | bytes 491552 | tf_op jit(solution)/shard_map/ppermute | solution.py:38
  650.5 11.9 %collective-permute-done.57 = bf16[4,24,768]{2,1,0:T(8,128)(2,1)S(1)} collective-permute-done((bf16[4,24,768]{2,1,0:T(8,128)(2,1)S(1)}, bf16[4,24,768]{2,1,0:T(8,128)(2,1)S(1)}, u32[]{:S(2)}, u32[]{:S(2)}) %collective-permute-start.57) | collective-permute-done | bytes 147488 | tf_op jit(solution)/shard_map/ppermute | solution.py:38
  662.4 3.9 collective-permute-start.60
  676.8 8.1 %collective-permute-done.62 = bf16[4,96,768]{2,1,0:T(8,128)(2,1)S(1)} collective-permute-done((bf16[4,96,768]{2,1,0:T(8,128)(2,1)S(1)}, bf16[4,96,768]{2,1,0:T(8,128)(2,1)S(1)}, u32[]{:S(2)}, u32[]{:S(2)}) %collective-permute-start.62) | collective-permute-done | bytes 589856 | tf_op jit(solution)/shard_map/ppermute | solution.py:50
  686.9 3.1 collective-permute-start.65
  694.8 10.3 %collective-permute-done.64 = bf16[96,768]{1,0:T(8,128)(2,1)S(1)} collective-permute-done((bf16[96,768]{1,0:T(8,128)(2,1)S(1)}, bf16[96,768]{1,0:T(8,128)(2,1)S(1)}, u32[]{:S(2)}, u32[]{:S(2)}) %collective-permute-start.64) | collective-permute-done | bytes 147488 | tf_op jit(solution)/shard_map/ppermute | solution.py:55
  705.9 2.8 add_convert_fusion
  714.1 14.3 %collective-permute-done.38 = bf16[4,128,768]{2,1,0:T(8,128)(2,1)S(1)} collective-permute-done((bf16[4,128,768]{2,1,0:T(8,128)(2,1)S(1)}, bf16[4,128,768]{2,1,0:T(8,128)(2,1)S(1)}, u32[]{:S(2)}, u32[]{:S(2)}) %collective-permute-start.38) | collective-permute-done | bytes 786464 | tf_op jit(solution)/shard_map/ppermute | solution.py:38
  736.8 10.5 %collective-permute-done.40 = bf16[128,768]{1,0:T(8,128)(2,1)S(1)} collective-permute-done((bf16[128,768]{1,0:T(8,128)(2,1)}, bf16[128,768]{1,0:T(8,128)(2,1)S(1)}, u32[]{:S(2)}, u32[]{:S(2)}) %collective-permute-start.40) | collective-permute-done | bytes 196640 | tf_op jit(solution)/shard_map/ppermute | solution.py:55
  (417 shorter events, 164.2 us)
Async XLA Ops:
  0.7 23.6 %collective-permute-start.16 = (bf16[24,768]{1,0:T(8,128)(2,1)}, bf16[24,768]{1,0:T(8,128)(2,1)S(1)}, u32[]{:S(2)}, u32[]{:S(2)}) collective-permute-start(bf16[24,768]{1,0:T(8,128)(2,1)} %param.25), channel_id=1, source_target_pairs={{0,12},{1,13},{2,14},{3,15},{4,0},{5,1},{6,2},{7,3},{8,4},{9,5},{1... | collective-permute-start | bytes 110600 | tf_op jit(solution)/shard_map/ppermute | solution.py:55
  5.8 18.5 %collective-permute-start.15 = (bf16[24,768]{1,0:T(8,128)(2,1)}, bf16[24,768]{1,0:T(8,128)(2,1)S(1)}, u32[]{:S(2)}, u32[]{:S(2)}) collective-permute-start(bf16[24,768]{1,0:T(8,128)(2,1)} %param.25), channel_id=1, source_target_pairs={{0,8},{1,9},{2,10},{3,11},{4,12},{5,13},{6,14},{7,15},{8,0},{9,1},... | collective-permute-start | bytes 110600 | tf_op jit(solution)/shard_map/ppermute | solution.py:55
  5.8 18.6 %collective-permute-start.14 = (bf16[24,768]{1,0:T(8,128)(2,1)}, bf16[24,768]{1,0:T(8,128)(2,1)S(1)}, u32[]{:S(2)}, u32[]{:S(2)}) collective-permute-start(bf16[24,768]{1,0:T(8,128)(2,1)} %param.25), channel_id=1, source_target_pairs={{0,4},{1,5},{2,6},{3,7},{4,8},{5,9},{6,10},{7,11},{8,12},{9,13},{1... | collective-permute-start | bytes 110600 | tf_op jit(solution)/shard_map/ppermute | solution.py:55
  6.8 22.8 %collective-permute-start.29 = (bf16[96,768]{1,0:T(8,128)(2,1)}, bf16[96,768]{1,0:T(8,128)(2,1)S(1)}, u32[]{:S(2)}, u32[]{:S(2)}) collective-permute-start(bf16[96,768]{1,0:T(8,128)(2,1)} %param.31), channel_id=1, source_target_pairs={{0,12},{1,13},{2,14},{3,15},{4,0},{5,1},{6,2},{7,3},{8,4},{9,5},{1... | collective-permute-start | bytes 442376 | tf_op jit(solution)/shard_map/ppermute | solution.py:55
  9.6 21.6 %collective-permute-start.28 = (bf16[96,768]{1,0:T(8,128)(2,1)}, bf16[96,768]{1,0:T(8,128)(2,1)S(1)}, u32[]{:S(2)}, u32[]{:S(2)}) collective-permute-start(bf16[96,768]{1,0:T(8,128)(2,1)} %param.31), channel_id=1, source_target_pairs={{0,8},{1,9},{2,10},{3,11},{4,12},{5,13},{6,14},{7,15},{8,0},{9,1},... | collective-permute-start | bytes 442376 | tf_op jit(solution)/shard_map/ppermute | solution.py:55
  25.7 31.0 %collective-permute-start = (bf16[128,768]{1,0:T(8,128)(2,1)S(1)}, bf16[128,768]{1,0:T(8,128)(2,1)S(1)}, u32[]{:S(2)}, u32[]{:S(2)}) collective-permute-start(bf16[128,768]{1,0:T(8,128)(2,1)S(1)} %bitcast.293), channel_id=1, source_target_pairs={{0,4},{1,5},{2,6},{3,7},{4,8},{5,9},{6,10},{7,11},{8,12},{9,13},{1... | collective-permute-start | bytes 589832 | tf_op jit(solution)/shard_map/ppermute | solution.py:55
  31.2 19.1 %collective-permute-start.7 = (bf16[48,1280]{1,0:T(8,128)(2,1)S(1)}, bf16[48,1280]{1,0:T(8,128)(2,1)S(1)}, u32[]{:S(2)}, u32[]{:S(2)}) collective-permute-start(bf16[48,1280]{1,0:T(8,128)(2,1)S(1)} %bitcast.312), channel_id=1, source_target_pairs={{0,8},{1,9},{2,10},{3,11},{4,12},{5,13},{6,14},{7,15},{8,0},{9,1},... | collective-permute-start | bytes 368648 | tf_op jit(solution)/shard_map/ppermute | solution.py:55
  32.2 21.0 %collective-permute-start.6 = (bf16[48,1280]{1,0:T(8,128)(2,1)S(1)}, bf16[48,1280]{1,0:T(8,128)(2,1)S(1)}, u32[]{:S(2)}, u32[]{:S(2)}) collective-permute-start(bf16[48,1280]{1,0:T(8,128)(2,1)S(1)} %bitcast.313), channel_id=1, source_target_pairs={{0,4},{1,5},{2,6},{3,7},{4,8},{5,9},{6,10},{7,11},{8,12},{9,13},{1... | collective-permute-start | bytes 368648 | tf_op jit(solution)/shard_map/ppermute | solution.py:55
  34.9 22.3 %collective-permute-start.1 = (bf16[128,768]{1,0:T(8,128)(2,1)S(1)}, bf16[128,768]{1,0:T(8,128)(2,1)S(1)}, u32[]{:S(2)}, u32[]{:S(2)}) collective-permute-start(bf16[128,768]{1,0:T(8,128)(2,1)S(1)} %bitcast.294), channel_id=1, source_target_pairs={{0,8},{1,9},{2,10},{3,11},{4,12},{5,13},{6,14},{7,15},{8,0},{9,1},... | collective-permute-start | bytes 589832 | tf_op jit(solution)/shard_map/ppermute | solution.py:55
  38.1 20.7 %collective-permute-start.2 = (bf16[128,768]{1,0:T(8,128)(2,1)S(1)}, bf16[128,768]{1,0:T(8,128)(2,1)S(1)}, u32[]{:S(2)}, u32[]{:S(2)}) collective-permute-start(bf16[128,768]{1,0:T(8,128)(2,1)S(1)} %bitcast.295), channel_id=1, source_target_pairs={{0,12},{1,13},{2,14},{3,15},{4,0},{5,1},{6,2},{7,3},{8,4},{9,5},{1... | collective-permute-start | bytes 589832 | tf_op jit(solution)/shard_map/ppermute | solution.py:55
  53.2 18.1 %collective-permute-start.23 = (bf16[48,1536]{1,0:T(8,128)(2,1)S(1)}, bf16[48,1536]{1,0:T(8,128)(2,1)S(1)}, u32[]{:S(2)}, u32[]{:S(2)}) collective-permute-start(bf16[48,1536]{1,0:T(8,128)(2,1)S(1)} %bitcast.308), channel_id=1, source_target_pairs={{0,8},{1,9},{2,10},{3,11},{4,12},{5,13},{6,14},{7,15},{8,0},{9,1},... | collective-permute-start | bytes 442376 | tf_op jit(solution)/shard_map/ppermute | solution.py:55
  57.2 37.5 %collective-permute-start.30 = (bf16[4,96,768]{2,1,0:T(8,128)(2,1)}, bf16[4,96,768]{2,1,0:T(8,128)(2,1)}, u32[]{:S(2)}, u32[]{:S(2)}) collective-permute-start(bf16[4,96,768]{2,1,0:T(8,128)(2,1)} %get-tuple-element.103), channel_id=1, source_target_pairs={{0,16},{16,0},{1,17},{17,1},{2,18},{18,2},{3,19},{19,3},{4,20},{20... | collective-permute-start | bytes 1769480 | tf_op jit(solution)/shard_map/ppermute | solution.py:50
  72.8 20.8 %collective-permute-start.3 = (bf16[4,128,768]{2,1,0:T(8,128)(2,1)}, bf16[4,128,768]{2,1,0:T(8,128)(2,1)}, u32[]{:S(2)}, u32[]{:S(2)}) collective-permute-start(bf16[4,128,768]{2,1,0:T(8,128)(2,1)} %pad_maximum_fusion.4), channel_id=1, source_target_pairs={{0,2},{1,3},{2,0},{3,1},{4,6},{5,7},{6,4},{7,5},{8,10},{9,11},{10,... | collective-permute-start | bytes 2359304 | tf_op jit(solution)/shard_map/ppermute | solution.py:38
  75.4 30.7 %collective-permute-start.25 = (bf16[4,48,1536]{2,1,0:T(8,128)(2,1)}, bf16[4,48,1536]{2,1,0:T(8,128)(2,1)}, u32[]{:S(2)}, u32[]{:S(2)}) collective-permute-start(bf16[4,48,1536]{2,1,0:T(8,128)(2,1)} %get-tuple-element.105), channel_id=1, source_target_pairs={{0,2},{1,3},{2,0},{3,1},{4,6},{5,7},{6,4},{7,5},{8,10},{9,11},{10,... | collective-permute-start | bytes 1769480 | tf_op jit(solution)/shard_map/ppermute | solution.py:38
  76.8 33.1 %collective-permute-start.10 = (bf16[2,4,48,640]{3,2,1,0:T(8,128)(2,1)}, bf16[2,4,48,640]{3,2,1,0:T(8,128)(2,1)}, u32[]{:S(2)}, u32[]{:S(2)}) collective-permute-start(bf16[2,4,48,640]{3,2,1,0:T(8,128)(2,1)} %pad_maximum_fusion.9.own_ref), channel_id=1, source_target_pairs={{0,16},{16,0},{1,17},{17,1},{2,18},{18,2},{3,19},{19,3},{4,20},{20... | collective-permute-start | bytes 1474568 | tf_op jit(solution)/shard_map/ppermute | solution.py:50
  82.9 60.3 %collective-permute-start.12 = (bf16[2,4,48,640]{3,2,1,0:T(8,128)(2,1)}, bf16[2,4,48,640]{3,2,1,0:T(8,128)(2,1)}, u32[]{:S(2)}, u32[]{:S(2)}) collective-permute-start(bf16[2,4,48,640]{3,2,1,0:T(8,128)(2,1)} %pad_maximum_fusion.10.own_ref), channel_id=1, source_target_pairs={{0,2},{1,3},{2,0},{3,1},{4,6},{5,7},{6,4},{7,5},{8,10},{9,11},{10,... | collective-permute-start | bytes 1474568 | tf_op jit(solution)/shard_map/ppermute | solution.py:38
  93.5 83.8 %collective-permute-start.19 = (bf16[16,24,768]{2,1,0:T(8,128)(2,1)}, bf16[16,24,768]{2,1,0:T(8,128)(2,1)}, u32[]{:S(2)}, u32[]{:S(2)}) collective-permute-start(bf16[16,24,768]{2,1,0:T(8,128)(2,1)} %bitcast.42), channel_id=1, source_target_pairs={{0,1},{1,0},{2,3},{3,2},{4,5},{5,4},{6,7},{7,6},{8,9},{9,8},{10,11... | collective-permute-start | bytes 1769480 | tf_op jit(solution)/shard_map/ppermute | solution.py:38
  94.8 83.9 %collective-permute-start.4 = (bf16[1024,768]{1,0:T(8,128)(2,1)S(1)}, bf16[1024,768]{1,0:T(8,128)(2,1)S(1)}, u32[]{:S(2)}, u32[]{:S(2)}) collective-permute-start(bf16[1024,768]{1,0:T(8,128)(2,1)S(1)} %bitcast.283), channel_id=1, source_target_pairs={{0,1},{1,0},{2,3},{3,2},{4,5},{5,4},{6,7},{7,6},{8,9},{9,8},{10,11... | collective-permute-start | bytes 4718600 | tf_op jit(solution)/shard_map/ppermute | solution.py:38
  106.2 89.6 %collective-permute-start.31 = (bf16[2,4,96,768]{3,2,1,0:T(8,128)(2,1)}, bf16[2,4,96,768]{3,2,1,0:T(8,128)(2,1)}, u32[]{:S(2)}, u32[]{:S(2)}) collective-permute-start(bf16[2,4,96,768]{3,2,1,0:T(8,128)(2,1)} %pad_maximum_fusion.3.own_ref), channel_id=1, source_target_pairs={{0,2},{1,3},{2,0},{3,1},{4,6},{5,7},{6,4},{7,5},{8,10},{9,11},{10,... | collective-permute-start | bytes 3538952 | tf_op jit(solution)/shard_map/ppermute | solution.py:38
  109.9 159.3 %collective-permute-start.26 = (bf16[2,4,48,1536]{3,2,1,0:T(8,128)(2,1)}, bf16[2,4,48,1536]{3,2,1,0:T(8,128)(2,1)}, u32[]{:S(2)}, u32[]{:S(2)}) collective-permute-start(bf16[2,4,48,1536]{3,2,1,0:T(8,128)(2,1)} %pad_maximum_fusion.2.own_ref), channel_id=1, source_target_pairs={{0,16},{16,0},{1,17},{17,1},{2,18},{18,2},{3,19},{19,3},{4,20},{20... | collective-permute-start | bytes 3538952 | tf_op jit(solution)/shard_map/ppermute | solution.py:50
  194.4 148.2 %collective-permute-start.20 = (bf16[128,768]{1,0:T(8,128)(2,1)S(1)}, bf16[128,768]{1,0:T(8,128)(2,1)S(1)}, u32[]{:S(2)}, u32[]{:S(2)}) collective-permute-start(bf16[128,768]{1,0:T(8,128)(2,1)S(1)} %fusion.39), channel_id=1, source_target_pairs={{0,1},{1,0},{2,3},{3,2},{4,5},{5,4},{6,7},{7,6},{8,9},{9,8},{10,11... | collective-permute-start | bytes 589832 | tf_op jit(solution)/shard_map/ppermute | solution.py:38
  366.8 159.6 %collective-permute-start.34 = (f32[128,768]{1,0:T(8,128)}, f32[128,768]{1,0:T(8,128)}, u32[]{:S(2)}, u32[]{:S(2)}) collective-permute-start(f32[128,768]{1,0:T(8,128)} %slice.413), channel_id=1, source_target_pairs={{0,1},{1,0},{2,3},{3,2},{4,5},{5,4},{6,7},{7,6},{8,9},{9,8},{10,11... | collective-permute-start | bytes 1179656 | tf_op jit(solution)/shard_map/ppermute | solution.py:38
  442.5 198.4 %collective-permute-start.49 = (bf16[2,4,48,1536]{3,2,1,0:T(8,128)(2,1)}, bf16[2,4,48,1536]{3,2,1,0:T(8,128)(2,1)}, u32[]{:S(2)}, u32[]{:S(2)}) collective-permute-start(bf16[2,4,48,1536]{3,2,1,0:T(8,128)(2,1)} %get-tuple-element.50), channel_id=1, source_target_pairs={{0,16},{16,0},{1,17},{17,1},{2,18},{18,2},{3,19},{19,3},{4,20},{20... | collective-permute-start | bytes 3538952 | tf_op jit(solution)/shard_map/ppermute | solution.py:50
  525.8 117.8 %collective-permute-start.61 = (bf16[2,4,96,768]{3,2,1,0:T(8,128)(2,1)}, bf16[2,4,96,768]{3,2,1,0:T(8,128)(2,1)}, u32[]{:S(2)}, u32[]{:S(2)}) collective-permute-start(bf16[2,4,96,768]{3,2,1,0:T(8,128)(2,1)} %get-tuple-element.52), channel_id=1, source_target_pairs={{0,2},{1,3},{2,0},{3,1},{4,6},{5,7},{6,4},{7,5},{8,10},{9,11},{10,... | collective-permute-start | bytes 3538952 | tf_op jit(solution)/shard_map/ppermute | solution.py:38
  535.5 90.1 %collective-permute-start.55 = (bf16[16,24,768]{2,1,0:T(8,128)(2,1)}, bf16[16,24,768]{2,1,0:T(8,128)(2,1)}, u32[]{:S(2)}, u32[]{:S(2)}) collective-permute-start(bf16[16,24,768]{2,1,0:T(8,128)(2,1)} %dynamic-slice_bitcast_fusion), channel_id=1, source_target_pairs={{0,1},{1,0},{2,3},{3,2},{4,5},{5,4},{6,7},{7,6},{8,9},{9,8},{10,11... | collective-permute-start | bytes 1769480 | tf_op jit(solution)/shard_map/ppermute | solution.py:38
  550.6 155.3 %collective-permute-start.37 = (bf16[1024,768]{1,0:T(8,128)(2,1)}, bf16[1024,768]{1,0:T(8,128)(2,1)}, u32[]{:S(2)}, u32[]{:S(2)}) collective-permute-start(bf16[1024,768]{1,0:T(8,128)(2,1)} %convolution_convert_fusion.2), channel_id=1, source_target_pairs={{0,1},{1,0},{2,3},{3,2},{4,5},{5,4},{6,7},{7,6},{8,9},{9,8},{10,11... | collective-permute-start | bytes 4718600 | tf_op jit(solution)/shard_map/ppermute | solution.py:38
  593.3 35.6 %collective-permute-start.42 = (bf16[2,4,48,640]{3,2,1,0:T(8,128)(2,1)}, bf16[2,4,48,640]{3,2,1,0:T(8,128)(2,1)S(1)}, u32[]{:S(2)}, u32[]{:S(2)}) collective-permute-start(bf16[2,4,48,640]{3,2,1,0:T(8,128)(2,1)} %get-tuple-element.46), channel_id=1, source_target_pairs={{0,16},{16,0},{1,17},{17,1},{2,18},{18,2},{3,19},{19,3},{4,20},{20... | collective-permute-start | bytes 1474568 | tf_op jit(solution)/shard_map/ppermute | solution.py:50
  628.9 19.2 %collective-permute-start.56 = (bf16[2,4,24,768]{3,2,1,0:T(8,128)(2,1)S(1)}, bf16[2,4,24,768]{3,2,1,0:T(8,128)(2,1)S(1)}, u32[]{:S(2)}, u32[]{:S(2)}) collective-permute-start(bf16[2,4,24,768]{3,2,1,0:T(8,128)(2,1)S(1)} %copy_bitcast_fusion), channel_id=1, source_target_pairs={{0,16},{16,0},{1,17},{17,1},{2,18},{18,2},{3,19},{19,3},{4,20},{20... | collective-permute-start | bytes 884744 | tf_op jit(solution)/shard_map/ppermute | solution.py:50
  643.6 31.9 %collective-permute-start.50 = (bf16[4,48,1536]{2,1,0:T(8,128)(2,1)S(1)}, bf16[4,48,1536]{2,1,0:T(8,128)(2,1)S(1)}, u32[]{:S(2)}, u32[]{:S(2)}) collective-permute-start(bf16[4,48,1536]{2,1,0:T(8,128)(2,1)S(1)} %fusion.20), channel_id=1, source_target_pairs={{0,2},{1,3},{2,0},{3,1},{4,6},{5,7},{6,4},{7,5},{8,10},{9,11},{10,... | collective-permute-start | bytes 1769480 | tf_op jit(solution)/shard_map/ppermute | solution.py:38
  669.1 66.8 %collective-permute-start.36 = (f32[128,768]{1,0:T(8,128)}, f32[128,768]{1,0:T(8,128)}, u32[]{:S(2)}, u32[]{:S(2)}) collective-permute-start(f32[128,768]{1,0:T(8,128)} %slice.416), channel_id=1, source_target_pairs={{0,1},{1,0},{2,3},{3,2},{4,5},{5,4},{6,7},{7,6},{8,9},{9,8},{10,11... | collective-permute-start | bytes 1179656 | tf_op jit(solution)/shard_map/ppermute | solution.py:38
  708.9 19.5 %collective-permute-start.38 = (bf16[4,128,768]{2,1,0:T(8,128)(2,1)S(1)}, bf16[4,128,768]{2,1,0:T(8,128)(2,1)S(1)}, u32[]{:S(2)}, u32[]{:S(2)}) collective-permute-start(bf16[4,128,768]{2,1,0:T(8,128)(2,1)S(1)} %bitcast.306), channel_id=1, source_target_pairs={{0,2},{1,3},{2,0},{3,1},{4,6},{5,7},{6,4},{7,5},{8,10},{9,11},{10,... | collective-permute-start | bytes 2359304 | tf_op jit(solution)/shard_map/ppermute | solution.py:38
  729.4 17.8 %collective-permute-start.40 = (bf16[128,768]{1,0:T(8,128)(2,1)}, bf16[128,768]{1,0:T(8,128)(2,1)S(1)}, u32[]{:S(2)}, u32[]{:S(2)}) collective-permute-start(bf16[128,768]{1,0:T(8,128)(2,1)} %get-tuple-element.95), channel_id=1, source_target_pairs={{0,8},{1,9},{2,10},{3,11},{4,12},{5,13},{6,14},{7,15},{8,0},{9,1},... | collective-permute-start | bytes 589832 | tf_op jit(solution)/shard_map/ppermute | solution.py:55
  (97 other events, 1911.4 us)

commit v3 on v1

v3 whole, which is shorter than its diff:
```python
import math

import jax
import jax.numpy as jnp
from jax import lax
from jax.experimental import pallas as pl
from jax.experimental.pallas import tpu as pltpu
from jax.sharding import PartitionSpec as P

HEADS = 12
HD = 64
WIDTH = HEADS * HD
HALF = WIDTH // 2
NH = HEADS // 2
EPSILON = 1e-12
ROOT_HALF = 0.7071067811865476
GAUSS_FACTOR = 0.3989422804014327
F32 = jnp.float32
BF16 = jnp.bfloat16
AUX = 128
WIDE = HALF + AUX
MIB = 2**20


def mm(a, b):
    return lax.dot_general(a, b, (((1,), (0,)), ((), ())), preferred_element_type=F32)


def mm_t(a, b):
    return lax.dot_general(a, b, (((1,), (1,)), ((), ())), preferred_element_type=F32)


def t_mm(a, b):
    return lax.dot_general(a, b, (((0,), (0,)), ((), ())), preferred_element_type=F32)


def shape(dims, dtype):
    return jax.ShapeDtypeStruct(dims, dtype)


def swap_ctx(value, bit):
    n = lax.axis_size("ctx")
    return lax.ppermute(value, "ctx", [(i, i ^ bit) for i in range(n)])


def swap_core(value):
    return swap_ctx(value, 1)


def swap_y(value):
    return swap_ctx(value, 2)


def swap_x(value):
    return lax.ppermute(value, "seq", [(0, 1), (1, 0)])


def shift_z(value, k):
    n = lax.axis_size("ctx")
    return lax.ppermute(value, "ctx", [(i, (i + 4 * k) % n) for i in range(n)])


def place():
    at = lax.axis_index("ctx")
    return lax.axis_index("seq"), at // 4, (at // 2) % 2, at % 2


def z_groups():
    n = lax.axis_size("ctx")
    return [[i + 4 * j for j in range(n // 4)] for i in range(4)]


def turned(blocks, start, forward):
    zs = blocks.shape[0]
    if not forward:
        blocks, start = jnp.flip(blocks, 0), zs - 1 - start
    return lax.dynamic_slice_in_dim(jnp.concatenate([blocks, blocks]), start, zs, 0)


def along_z(block):
    zs = lax.axis_size("ctx") // 4
    if zs > 4:
        every = lax.all_gather(block, "ctx", axis_index_groups=z_groups())
        return turned(every, lax.axis_index("ctx") // 4, False)
    return jnp.stack([block] + [shift_z(block, k) for k in range(1, zs)])


def sum_z(along):
    zs = lax.axis_size("ctx") // 4
    if zs > 4:
        every = turned(along, (zs - lax.axis_index("ctx") // 4) % zs, True)
        every = lax.all_to_all(every, "ctx", 0, 0, axis_index_groups=z_groups())
        return jnp.sum(every.astype(F32), axis=0)
    total = along[0].astype(F32)
    for k in range(1, zs):
        total = total + shift_z(along[k], k).astype(F32)
    return total


def to_mesh_order(blocks):
    x, z, y, _ = place()
    zs = blocks.shape[2]
    blocks = jnp.concatenate([blocks[:, :, :1], jnp.flip(blocks[:, :, 1:], 2)], axis=2)
    blocks = lax.dynamic_slice_in_dim(jnp.concatenate([blocks, blocks], axis=2), zs - z, zs, 2)
    for axis, bit in enumerate((x, y)):
        blocks = jnp.where(bit == 0, blocks, jnp.flip(blocks, axis))
    return jnp.swapaxes(blocks, 1, 2)


def to_distance(blocks):
    x, z, y, _ = place()
    zs = blocks.shape[1]
    blocks = jnp.swapaxes(blocks, 1, 2)
    blocks = lax.dynamic_slice_in_dim(jnp.concatenate([blocks, blocks], axis=2), z, zs, 2)
    for axis, bit in enumerate((x, y)):
        blocks = jnp.where(bit == 0, blocks, jnp.flip(blocks, axis))
    return blocks


def after(value, *ready):
    return lax.optimization_barrier((value, *ready))[0]


def chip_of(here, xr, yr, k, zs):
    x, z, y, _ = here
    return ((x ^ xr) * zs + lax.rem(z + k + zs, zs)) * 2 + (y ^ yr)


def rows_at(chip, rows):
    return pl.ds(pl.multiple_of(chip * rows, 16), rows)


def kernel(body, args, outs, name, limit=14, scratch=(), flops=0, bytes_accessed=0):
    return pl.pallas_call(
        body,
        in_specs=[pl.BlockSpec(memory_space=pltpu.VMEM) for _ in args],
        out_specs=[pl.BlockSpec(memory_space=pltpu.VMEM) for _ in outs],
        out_shape=list(outs),
        scratch_shapes=list(scratch),
        compiler_params=pltpu.CompilerParams(vmem_limit_bytes=limit * MIB),
        cost_estimate=pl.CostEstimate(
            flops=flops, bytes_accessed=bytes_accessed, transcendentals=0
        ),
        name=name,
    )(*args)


def build_qkv(along, by_y, by_x, far_a, far_b):
    zs, rows, _ = along.shape
    cut = zs // 2
    ends = (0, WIDE, WIDE + WIDTH, WIDE + WIDTH + HALF)
    if rows % 16:
        far = jnp.concatenate([far_a, far_b])
        full = to_mesh_order(jnp.stack([along, by_y, by_x, far]).reshape(2, 2, zs, rows, -1))
        full = full.reshape(WIDTH, -1)
        return [full[:, lo:hi] for lo, hi in zip(ends, ends[1:])]

    def body(al_ref, y_ref, x_ref, fa_ref, fb_ref, *outs):
        here = place()
        for k in range(zs):
            far = (fa_ref, k) if k < cut else (fb_ref, k - cut)
            for xr, yr, (ref, i) in (
                (0, 0, (al_ref, k)),
                (0, 1, (y_ref, k)),
                (1, 0, (x_ref, k)),
                (1, 1, far),
            ):
                to = rows_at(chip_of(here, xr, yr, -k, zs), rows)
                for out, lo, hi in zip(outs, ends, ends[1:]):
                    out[to, :] = ref[i, :, lo:hi]

    return kernel(
        body,
        (along, by_y, by_x, far_a, far_b),
        [shape((WIDTH, hi - lo), BF16) for lo, hi in zip(ends, ends[1:])],
        "build_qkv",
        flops=10**6,
        bytes_accessed=4 * 10**6,
    )


def build_rest(along, by_y, by_x, far_a, far_b, rows, hidden):
    zs = along.shape[0]
    quarters = zs * 4 * hidden // HALF
    first = quarters * rows
    units = zs * 4 * hidden
    if rows % 16:
        far = jnp.concatenate([far_a, far_b], axis=1)
        full = to_mesh_order(
            jnp.stack([along, by_y, by_x, far]).reshape(2, 2, zs, -1, HALF)
        ).reshape(4 * zs, -1, HALF)
        w1 = jnp.swapaxes(full[:, :first].reshape(4 * zs, quarters, rows, HALF), 1, 2)
        w2 = jnp.swapaxes(full[:, first:].reshape(4 * zs, 2, hidden, HALF), 1, 2)
        return w1.reshape(WIDTH, units), w2.reshape(units, WIDTH)

    def body(al_ref, y_ref, x_ref, fa_ref, fb_ref, w1_ref, w2_ref):
        here = place()
        for k in range(zs):
            for xr, yr, ref, low, back in (
                (0, 0, al_ref, al_ref, 0),
                (0, 1, y_ref, y_ref, 0),
                (1, 0, x_ref, x_ref, 0),
                (1, 1, fa_ref, fb_ref, first),
            ):
                chip = chip_of(here, xr, yr, -k, zs)
                to, down = rows_at(chip, rows), rows_at(chip, hidden)
                for j in range(quarters):
                    w1_ref[to, j * HALF : (j + 1) * HALF] = ref[k, j * rows : (j + 1) * rows, :]
                for j in range(2):
                    lo = first + j * hidden - back
                    w2_ref[down, j * HALF : (j + 1) * HALF] = low[k, lo : lo + hidden, :]

    return kernel(
        body,
        (along, by_y, by_x, far_a, far_b),
        (shape((WIDTH, units), BF16), shape((units, WIDTH), BF16)),
        "build_rest",
        flops=10**6,
        bytes_accessed=10**7,
    )


def whole_spec(*dims):
    return pl.BlockSpec(dims, lambda i: (0,) * len(dims))


def attend_step(q_ref, kv_ref, m_ref, l_ref, acc_ref):
    for h in range(NH):
        lo = h * HD
        qh = q_ref[:, lo : lo + HD]
        kh = kv_ref[:, lo : lo + HD]
        vh = kv_ref[:, HALF + lo : HALF + lo + HD]
        s = mm_t(kh, qh)
        before = m_ref[h : h + 1, :]
        top = jnp.maximum(before, jnp.max(s, axis=0, keepdims=True))
        p = jnp.exp(s - top)
        factor = jnp.exp(before - top)
        m_ref[h : h + 1, :] = top
        l_ref[h : h + 1, :] = l_ref[h : h + 1, :] * factor + jnp.sum(p, axis=0, keepdims=True)
        acc_ref[lo : lo + HD, :] = acc_ref[lo : lo + HD, :] * factor + t_mm(vh, p.astype(BF16))


def keys_values(x_ref, w_ref, v_bias, kv_ref):
    kv_ref[:, :HALF] = mm(x_ref[...], w_ref[:, :HALF]).astype(BF16)
    kv_ref[:, HALF:] = (mm(x_ref[...], w_ref[:, HALF:]) + v_bias).astype(BF16)


def attend_cost(tokens, keys):
    return pl.CostEstimate(
        flops=8 * tokens * keys * HALF + 2 * keys * WIDTH * WIDTH,
        bytes_accessed=4 * keys * WIDTH,
        transcendentals=2 * tokens * keys * NH,
    )


def attend_first(own, got, xo, wq, wkv):
    tokens, keys = own.shape[0], xo.shape[0]
    block = math.gcd(keys, 1024)
    rows = pl.BlockSpec((block, WIDTH), lambda i: (i, 0))

    def body(o_ref, g_ref, x_ref, wq_ref, wkv_ref, q_ref, kv_ref, vec_ref, b_ref, m_ref, l_ref, acc_ref):
        @pl.when(pl.program_id(0) == 0)
        def _():
            core = place()[3]
            vecs = jnp.transpose(wq_ref[:, HALF:].astype(F32))
            vec_ref[...] = vecs[:16]
            b_ref[...] = jnp.where(core == 0, vecs[:8, :HALF], vecs[:8, HALF:])
            for i, ref in enumerate((o_ref, g_ref)):
                part = mm(ref[...], wq_ref[:, :HALF]) + b_ref[0:1, :]
                q_ref[i * tokens : (i + 1) * tokens, :] = part.astype(BF16) * BF16(0.125)
            m_ref[...] = jnp.full(m_ref.shape, -1e30, F32)
            l_ref[...] = jnp.zeros(l_ref.shape, F32)
            acc_ref[...] = jnp.zeros(acc_ref.shape, F32)

        keys_values(x_ref, wkv_ref, b_ref[1:2, :], kv_ref)
        attend_step(q_ref, kv_ref, m_ref, l_ref, acc_ref)

    return pl.pallas_call(
        body,
        grid=(keys // block,),
        in_specs=[
            whole_spec(tokens, WIDTH),
            whole_spec(tokens, WIDTH),
            rows,
            whole_spec(*wq.shape),
            whole_spec(*wkv.shape),
        ],
        out_specs=[
            whole_spec(2 * tokens, HALF),
            rows,
            whole_spec(16, WIDTH),
            whole_spec(8, HALF),
            whole_spec(8, 2 * tokens),
            whole_spec(8, 2 * tokens),
            whole_spec(HALF, 2 * tokens),
        ],
        out_shape=[
            shape((2 * tokens, HALF), BF16),
            shape((keys, WIDTH), BF16),
            shape((16, WIDTH), F32),
            shape((8, HALF), F32),
            shape((8, 2 * tokens), F32),
            shape((8, 2 * tokens), F32),
            shape((HALF, 2 * tokens), F32),
        ],
        compiler_params=pltpu.CompilerParams(vmem_limit_bytes=20 * MIB),
        cost_estimate=attend_cost(tokens, keys),
        name="attend_first",
    )(own, got, xo, wq, wkv)


def attend_last(q, xc, wkv, bias, top, total, weighted):
    tokens, keys = q.shape[0], xc.shape[0]
    block = math.gcd(keys, 1024)
    rows = pl.BlockSpec((block, WIDTH), lambda i: (i, 0))

    def body(q_ref, x_ref, w_ref, b_ref, mi_ref, li_ref, ai_ref, kv_ref, o_ref, ctx_ref, lse_ref, m_s, l_s, acc_s):
        @pl.when(pl.program_id(0) == 0)
        def _():
            m_s[...] = mi_ref[...]
            l_s[...] = li_ref[...]
            acc_s[...] = ai_ref[...]

        keys_values(x_ref, w_ref, b_ref[1:2, :], kv_ref)
        attend_step(q_ref, kv_ref, m_s, l_s, acc_s)

        @pl.when(pl.program_id(0) == pl.num_programs(0) - 1)
        def _():
            lse_ref[...] = m_s[...] + jnp.log(l_s[...])
            for h in range(NH):
                lo = h * HD
                o_ref[lo : lo + HD, :] = acc_s[lo : lo + HD, :] / l_s[h : h + 1, :]
            ctx_ref[...] = jnp.transpose(o_ref[...]).astype(BF16)

    return pl.pallas_call(
        body,
        grid=(keys // block,),
        in_specs=[
            whole_spec(tokens, HALF),
            rows,
            whole_spec(*wkv.shape),
            whole_spec(8, HALF),
            whole_spec(8, tokens),
            whole_spec(8, tokens),
            whole_spec(HALF, tokens),
        ],
        out_specs=[
            rows,
            whole_spec(HALF, tokens),
            whole_spec(tokens, HALF),
            whole_spec(8, tokens),
        ],
        out_shape=[
            shape((keys, WIDTH), BF16),
            shape((HALF, tokens), F32),
            shape((tokens, HALF), BF16),
            shape((8, tokens), F32),
        ],
        scratch_shapes=[
            pltpu.VMEM((8, tokens), F32),
            pltpu.VMEM((8, tokens), F32),
            pltpu.VMEM((HALF, tokens), F32),
        ],
        compiler_params=pltpu.CompilerParams(vmem_limit_bytes=20 * MIB),
        cost_estimate=attend_cost(tokens // 2, keys),
        name="attend_last",
    )(q, xc, wkv, bias, top, total, weighted)


def unit_places(chips, per, rows, core):
    units = chips * per * rows
    unit = lax.broadcasted_iota(jnp.int32, (WIDTH, units), 1)
    at = lax.broadcasted_iota(jnp.int32, (WIDTH, units), 0)
    chip, inside = unit // (per * rows), lax.rem(unit, rows)
    return (at == chip * (2 * rows) + core * rows + inside).astype(BF16)


def unit_bias(vecs, chips, per, rows):
    units = chips * per * rows

    def body(v_ref, out_ref):
        every = mm(v_ref[...].astype(BF16), unit_places(chips, per, rows, place()[3]))
        turn = lax.rem(lax.broadcasted_iota(jnp.int32, (16, units), 1) // rows, per)
        row = lax.broadcasted_iota(jnp.int32, (16, units), 0)
        out_ref[...] = column_sum(jnp.where(row == 9 + turn, every, 0.0))

    return kernel(body, (vecs,), (shape((1, units), F32),), "unit_bias", flops=10**8)[0]


def unit_rows(sums, chips, per, rows):
    units = chips * per * rows

    def body(s_ref, out_ref):
        turn = lax.rem(lax.broadcasted_iota(jnp.int32, (8, units), 1) // rows, per)
        row = lax.broadcasted_iota(jnp.int32, (8, units), 0)
        spread_out = jnp.where(row == turn, s_ref[...], 0.0).astype(BF16)
        out_ref[...] = mm_t(spread_out, unit_places(chips, per, rows, place()[3]))

    return kernel(body, (sums,), (shape((8, WIDTH), F32),), "unit_rows", flops=10**8)[0]


def norm_forward(residual, gain, shift):
    center = residual - jnp.mean(residual, axis=-1, keepdims=True)
    scale = lax.rsqrt(jnp.mean(center * center, axis=-1, keepdims=True) + EPSILON)
    normed = center * scale
    return normed * gain + shift, normed, scale


def norm_backward(grad_out, normed, scale, gain):
    grad_normed = grad_out * gain
    return scale * (
        grad_normed
        - jnp.mean(grad_normed, axis=-1, keepdims=True)
        - normed * jnp.mean(grad_normed * normed, axis=-1, keepdims=True)
    )


def column_sum(value):
    return jnp.sum(value, axis=0, keepdims=True)


def halves(core, own, other):
    left = jnp.where(core == 0, own, other)
    right = jnp.where(core == 0, other, own)
    return left, right


def mix(ctx, ctx_got, mixer_own, mixer_got, vecs, inputs):
    tokens = inputs.shape[0]

    def body(o_ref, g_ref, mo_ref, mg_ref, v_ref, x_ref, low_ref, row_ref, n_ref, s_ref):
        core = place()[3]
        mine = pl.ds(pl.multiple_of(core * HALF, HALF), HALF)
        others = pl.ds(pl.multiple_of((1 - core) * HALF, HALF), HALF)
        parts = [
            mm(o_ref[:tokens, :], ref[mine, :]) + mm(g_ref[tokens:, :], ref[others, :])
            for ref in (mo_ref, mg_ref)
        ]
        attended = jnp.concatenate(halves(core, *parts), axis=1) + v_ref[2:3, :]
        rows, normed, scale = norm_forward(
            x_ref[...].astype(F32) + attended, v_ref[3:4, :], v_ref[4:5, :]
        )
        low_ref[...] = rows.astype(BF16)
        row_ref[...] = rows
        n_ref[...] = normed
        s_ref[...] = scale

    return kernel(
        body,
        (ctx, ctx_got, mixer_own, mixer_got, vecs, inputs),
        (
            shape((tokens, WIDTH), BF16),
            shape((tokens, WIDTH), F32),
            shape((tokens, WIDTH), F32),
            shape((tokens, 1), F32),
        ),
        "mix",
        flops=10**9,
        bytes_accessed=3 * 10**6,
    )


def feed(own, got, w_inner, i_bias, w_outer):
    tokens = own.shape[0]
    units = w_inner.shape[1]

    def body(o_ref, g_ref, w1_ref, b_ref, w2_ref, two_ref, act_ref, slope_ref, mine_ref, send_ref):
        two_ref[:tokens, :] = o_ref[...]
        two_ref[tokens:, :] = g_ref[...]
        u = mm(two_ref[...], w1_ref[...]) + b_ref[...]
        cdf = 0.5 * (1.0 + lax.erf(u * ROOT_HALF))
        slope_ref[...] = cdf + u * jnp.exp(-0.5 * u * u) * GAUSS_FACTOR
        act_ref[...] = (u * cdf).astype(BF16)
        part = mm(act_ref[...], w2_ref[...])
        mine_ref[...] = part[:tokens]
        send_ref[...] = part[tokens:]

    return kernel(
        body,
        (own, got, w_inner, i_bias, w_outer),
        (
            shape((2 * tokens, WIDTH), BF16),
            shape((2 * tokens, units), BF16),
            shape((2 * tokens, units), F32),
            shape((tokens, WIDTH), F32),
            shape((tokens, WIDTH), F32),
        ),
        "feed",
        flops=3 * 10**9,
        bytes_accessed=8 * 10**6,
    )


def crown(mine, got, first_rows, vecs, out_cot, term_cot):
    tokens = mine.shape[0]

    def body(
        m_ref, g_ref, f_ref, v_ref, oc_ref, tc_ref, out_ref, term_ref, gs_ref, go_ref, sum_ref
    ):
        gain = v_ref[6:7, :]
        head = v_ref[8:9, :]
        outer = m_ref[...] + g_ref[...] + v_ref[5:6, :]
        rows, normed, scale = norm_forward(f_ref[...] + outer, gain, v_ref[7:8, :])
        out_ref[...] = rows.astype(BF16)
        logits = jnp.sum(rows * head, axis=-1, keepdims=True)
        small = jnp.exp(-jnp.abs(logits))
        term = jnp.maximum(logits, 0.0) + jnp.log1p(small)
        term_ref[...] = jnp.transpose(jnp.broadcast_to(term, (tokens, 128)))[0:1, :]
        sig = jnp.where(logits >= 0.0, 1.0, small) / (1.0 + small)
        cot = jnp.transpose(jnp.broadcast_to(tc_ref[...], (128, tokens)))[:, 0:1]
        slope = cot * sig
        grad_final = oc_ref[...].astype(F32) + slope * head
        grad = norm_backward(grad_final, normed, scale, gain)
        low = grad.astype(BF16)
        gs_ref[...] = grad
        go_ref[...] = low
        sum_ref[...] = jnp.concatenate(
            [
                column_sum(low.astype(F32)),
                column_sum(grad_final * normed),
                column_sum(grad_final),
                column_sum(slope * rows),
                jnp.zeros((4, WIDTH), F32),
            ],
            axis=0,
        )

    return kernel(
        body,
        (mine, got, first_rows, vecs, out_cot, term_cot),
        (
            shape((tokens, WIDTH), BF16),
            shape((1, tokens), F32),
            shape((tokens, WIDTH), F32),
            shape((tokens, WIDTH), BF16),
            shape((8, WIDTH), F32),
        ),
        "crown",
        flops=10**8,
        bytes_accessed=3 * 10**6,
    )


def feed_back(own, got, slope, w_inner, w_outer):
    tokens = own.shape[0]
    units = w_inner.shape[1]

    def body(o_ref, g_ref, s_ref, w1_ref, w2_ref, two_ref, gi_ref, mine_ref, send_ref, sum_ref):
        two_ref[:tokens, :] = o_ref[...]
        two_ref[tokens:, :] = g_ref[...]
        low = (mm_t(two_ref[...], w2_ref[...]) * s_ref[...]).astype(BF16)
        gi_ref[...] = low
        sum_ref[...] = column_sum(low.astype(F32))
        part = mm_t(gi_ref[...], w1_ref[...])
        mine_ref[...] = part[:tokens]
        send_ref[...] = part[tokens:]

    return kernel(
        body,
        (own, got, slope, w_inner, w_outer),
        (
            shape((2 * tokens, WIDTH), BF16),
            shape((2 * tokens, units), BF16),
            shape((tokens, WIDTH), F32),
            shape((tokens, WIDTH), F32),
            shape((1, units), F32),
        ),
        "feed_back",
        flops=3 * 10**9,
        bytes_accessed=8 * 10**6,
    )


def mix_back(mine, got, grad_second, normed, scale, vecs, mixer_own, mixer_got):
    tokens = mine.shape[0]

    def body(
        m_ref, g_ref, gs_ref, n_ref, s_ref, v_ref, mo_ref, mg_ref, res_ref, keep_ref, send_ref, sum_ref
    ):
        core = place()[3]
        first = gs_ref[...] + m_ref[...] + g_ref[...]
        normal = n_ref[...]
        grad = norm_backward(first, normal, s_ref[...], v_ref[3:4, :])
        res_ref[...] = grad
        low = grad.astype(BF16)
        sum_ref[...] = jnp.concatenate(
            [
                column_sum(low.astype(F32)),
                column_sum(first * normal),
                column_sum(first),
                jnp.zeros((5, WIDTH), F32),
            ],
            axis=0,
        )
        mine_low, other_low = halves(core, low[:, :HALF], low[:, HALF:])
        ctx = (mm_t(mine_low, mo_ref[...]) + mm_t(other_low, mg_ref[...])).astype(BF16)
        mine_ctx, other_ctx = halves(core, ctx[:, :HALF], ctx[:, HALF:])
        keep_ref[:, :HALF] = mine_ctx
        keep_ref[:, HALF:] = mine_low
        send_ref[:, :HALF] = other_ctx
        send_ref[:, HALF:] = other_low

    return kernel(
        body,
        (mine, got, grad_second, normed, scale, vecs, mixer_own, mixer_got),
        (
            shape((tokens, WIDTH), F32),
            shape((tokens, WIDTH), BF16),
            shape((tokens, WIDTH), BF16),
            shape((8, WIDTH), F32),
        ),
        "mix_back",
        flops=10**9,
        bytes_accessed=4 * 10**6,
    )


def attend_back_step(q_ref, g_ref, lse_ref, delta_ref, kv_ref, out_ref, acc_ref, sum_ref):
    held = []
    for h in range(NH):
        lo = h * HD
        qh = q_ref[:, lo : lo + HD]
        gh = g_ref[:, lo : lo + HD]
        kh = kv_ref[:, lo : lo + HD]
        vh = kv_ref[:, HALF + lo : HALF + lo + HD]
        p = jnp.exp(mm_t(kh, qh) - lse_ref[h : h + 1, :])
        dp = mm_t(vh, gh)
        ds = (p * (dp - delta_ref[h : h + 1, :])).astype(BF16)
        acc_ref[lo : lo + HD, :] += t_mm(kh, ds)
        held.append((mm(ds, qh).astype(BF16), mm(p.astype(BF16), gh).astype(BF16)))
        if h % 2 == 1:
            (dk0, dv0), (dk1, dv1) = held
            held = []
            at = lo - HD
            dv = jnp.concatenate([dv0, dv1], axis=1)
            out_ref[:, at : at + 2 * HD] = jnp.concatenate([dk0, dk1], axis=1)
            out_ref[:, HALF + at : HALF + at + 2 * HD] = dv
            sum_ref[1:2, at : at + 2 * HD] += column_sum(dv.astype(F32))


def attend_back_cost(tokens, keys):
    return pl.CostEstimate(
        flops=10 * tokens * keys * HALF,
        bytes_accessed=4 * keys * WIDTH,
        transcendentals=tokens * keys * NH,
    )


def attend_back_first(q, low, low_got, o, lse, kv):
    tokens, keys = q.shape[0], kv.shape[0]
    block = math.gcd(keys, 1024)
    rows = pl.BlockSpec((block, WIDTH), lambda i: (i, 0))

    def body(q_ref, go_ref, gc_ref, o_ref, lse_ref, kv_ref, d_ref, g_ref, delta_ref, acc_ref, sum_ref):
        @pl.when(pl.program_id(0) == 0)
        def _():
            acc_ref[...] = jnp.zeros(acc_ref.shape, F32)
            sum_ref[...] = jnp.zeros(sum_ref.shape, F32)
            g_ref[: tokens // 2, :] = go_ref[:, :HALF]
            g_ref[tokens // 2 :, :] = gc_ref[:, :HALF]
            prod = jnp.transpose(g_ref[...].astype(F32)) * o_ref[...]
            for h in range(NH):
                delta_ref[h : h + 1, :] = column_sum(prod[h * HD : (h + 1) * HD, :])

        attend_back_step(q_ref, g_ref, lse_ref, delta_ref, kv_ref, d_ref, acc_ref, sum_ref)

    return pl.pallas_call(
        body,
        grid=(keys // block,),
        in_specs=[
            whole_spec(tokens, HALF),
            whole_spec(tokens // 2, WIDTH),
            whole_spec(tokens // 2, WIDTH),
            whole_spec(HALF, tokens),
            whole_spec(8, tokens),
            rows,
        ],
        out_specs=[
            rows,
            whole_spec(tokens, HALF),
            whole_spec(8, tokens),
            whole_spec(HALF, tokens),
            whole_spec(8, HALF),
        ],
        out_shape=[
            shape((keys, WIDTH), BF16),
            shape((tokens, HALF), BF16),
            shape((8, tokens), F32),
            shape((HALF, tokens), F32),
            shape((8, HALF), F32),
        ],
        compiler_params=pltpu.CompilerParams(vmem_limit_bytes=20 * MIB),
        cost_estimate=attend_back_cost(tokens, keys),
        name="attend_back_first",
    )(q, low, low_got, o, lse, kv)


def attend_back_last(q, g, lse, delta, acc, sums, kv, wq):
    tokens, keys = q.shape[0], kv.shape[0]
    block = math.gcd(keys, 1024)
    rows = pl.BlockSpec((block, WIDTH), lambda i: (i, 0))

    def body(q_ref, g_ref, lse_ref, delta_ref, ai_ref, si_ref, kv_ref, w_ref, d_ref, dq_ref, sum_ref, send_ref, acc_s):
        @pl.when(pl.program_id(0) == 0)
        def _():
            acc_s[...] = ai_ref[...]
            sum_ref[...] = si_ref[...]

        attend_back_step(q_ref, g_ref, lse_ref, delta_ref, kv_ref, d_ref, acc_s, sum_ref)

        @pl.when(pl.program_id(0) == pl.num_programs(0) - 1)
        def _():
            dq = jnp.transpose(acc_s[...] * 0.125).astype(BF16)
            dq_ref[...] = dq
            sum_ref[0:1, :] = column_sum(dq.astype(F32))
            send_ref[...] = mm_t(dq[tokens // 2 :], w_ref[:, :HALF]).astype(BF16)

    return pl.pallas_call(
        body,
        grid=(keys // block,),
        in_specs=[
            whole_spec(tokens, HALF),
            whole_spec(tokens, HALF),
            whole_spec(8, tokens),
            whole_spec(8, tokens),
            whole_spec(HALF, tokens),
            whole_spec(8, HALF),
            rows,
            whole_spec(*wq.shape),
        ],
        out_specs=[
            rows,
            whole_spec(tokens, HALF),
            whole_spec(8, HALF),
            whole_spec(tokens // 2, WIDTH),
        ],
        out_shape=[
            shape((keys, WIDTH), BF16),
            shape((tokens, HALF), BF16),
            shape((8, HALF), F32),
            shape((tokens // 2, WIDTH), BF16),
        ],
        scratch_shapes=[pltpu.VMEM((HALF, tokens), F32)],
        compiler_params=pltpu.CompilerParams(vmem_limit_bytes=20 * MIB),
        cost_estimate=attend_back_cost(tokens, keys),
        name="attend_back_last",
    )(q, g, lse, delta, acc, sums, kv, wq)


def input_part_other(dkv, wkv):
    keys = dkv.shape[0]
    block = math.gcd(keys, 1024)
    rows = pl.BlockSpec((block, WIDTH), lambda i: (i, 0))

    def body(d_ref, w_ref, out_ref):
        out_ref[...] = mm_t(d_ref[...], w_ref[...]).astype(BF16)

    return pl.pallas_call(
        body,
        grid=(keys // block,),
        in_specs=[rows, whole_spec(*wkv.shape)],
        out_specs=rows,
        out_shape=shape((keys, WIDTH), BF16),
        compiler_params=pltpu.CompilerParams(vmem_limit_bytes=12 * MIB),
        cost_estimate=pl.CostEstimate(
            flops=2 * keys * WIDTH * WIDTH, bytes_accessed=4 * keys * WIDTH, transcendentals=0
        ),
        name="input_part_other",
    )(dkv, wkv)


def input_part_own(dkv, wkv, got, dq, wq, q_got):
    keys = dkv.shape[0]
    tokens = q_got.shape[0]
    block = math.gcd(keys // 2, 512)
    half = keys // 2 // block
    rows = pl.BlockSpec((block, WIDTH), lambda i: (i, 0))

    def body(d_ref, w_ref, g_ref, dq_ref, wq_ref, qg_ref, keep_ref, send_ref, part_s):
        step = pl.program_id(0)
        part_s[...] = mm_t(d_ref[...], w_ref[...]) + g_ref[...].astype(F32)

        @pl.when(step == 0)
        def _():
            part_s[:tokens, :] += mm_t(dq_ref[:tokens, :], wq_ref[:, :HALF]) + qg_ref[...].astype(
                F32
            )

        @pl.when(step < half)
        def _():
            keep_ref[...] = part_s[...].astype(BF16)

        @pl.when(step >= half)
        def _():
            send_ref[...] = part_s[...].astype(BF16)

    return pl.pallas_call(
        body,
        grid=(2 * half,),
        in_specs=[
            rows,
            whole_spec(*wkv.shape),
            rows,
            whole_spec(*dq.shape),
            whole_spec(*wq.shape),
            whole_spec(*q_got.shape),
        ],
        out_specs=[
            pl.BlockSpec((block, WIDTH), lambda i: (jnp.minimum(i, half - 1), 0)),
            pl.BlockSpec((block, WIDTH), lambda i: (jnp.maximum(i - half, 0), 0)),
        ],
        out_shape=[shape((keys // 2, WIDTH), BF16)] * 2,
        scratch_shapes=[pltpu.VMEM((block, WIDTH), F32)],
        compiler_params=pltpu.CompilerParams(vmem_limit_bytes=12 * MIB),
        cost_estimate=pl.CostEstimate(
            flops=2 * keys * WIDTH * WIDTH, bytes_accessed=4 * keys * WIDTH, transcendentals=0
        ),
        name="input_part_own",
    )(dkv, wkv, got, dq, wq, q_got)


def spread(zs, rows, cols, args, fill, name, scratch):
    count = len(args)

    def body(*refs):
        ins, outs, part_s = refs[:count], refs[count : count + 4], refs[-1]
        fill(ins, part_s)
        here = place()
        for k in range(zs):
            for i, out in enumerate(outs):
                chip = chip_of(here, i // 2, i % 2, k, zs)
                out[k] = part_s[rows_at(chip, rows), :]

    return kernel(
        body,
        args,
        [shape((zs, rows, cols), BF16)] * 4,
        name,
        scratch=[pltpu.VMEM(scratch, BF16)],
        flops=2 * 10**9,
        bytes_accessed=6 * 10**6,
    )


def spread_product(left, right, zs):
    total, cols = left.shape[1], right.shape[1]
    rows = total // (4 * zs)
    if rows % 16:
        full = t_mm(left, right).astype(BF16).reshape(2, zs, 2, rows, cols)
        full = to_distance(full).reshape(4, zs, rows, cols)
        return full[0], full[1], full[2], full[3]

    def fill(ins, part_s):
        part_s[...] = t_mm(ins[0][...], ins[1][...]).astype(BF16)

    return spread(zs, rows, cols, (left, right), fill, "spread", (total, cols))


def spread_qkv(zs, x_own, x_got, dq, qv, mid, top, unit, g_kv, ctx, ctx_got, low, low_got):
    tokens = x_own.shape[0]
    rows = WIDTH // (4 * zs)
    cols = WIDE + WIDTH + HALF

    def fill(ins, part_s):
        xo, xg, dq_r, qv_r, mid_r, top_r, unit_r, kv_r, c_r, cg_r, l_r, lg_r = ins
        core = place()[3]
        part_s[:, :HALF] = (
            t_mm(xo[...], dq_r[:tokens, :]) + t_mm(xg[...], dq_r[tokens:, :])
        ).astype(BF16)
        zero = jnp.zeros((2, HALF), F32)
        sums = jnp.concatenate(
            [
                jnp.concatenate(halves(core, qv_r[0:2, :], zero), axis=1),
                mid_r[0:3, :],
                top_r[0:4, :],
                unit_r[...],
                jnp.zeros((AUX - 17, WIDTH), F32),
            ],
            axis=0,
        )
        part_s[:, HALF:WIDE] = jnp.transpose(sums).astype(BF16)
        part_s[:, WIDE : WIDE + WIDTH] = kv_r[...]
        lows = (l_r[:, HALF:], lg_r[:, HALF:])
        part_s[pl.ds(pl.multiple_of(core * HALF, HALF), HALF), WIDE + WIDTH :] = (
            t_mm(c_r[:tokens, :], lows[0]) + t_mm(c_r[tokens:, :], lows[1])
        ).astype(BF16)
        part_s[pl.ds(pl.multiple_of((1 - core) * HALF, HALF), HALF), WIDE + WIDTH :] = (
            t_mm(cg_r[tokens:, :], lows[0]) + t_mm(cg_r[:tokens, :], lows[1])
        ).astype(BF16)

    args = (x_own, x_got, dq, qv, mid, top, unit, g_kv, ctx, ctx_got, low, low_got)
    if rows % 16 == 0:
        return spread(zs, rows, cols, args, fill, "spread_qkv", (WIDTH, cols))

    def body(*refs):
        fill(refs[:12], refs[12])

    full = kernel(body, args, [shape((WIDTH, cols), BF16)], "fill_qkv")[0]
    full = to_distance(full.reshape(2, zs, 2, rows, cols)).reshape(4, zs, rows, cols)
    return full[0], full[1], full[2], full[3]


def shards(
    layer_input,
    query_weight,
    query_bias,
    key_weight,
    value_weight,
    value_bias,
    mixer_weight,
    mixer_bias,
    first_gain,
    first_shift,
    inner_weight,
    inner_bias,
    outer_weight,
    outer_bias,
    second_gain,
    second_shift,
    head_weight,
    out_cotangent,
    term_cotangent,
):
    core = place()[3]
    chips = lax.axis_size("ctx")
    zs = chips // 4
    inputs = layer_input[0]
    tokens = inputs.shape[0]
    rows = query_weight.shape[0]
    hidden = outer_weight.shape[0]
    ff = inner_weight.shape[1]
    units = ff // 2
    per = hidden // rows

    def in_order(own, other, axis):
        return jnp.stack(halves(core, own, other), axis=axis)

    aux = jnp.concatenate(
        [
            query_bias,
            value_bias,
            mixer_bias,
            first_gain,
            first_shift,
            outer_bias,
            second_gain,
            second_shift,
            head_weight,
            inner_bias,
        ]
    ).reshape(9 + per, rows)
    aux = jnp.transpose(jnp.pad(aux, ((0, AUX - 9 - per), (0, 0))))
    four = (query_weight, key_weight, value_weight, mixer_weight)

    def side_of(side):
        q, k, v, m = (lax.dynamic_slice_in_dim(w, side * HALF, HALF, 1) for w in four)
        return jnp.concatenate([q, aux, k, v, m], axis=1)

    x_along = along_z(inputs)
    x_got = swap_core(inputs)
    qkv_block = in_order(side_of(core), swap_core(side_of(1 - core)), 0)
    qkv = along_z(qkv_block.reshape(2 * rows, WIDE + WIDTH + HALF))
    xo = jnp.concatenate([x_along, swap_y(x_along)]).reshape(2 * zs * tokens, WIDTH)
    xc = swap_core(xo)
    qkv_y, qkv_x = swap_y(qkv), swap_x(qkv)
    wq, wkv, mixer_own = build_qkv(
        qkv, qkv_y, qkv_x, swap_x(qkv_y[: zs // 2]), swap_y(qkv_x[zs // 2 :])
    )
    mixer_got = swap_core(mixer_own)

    inner_split = inner_weight.reshape(rows, chips, 2, hidden)

    def inner_of(side):
        return pick(inner_split, side, 2).reshape(rows, units)

    both = in_order(inner_of(core), swap_core(inner_of(1 - core)), 0).reshape(2 * rows, units)
    quarters = units // HALF
    first = quarters * 2 * rows
    rest = jnp.concatenate(
        [both[:, j * HALF : (j + 1) * HALF] for j in range(quarters)]
        + [outer_weight[:, :HALF], outer_weight[:, HALF:]]
    )
    rest = along_z(after(rest, qkv))

    q_scaled, kvo, vecs, bias, top, total, weighted = attend_first(inputs, x_got, xo, wq, wkv)
    rest = after(rest, q_scaled)
    rest_y, rest_x = swap_y(rest), swap_x(rest)
    kvc, o_exact, ctx, lse = attend_last(q_scaled, xc, wkv, bias, top, total, weighted)
    w_inner, w_outer = build_rest(
        rest,
        rest_y,
        rest_x,
        swap_x(rest_y[:, :first]),
        swap_y(rest_x[:, first:]),
        2 * rows,
        hidden,
    )
    ctx_got = swap_core(ctx)
    i_bias = unit_bias(vecs, chips, per, rows)
    first_low, first_rows, first_normed, first_scale = mix(
        ctx, ctx_got, mixer_own, mixer_got, vecs, inputs
    )

    first2, active, slope, mine, away = feed(
        first_low, swap_core(first_low), w_inner, i_bias, w_outer
    )
    final_low, term, grad_second, grad_outer, top_sums = crown(
        mine, swap_core(away), first_rows, vecs, out_cotangent[0], term_cotangent
    )
    grad_outer2, grad_inner, mine, away, inner_sums = feed_back(
        grad_outer, swap_core(grad_outer), slope, w_inner, w_outer
    )
    got = swap_core(away)
    keep2, y2, x2, far2 = spread_product(active, grad_outer2, zs)
    far2 = swap_y(far2)
    keep1, y1, x1, far1 = spread_product(first2, grad_inner, zs)
    far1 = swap_x(far1)

    grad_residual, low, low_send, mid_sums = mix_back(
        mine, got, grad_second, first_normed, first_scale, vecs, mixer_own, mixer_got
    )
    low_got = swap_core(low_send)
    y2 = swap_y(after(y2, low_got))
    x1 = swap_x(after(x1, low_got))
    dkvc, g_both, delta, acc, qv_sums = attend_back_first(
        q_scaled, low, low_got, o_exact, lse, kvc
    )
    away = swap_core(input_part_other(dkvc, wkv))
    x2, y1 = after(x2 + far2, dkvc), after(y1 + far1, dkvc)
    x2 = swap_x(x2)
    y1 = swap_y(y1)
    dkvo, dq, qv_sums, q_away = attend_back_last(
        q_scaled, g_both, lse, delta, acc, qv_sums, kvo, wq
    )

    part, part_y = input_part_own(dkvo, wkv, away, dq, wq, swap_core(q_away))
    part = (part + swap_y(part_y)).reshape(zs, tokens, WIDTH)
    total = sum_z(jnp.concatenate([part[:1], jnp.flip(part[1:], 0)]))
    input_grad = (grad_residual + total).astype(BF16)

    g_kv = (t_mm(xo, dkvo) + t_mm(xc, dkvc)).astype(BF16)
    keep, yq, xq, far = spread_qkv(
        zs,
        inputs,
        x_got,
        dq,
        qv_sums,
        mid_sums,
        top_sums,
        unit_rows(inner_sums, chips, per, rows),
        g_kv,
        ctx,
        ctx_got,
        low,
        low_got,
    )
    cut = zs // 2
    far_a, far_b = swap_x(far[:cut]), swap_y(far[cut:])
    yq = swap_y(jnp.concatenate([yq[:cut] + far_a, yq[cut:]]))
    xq = swap_x(jnp.concatenate([xq[:cut], xq[cut:] + far_b]))
    g_outer = sum_z(keep2 + y2 + x2)
    g_inner = sum_z(keep1 + y1 + x1)
    g_qkv = sum_z(keep + yq + xq)

    g_all = jnp.concatenate([g_qkv, g_inner], axis=1).reshape(2, rows, -1)
    own, got = pick(g_all, core, 0), swap_core(pick(g_all, 1 - core, 0))

    def columns(lo):
        return jnp.concatenate(
            halves(core, own[:, lo : lo + HALF], got[:, lo : lo + HALF]), axis=1
        )

    at1 = WIDE + WIDTH + HALF
    g_inner = in_order(
        own[:, at1:].reshape(rows, chips, hidden), got[:, at1:].reshape(rows, chips, hidden), 2
    ).reshape(rows, ff)
    sm = jnp.transpose(own[:, HALF:WIDE] + got[:, HALF:WIDE])
    return (
        final_low[None],
        term,
        input_grad[None],
        columns(0),
        sm[0],
        columns(WIDE),
        columns(WIDE + HALF),
        sm[1],
        columns(WIDE + WIDTH),
        sm[2],
        sm[3],
        sm[4],
        g_inner,
        sm[9 : 9 + per].reshape(hidden),
        g_outer.reshape(hidden, WIDTH),
        sm[5],
        sm[6],
        sm[7],
        sm[8],
    )


def pick(value, index, axis):
    return lax.dynamic_index_in_dim(value, index, axis, keepdims=False)


def solution(mesh):
    both = ("seq", "ctx")
    tok, mat, vec = P("seq", "ctx", None), P(both, None), P(both)
    term = P("seq", "ctx")
    in_specs = (
        tok, mat, vec, mat, mat, vec, mat, vec, vec, vec,
        mat, vec, mat, vec, vec, vec, vec, tok, term,
    )
    out_specs = (
        tok, term, tok, mat, vec, mat, mat, vec, mat, vec,
        vec, vec, mat, vec, mat, vec, vec, vec, vec,
    )
    return jax.shard_map(
        shards, mesh=mesh, in_specs=in_specs, out_specs=out_specs, check_vma=False
    )
```

time: 413 us -> 289 us (0.70)
  waiting for transfers between devices: 190 us -> 154 us
  local copies, waits for them, and re-layouts: 56.1 us -> 22.6 us
  other arithmetic: 32.8 us -> 6.99 us
  starting transfers between devices: 81.3 us -> 55.8 us
  matrix products: 17.3 us -> 2.9 us
  Pallas kernels: 27.9 us -> 40.7 us
    ppermute x30 -> x21, waiting for transfers between devices: 88.4 us -> 52 us  [shift_z(): return lax.ppermute(value, 'ctx', [(i, (i + 4 * k) % n) for i in range(n)])]
    ppermute x30 -> x21, starting transfers between devices: 61 us -> 31.6 us  [shift_z(): return lax.ppermute(value, 'ctx', [(i, (i + 4 * k) % n) for i in range(n)])]
    another operation x26 -> x0, local copies, waits for them, and re-layouts: 19.3 us -> none  [the longest x7 9.38 us: shards(): jnp.stack([lax.dynamic_update_slice(zero, sums[None, :HALF], (core, 0)).r...]
    dot_general x8 -> x0, matrix products: 12.8 us -> none  [the longest x4 8.09 us: mm_t(): lax.dot_general(a, b, (((1,), (1,)), ((), ())), preferred_element_type=F32)]
    pallas_call x2 -> x18, Pallas kernels: 27.9 us -> 40.7 us  [the longest x12 11 us: kernel(): pl.pallas_call(body, in_specs=[pl.BlockSpec(memory_space=pltpu.VMEM) for...]
    another operation x34 -> x8, other arithmetic: 11.5 us -> 0.9 us  [the longest x5 0.52 us: in_order(): return jnp.stack(halves(core, own, other), axis=axis)]
    ppermute x8 -> x9, waiting for transfers between devices: 51.9 us -> 61.8 us  [swap_x(): return lax.ppermute(value, 'seq', [(0, 1), (1, 0)])]
    ppermute x23 -> x25, waiting for transfers between devices: 49.3 us -> 40.4 us  [swap_ctx(): return lax.ppermute(value, 'ctx', [(i, i ^ bit) for i in range(n)])]
  transfers between devices with their start and end apart: 61 -> 55, of which waited for: 23 -> 28; matrix products, arithmetic and copies ran while one was open for 18% -> 9% of each run, Pallas kernels for 7% -> 11%
where the time goes in v3:
time: 289 us; the launch traced here: 285 us
  waiting for transfers between devices  154 us (53%)
  starting transfers between devices  55.8 us (19%)
  Pallas kernels  40.7 us (14%)
  local copies, waits for them, and re-layouts  22.6 us (8%)
  other arithmetic  6.99 us (2%)
  matrix products  2.9 us (1%)
    ppermute x9, waiting for transfers between devices, swap_x(): return lax.ppermute(value, 'seq', [(0, 1), (1, 0)])  61.8 us
    ppermute x21, waiting for transfers between devices, shift_z(): return lax.ppermute(value, 'ctx', [(i, (i + 4 * k) % n) for i in range(n)])  52 us
    ppermute x25, waiting for transfers between devices, swap_ctx(): return lax.ppermute(value, 'ctx', [(i, i ^ bit) for i in range(n)])  40.4 us
    ppermute x21, starting transfers between devices, shift_z(): return lax.ppermute(value, 'ctx', [(i, (i + 4 * k) % n) for i in range(n)])  31.6 us
    ppermute x25, starting transfers between devices, swap_ctx(): return lax.ppermute(value, 'ctx', [(i, i ^ bit) for i in range(n)])  14.6 us
    pallas_call x12, Pallas kernels, kernel(): pl.pallas_call(body, in_specs=[pl.BlockSpec(memory_space=pltpu.VMEM) for...  11 us
    ppermute x9, starting transfers between devices, swap_x(): return lax.ppermute(value, 'seq', [(0, 1), (1, 0)])  9.6 us
    unnamed x41, local copies, waits for them, and re-layouts  7.39 us
  transfers between devices with their start and end apart: 55, of which 28 were waited for; matrix products, arithmetic and copies ran while one was open for 9% of the time, Pallas kernels for 11%

profile of v3, /device:TPU:0, one launch (start us, length us, event | category | flops | bytes accessed | tf_op | source)
XLA Modules:
  0.0 284.7 jit_solution(5324841815376056809)
XLA Ops:
  0.7 5.1 %collective-permute-start.3 = (bf16[128,768]{1,0:T(8,128)(2,1)}, bf16[128,768]{1,0:T(8,128)(2,1)S(1)}, u32[]{:S(2)}, u32[]{:S(2)}) collective-permute-start(bf16[128,768]{1,0:T(8,128)(2,1)} %bitcast.78), channel_id=1, source_target_pairs={{0,12},{1,13},{2,14},{3,15},{4,0},{5,1},{6,2},{7,3},{8,4},{9,5},{1... | collective-permute-start | bytes 589832 | tf_op jit(solution)/shard_map/ppermute | solution.py:60
  6.8 6.8 %concatenate.38 = bf16[312]{0:T(512)(128)(2,1)S(1)} concatenate(bf16[24]{0:T(256)(128)(2,1)} %param.21, bf16[24]{0:T(256)(128)(2,1)} %param.24, bf16[24]{0:T(256)(128)(2,1)} %param.26, bf16[24]{0:T(256)(128)(2,1)} %param.27, bf16[24]{0:T(256)(128)(2,1)} %param.28, bf16[24]{0:T(256)(128)(2,1)} %param.32, bf16[24]{0:T(256)(128)(2,1)} %param.33, bf16[24]{0:T(256)(128)(2,1)} %param.34, ...), dimensions={0} | concatenate | bytes 1248 | tf_op jit(solution)/shard_map/concatenate | solution.py:938
  21.1 2.9 %collective-permute-start.8 = (bf16[48,1664]{1,0:T(8,128)(2,1)S(1)}, bf16[48,1664]{1,0:T(8,128)(2,1)S(1)}, u32[]{:S(2)}, u32[]{:S(2)}) collective-permute-start(bf16[48,1664]{1,0:T(8,128)(2,1)S(1)} %bitcast.95), channel_id=1, source_target_pairs={{0,12},{1,13},{2,14},{3,15},{4,0},{5,1},{6,2},{7,3},{8,4},{9,5},{1... | collective-permute-start | bytes 479240 | tf_op jit(solution)/shard_map/ppermute | solution.py:60
  28.5 11.2 %collective-permute-done.7 = bf16[48,1664]{1,0:T(8,128)(2,1)S(1)} collective-permute-done((bf16[48,1664]{1,0:T(8,128)(2,1)S(1)}, bf16[48,1664]{1,0:T(8,128)(2,1)S(1)}, u32[]{:S(2)}, u32[]{:S(2)}) %collective-permute-start.7) | collective-permute-done | bytes 159776 | tf_op jit(solution)/shard_map/ppermute | solution.py:60
  44.4 11.3 %collective-permute-done.10.x_ref = bf16[4,48,1664]{2,1,0:T(8,128)(2,1)S(1)} collective-permute-done((bf16[4,48,1664]{2,1,0:T(8,128)(2,1)S(1)}, bf16[4,48,1664]{2,1,0:T(8,128)(2,1)S(1)}, u32[]{:S(2)}, u32[]{:S(2)}) %collective-permute-start.10) | collective-permute-done | bytes 639008 | tf_op jit(solution)/shard_map/ppermute | solution.py:55
  55.9 2.3 collective-permute-done.9.y_ref
  61.5 7.8 %collective-permute-done.19 = bf16[384,384]{1,0:T(8,128)(2,1)S(1)} collective-permute-done((bf16[384,384]{1,0:T(8,128)(2,1)S(1)}, bf16[384,384]{1,0:T(8,128)(2,1)S(1)}, u32[]{:S(2)}, u32[]{:S(2)}) %collective-permute-start.19) | collective-permute-done | bytes 294944 | tf_op jit(solution)/shard_map/ppermute | solution.py:60
  70.7 6.4 %attend_first.1 = (bf16[256,384]{1,0:T(8,128)(2,1)S(1)}, bf16[1024,768]{1,0:T(8,128)(2,1)S(1)}, f32[16,768]{1,0:T(8,128)S(1)}, f32[8,384]{1,0:T(8,128)S(1)}, f32...) custom-call(bf16[128,768]{1,0:T(8,128)(2,1)S(1)} %bitcast.82, ...), custom_call_target="tpu_custom_call" | custom-call | flops 1610612736 | bytes 3145728 | tf_op jit(solution)/shard_map/attend_first/pallas_call | solution.py:278
  78.3 27.0 %collective-permute-done.22.x_ref = bf16[4,384,384]{2,1,0:T(8,128)(2,1)S(1)} collective-permute-done((bf16[4,384,384]{2,1,0:T(8,128)(2,1)S(1)}, bf16[4,384,384]{2,1,0:T(8,128)(2,1)S(1)}, u32[]{:S(2)}, u32[]{:S(2)}) %collective-permute-start.22) | collective-permute-done | bytes 1179680 | tf_op jit(solution)/shard_map/ppermute | solution.py:55
  107.1 6.2 %attend_last.1 = (bf16[1024,768]{1,0:T(8,128)(2,1)S(1)}, f32[384,256]{1,0:T(8,128)S(1)}, bf16[256,384]{1,0:T(8,128)(2,1)S(1)}, f32[8,256]{1,0:T(8,128)S(1)}) custom-call(bf16[256,384]{1,0:T(8,128)(2,1)S(1)} %get-tuple-element.89.q_ref, bf16[1024,768]{1,0:T(8,128)(2,1)S(1)} %collective-permute-done.13.x_ref, ...), custom_call_target="tpu_custom_call" | custom-call | flops 1610612736 | bytes 3145728 | tf_op jit(solution)/shard_map/attend_last/pallas_call | solution.py:335
  116.3 3.6 %collective-permute-done.24.fb_ref = bf16[4,192,384]{2,1,0:T(8,128)(2,1)S(1)} collective-permute-done((bf16[4,192,384]{2,1,0:T(8,128)(2,1)S(1)}, bf16[4,192,384]{2,1,0:T(8,128)(2,1)S(1)}, u32[]{:S(2)}, u32[]{:S(2)}) %collective-permute-start.24) | collective-permute-done | bytes 589856 | tf_op jit(solution)/shard_map/ppermute | solution.py:43
  120.8 1.8 feed.1
  122.7 1.7 collective-permute-done.25.g_ref
  134.6 4.7 %attend_back_first.1 = (bf16[1024,768]{1,0:T(8,128)(2,1)S(1)}, bf16[256,384]{1,0:T(8,128)(2,1)S(1)}, f32[8,256]{1,0:T(8,128)S(1)}, f32[384,256]{1,0:T(8,128)S(1)}, f32[8,384]{1,0:T(8,128)S(1)}) custom-call(bf16[256,384]{1,0:T(8,128)(2,1)S(1)} %get-tuple-element.89.q_ref, bf16[128,768]{1,0:T(8,128)(2,1)S(1)} %get-tuple-element.115.go_ref.refs_10_, ...), custom_call_target="tpu_custom_call" | custom-call | flops 1006632960 | bytes 3145728 | tf_op jit(solution)/shard_map/attend_back_first/pallas_call | solution.py:667
  139.3 5.9 %attend_back_last.1 = (bf16[1024,768]{1,0:T(8,128)(2,1)S(1)}, bf16[256,384]{1,0:T(8,128)(2,1)S(1)}, f32[8,384]{1,0:T(8,128)S(1)}, bf16[128,768]{1,0:T(8,128)(2,1)}) custom-call(bf16[256,384]{1,0:T(8,128)(2,1)S(1)} %get-tuple-element.89.q_ref, bf16[256,384]{1,0:T(8,128)(2,1)S(1)} %get-tuple-element.120.g_ref, f32[8,256]{1,0:T(8,128)S(1)} %get-tuple-element.118.lse_ref, ...), custom_call_target="tpu_custom_call" | custom-call | flops 1006632960 | bytes 3145728 | tf_op jit(solution)/shard_map/attend_back_last/pallas_call | solution.py:718
  153.6 2.6 input_part_other.1
  156.3 3.3 %collective-permute-done.35 = bf16[2,48,1664]{2,1,0:T(8,128)(2,1)S(1)} collective-permute-done((bf16[2,48,1664]{2,1,0:T(8,128)(2,1)S(1)}, bf16[2,48,1664]{2,1,0:T(8,128)(2,1)S(1)}, u32[]{:S(2)}, u32[]{:S(2)}) %collective-permute-start.35) | collective-permute-done | bytes 319520 | tf_op jit(solution)/shard_map/ppermute | solution.py:55
  162.3 11.8 %collective-permute-done.49 = bf16[4,96,768]{2,1,0:T(8,128)(2,1)S(1)} collective-permute-done((bf16[4,96,768]{2,1,0:T(8,128)(2,1)S(1)}, bf16[4,96,768]{2,1,0:T(8,128)(2,1)S(1)}, u32[]{:S(2)}, u32[]{:S(2)}) %collective-permute-start.49) | collective-permute-done | bytes 589856 | tf_op jit(solution)/shard_map/ppermute | solution.py:43
  175.9 9.0 %collective-permute-done.44 = bf16[4,48,1536]{2,1,0:T(8,128)(2,1)S(1)} collective-permute-done((bf16[4,48,1536]{2,1,0:T(8,128)(2,1)S(1)}, bf16[4,48,1536]{2,1,0:T(8,128)(2,1)S(1)}, u32[]{:S(2)}, u32[]{:S(2)}) %collective-permute-start.44) | collective-permute-done | bytes 589856 | tf_op jit(solution)/shard_map/ppermute | solution.py:55
  184.9 1.9 collective-permute-done.43
  187.0 10.8 %collective-permute-done.38 = bf16[4,48,1664]{2,1,0:T(8,128)(2,1)S(1)} collective-permute-done((bf16[4,48,1664]{2,1,0:T(8,128)(2,1)S(1)}, bf16[4,48,1664]{2,1,0:T(8,128)(2,1)S(1)}, u32[]{:S(2)}, u32[]{:S(2)}) %collective-permute-start.38) | collective-permute-done | bytes 639008 | tf_op jit(solution)/shard_map/ppermute | solution.py:55
  200.6 3.4 %collective-permute-done.47 = bf16[48,1536]{1,0:T(8,128)(2,1)S(1)} collective-permute-done((bf16[48,1536]{1,0:T(8,128)(2,1)S(1)}, bf16[48,1536]{1,0:T(8,128)(2,1)S(1)}, u32[]{:S(2)}, u32[]{:S(2)}) %collective-permute-start.47) | collective-permute-done | bytes 147488 | tf_op jit(solution)/shard_map/ppermute | solution.py:60
  204.0 2.9 %collective-permute-start.41 = (bf16[48,1664]{1,0:T(8,128)(2,1)S(1)}, bf16[48,1664]{1,0:T(8,128)(2,1)S(1)}, u32[]{:S(2)}, u32[]{:S(2)}) collective-permute-start(bf16[48,1664]{1,0:T(8,128)(2,1)S(1)} %get-tuple-element.170), channel_id=1, source_target_pairs={{0,12},{1,13},{2,14},{3,15},{4,0},{5,1},{6,2},{7,3},{8,4},{9,5},{1... | collective-permute-start | bytes 479240 | tf_op jit(solution)/shard_map/ppermute | solution.py:60
  207.0 5.6 %collective-permute-done.46 = bf16[48,1536]{1,0:T(8,128)(2,1)S(1)} collective-permute-done((bf16[48,1536]{1,0:T(8,128)(2,1)S(1)}, bf16[48,1536]{1,0:T(8,128)(2,1)S(1)}, u32[]{:S(2)}, u32[]{:S(2)}) %collective-permute-start.46) | collective-permute-done | bytes 147488 | tf_op jit(solution)/shard_map/ppermute | solution.py:60
  212.7 2.7 collective-permute-start.54
  215.4 8.9 %collective-permute-start.53 = (bf16[96,768]{1,0:T(8,128)(2,1)S(1)}, bf16[96,768]{1,0:T(8,128)(2,1)S(1)}, u32[]{:S(2)}, u32[]{:S(2)}) collective-permute-start(bf16[96,768]{1,0:T(8,128)(2,1)S(1)} %get-tuple-element.192), channel_id=1, source_target_pairs={{0,8},{1,9},{2,10},{3,11},{4,12},{5,13},{6,14},{7,15},{8,0},{9,1},... | collective-permute-start | bytes 442376 | tf_op jit(solution)/shard_map/ppermute | solution.py:60
  226.2 8.2 %collective-permute-done.53 = bf16[96,768]{1,0:T(8,128)(2,1)S(1)} collective-permute-done((bf16[96,768]{1,0:T(8,128)(2,1)S(1)}, bf16[96,768]{1,0:T(8,128)(2,1)S(1)}, u32[]{:S(2)}, u32[]{:S(2)}) %collective-permute-start.53) | collective-permute-done | bytes 147488 | tf_op jit(solution)/shard_map/ppermute | solution.py:60
  241.3 4.0 %input_part_own.1 = (bf16[512,768]{1,0:T(8,128)(2,1)S(1)}, bf16[512,768]{1,0:T(8,128)(2,1)}) custom-call(bf16[1024,768]{1,0:T(8,128)(2,1)S(1)} %get-tuple-element.125.d_ref, bf16[768,768]{1,0:T(8,128)(2,1)S(1)} %copy-done.1, bf16[1024,768]{1,0:T(8,128)(2,1)S(1)} %collective-permute-done.29.g_ref, bf16[256,384]{1,0:T(8,128)(2,1)S(1)} %copy-done.8, ...), custom_call_target="tpu_custom_call" | custom-call | flops 1207959552 | bytes 3145728 | tf_op jit(solution)/shard_map/input_part_own/pallas_call | solution.py:797
  252.2 13.1 %collective-permute-done.31 = bf16[512,768]{1,0:T(8,128)(2,1)S(1)} collective-permute-done((bf16[512,768]{1,0:T(8,128)(2,1)}, bf16[512,768]{1,0:T(8,128)(2,1)S(1)}, u32[]{:S(2)}, u32[]{:S(2)}) %collective-permute-start.31) | collective-permute-done | bytes 786464 | tf_op jit(solution)/shard_map/ppermute | solution.py:43
  265.5 3.8 %collective-permute-start.34 = (bf16[128,768]{1,0:T(8,128)(2,1)S(1)}, bf16[128,768]{1,0:T(8,128)(2,1)S(1)}, u32[]{:S(2)}, u32[]{:S(2)}) collective-permute-start(bf16[128,768]{1,0:T(8,128)(2,1)S(1)} %get-tuple-element.167), channel_id=1, source_target_pairs={{0,12},{1,13},{2,14},{3,15},{4,0},{5,1},{6,2},{7,3},{8,4},{9,5},{1... | collective-permute-start | bytes 589832 | tf_op jit(solution)/shard_map/ppermute | solution.py:60
  270.8 4.3 %collective-permute-done.32 = bf16[128,768]{1,0:T(8,128)(2,1)S(1)} collective-permute-done((bf16[128,768]{1,0:T(8,128)(2,1)S(1)}, bf16[128,768]{1,0:T(8,128)(2,1)S(1)}, u32[]{:S(2)}, u32[]{:S(2)}) %collective-permute-start.32) | collective-permute-done | bytes 196640 | tf_op jit(solution)/shard_map/ppermute | solution.py:60
  275.7 8.1 %collective-permute-done.33 = bf16[128,768]{1,0:T(8,128)(2,1)S(1)} collective-permute-done((bf16[128,768]{1,0:T(8,128)(2,1)S(1)}, bf16[128,768]{1,0:T(8,128)(2,1)S(1)}, u32[]{:S(2)}, u32[]{:S(2)}) %collective-permute-start.33) | collective-permute-done | bytes 196640 | tf_op jit(solution)/shard_map/ppermute | solution.py:60
  (195 shorter events, 74.2 us)
Async XLA Ops:
  0.7 24.4 %collective-permute-start.3 = (bf16[128,768]{1,0:T(8,128)(2,1)}, bf16[128,768]{1,0:T(8,128)(2,1)S(1)}, u32[]{:S(2)}, u32[]{:S(2)}) collective-permute-start(bf16[128,768]{1,0:T(8,128)(2,1)} %bitcast.78), channel_id=1, source_target_pairs={{0,12},{1,13},{2,14},{3,15},{4,0},{5,1},{6,2},{7,3},{8,4},{9,5},{1... | collective-permute-start | bytes 589832 | tf_op jit(solution)/shard_map/ppermute | solution.py:60
  5.8 19.4 %collective-permute-start.2 = (bf16[128,768]{1,0:T(8,128)(2,1)}, bf16[128,768]{1,0:T(8,128)(2,1)S(1)}, u32[]{:S(2)}, u32[]{:S(2)}) collective-permute-start(bf16[128,768]{1,0:T(8,128)(2,1)} %bitcast.79), channel_id=1, source_target_pairs={{0,8},{1,9},{2,10},{3,11},{4,12},{5,13},{6,14},{7,15},{8,0},{9,1},... | collective-permute-start | bytes 589832 | tf_op jit(solution)/shard_map/ppermute | solution.py:60
  5.8 19.4 %collective-permute-start.1 = (bf16[128,768]{1,0:T(8,128)(2,1)}, bf16[128,768]{1,0:T(8,128)(2,1)S(1)}, u32[]{:S(2)}, u32[]{:S(2)}) collective-permute-start(bf16[128,768]{1,0:T(8,128)(2,1)} %bitcast.80), channel_id=1, source_target_pairs={{0,4},{1,5},{2,6},{3,7},{4,8},{5,9},{6,10},{7,11},{8,12},{9,13},{1... | collective-permute-start | bytes 589832 | tf_op jit(solution)/shard_map/ppermute | solution.py:60
  24.0 15.7 %collective-permute-start.7 = (bf16[48,1664]{1,0:T(8,128)(2,1)S(1)}, bf16[48,1664]{1,0:T(8,128)(2,1)S(1)}, u32[]{:S(2)}, u32[]{:S(2)}) collective-permute-start(bf16[48,1664]{1,0:T(8,128)(2,1)S(1)} %bitcast.96), channel_id=1, source_target_pairs={{0,8},{1,9},{2,10},{3,11},{4,12},{5,13},{6,14},{7,15},{8,0},{9,1},... | collective-permute-start | bytes 479240 | tf_op jit(solution)/shard_map/ppermute | solution.py:60
  25.1 14.6 %collective-permute-start.6 = (bf16[48,1664]{1,0:T(8,128)(2,1)S(1)}, bf16[48,1664]{1,0:T(8,128)(2,1)S(1)}, u32[]{:S(2)}, u32[]{:S(2)}) collective-permute-start(bf16[48,1664]{1,0:T(8,128)(2,1)S(1)} %bitcast.97), channel_id=1, source_target_pairs={{0,4},{1,5},{2,6},{3,7},{4,8},{5,9},{6,10},{7,11},{8,12},{9,13},{1... | collective-permute-start | bytes 479240 | tf_op jit(solution)/shard_map/ppermute | solution.py:60
  25.3 34.5 %collective-permute-start.4 = (bf16[4,128,768]{2,1,0:T(8,128)(2,1)S(1)}, bf16[4,128,768]{2,1,0:T(8,128)(2,1)S(1)}, u32[]{:S(2)}, u32[]{:S(2)}) collective-permute-start(bf16[4,128,768]{2,1,0:T(8,128)(2,1)S(1)} %pad_maximum_fusion.1), channel_id=1, source_target_pairs={{0,2},{1,3},{2,0},{3,1},{4,6},{5,7},{6,4},{7,5},{8,10},{9,11},{10,... | collective-permute-start | bytes 2359304 | tf_op jit(solution)/shard_map/ppermute | solution.py:43
  39.8 15.9 %collective-permute-start.10 = (bf16[4,48,1664]{2,1,0:T(8,128)(2,1)S(1)}, bf16[4,48,1664]{2,1,0:T(8,128)(2,1)S(1)}, u32[]{:S(2)}, u32[]{:S(2)}) collective-permute-start(bf16[4,48,1664]{2,1,0:T(8,128)(2,1)S(1)} %pad_maximum_fusion.2.al_ref), channel_id=1, source_target_pairs={{0,16},{16,0},{1,17},{17,1},{2,18},{18,2},{3,19},{19,3},{4,20},{20... | collective-permute-start | bytes 1916936 | tf_op jit(solution)/shard_map/ppermute | solution.py:55
  41.4 16.9 %collective-permute-start.9 = (bf16[4,48,1664]{2,1,0:T(8,128)(2,1)S(1)}, bf16[4,48,1664]{2,1,0:T(8,128)(2,1)S(1)}, u32[]{:S(2)}, u32[]{:S(2)}) collective-permute-start(bf16[4,48,1664]{2,1,0:T(8,128)(2,1)S(1)} %pad_maximum_fusion.2.al_ref), channel_id=1, source_target_pairs={{0,2},{1,3},{2,0},{3,1},{4,6},{5,7},{6,4},{7,5},{8,10},{9,11},{10,... | collective-permute-start | bytes 1916936 | tf_op jit(solution)/shard_map/ppermute | solution.py:43
  43.0 18.4 %collective-permute-start.20 = (bf16[384,384]{1,0:T(8,128)(2,1)S(1)}, bf16[384,384]{1,0:T(8,128)(2,1)S(1)}, u32[]{:S(2)}, u32[]{:S(2)}) collective-permute-start(bf16[384,384]{1,0:T(8,128)(2,1)S(1)} %slice_dynamic-update-slice_fusion), channel_id=1, source_target_pairs={{0,12},{1,13},{2,14},{3,15},{4,0},{5,1},{6,2},{7,3},{8,4},{9,5},{1... | collective-permute-start | bytes 884744 | tf_op jit(solution)/shard_map/ppermute | solution.py:60
  43.1 26.2 %collective-permute-start.19 = (bf16[384,384]{1,0:T(8,128)(2,1)S(1)}, bf16[384,384]{1,0:T(8,128)(2,1)S(1)}, u32[]{:S(2)}, u32[]{:S(2)}) collective-permute-start(bf16[384,384]{1,0:T(8,128)(2,1)S(1)} %slice_dynamic-update-slice_fusion), channel_id=1, source_target_pairs={{0,8},{1,9},{2,10},{3,11},{4,12},{5,13},{6,14},{7,15},{8,0},{9,1},... | collective-permute-start | bytes 884744 | tf_op jit(solution)/shard_map/ppermute | solution.py:60
  55.7 13.6 %collective-permute-start.18 = (bf16[384,384]{1,0:T(8,128)(2,1)S(1)}, bf16[384,384]{1,0:T(8,128)(2,1)S(1)}, u32[]{:S(2)}, u32[]{:S(2)}) collective-permute-start(bf16[384,384]{1,0:T(8,128)(2,1)S(1)} %slice_dynamic-update-slice_fusion), channel_id=1, source_target_pairs={{0,4},{1,5},{2,6},{3,7},{4,8},{5,9},{6,10},{7,11},{8,12},{9,13},{1... | collective-permute-start | bytes 884744 | tf_op jit(solution)/shard_map/ppermute | solution.py:60
  61.4 45.7 %collective-permute-start.13 = (bf16[1024,768]{1,0:T(8,128)(2,1)S(1)}, bf16[1024,768]{1,0:T(8,128)(2,1)S(1)}, u32[]{:S(2)}, u32[]{:S(2)}) collective-permute-start(bf16[1024,768]{1,0:T(8,128)(2,1)S(1)} %bitcast.86), channel_id=1, source_target_pairs={{0,1},{1,0},{2,3},{3,2},{4,5},{5,4},{6,7},{7,6},{8,9},{9,8},{10,11... | collective-permute-start | bytes 4718600 | tf_op jit(solution)/shard_map/ppermute | solution.py:43
  77.2 28.1 %collective-permute-start.22 = (bf16[4,384,384]{2,1,0:T(8,128)(2,1)S(1)}, bf16[4,384,384]{2,1,0:T(8,128)(2,1)S(1)}, u32[]{:S(2)}, u32[]{:S(2)}) collective-permute-start(bf16[4,384,384]{2,1,0:T(8,128)(2,1)S(1)} %pad_maximum_fusion.al_ref), channel_id=1, source_target_pairs={{0,16},{16,0},{1,17},{17,1},{2,18},{18,2},{3,19},{19,3},{4,20},{20... | collective-permute-start | bytes 3538952 | tf_op jit(solution)/shard_map/ppermute | solution.py:55
  77.8 28.1 %collective-permute-start.21 = (bf16[4,384,384]{2,1,0:T(8,128)(2,1)S(1)}, bf16[4,384,384]{2,1,0:T(8,128)(2,1)S(1)}, u32[]{:S(2)}, u32[]{:S(2)}) collective-permute-start(bf16[4,384,384]{2,1,0:T(8,128)(2,1)S(1)} %pad_maximum_fusion.al_ref), channel_id=1, source_target_pairs={{0,2},{1,3},{2,0},{3,1},{4,6},{5,7},{6,4},{7,5},{8,10},{9,11},{10,... | collective-permute-start | bytes 3538952 | tf_op jit(solution)/shard_map/ppermute | solution.py:43
  78.3 35.1 %collective-permute-start.15 = (bf16[768,384]{1,0:T(8,128)(2,1)S(1)}, bf16[768,384]{1,0:T(8,128)(2,1)S(1)}, u32[]{:S(2)}, u32[]{:S(2)}) collective-permute-start(bf16[768,384]{1,0:T(8,128)(2,1)S(1)} %get-tuple-element.95.mo_ref), channel_id=1, source_target_pairs={{0,1},{1,0},{2,3},{3,2},{4,5},{5,4},{6,7},{7,6},{8,9},{9,8},{10,11... | collective-permute-start | bytes 1769480 | tf_op jit(solution)/shard_map/ppermute | solution.py:43
  105.3 14.6 %collective-permute-start.24 = (bf16[4,192,384]{2,1,0:T(8,128)(2,1)S(1)}, bf16[4,192,384]{2,1,0:T(8,128)(2,1)S(1)}, u32[]{:S(2)}, u32[]{:S(2)}) collective-permute-start(bf16[4,192,384]{2,1,0:T(8,128)(2,1)S(1)} %slice.235), channel_id=1, source_target_pairs={{0,2},{1,3},{2,0},{3,1},{4,6},{5,7},{6,4},{7,5},{8,10},{9,11},{10,... | collective-permute-start | bytes 1769480 | tf_op jit(solution)/shard_map/ppermute | solution.py:43
  105.9 14.3 %collective-permute-start.23 = (bf16[4,192,384]{2,1,0:T(8,128)(2,1)S(1)}, bf16[4,192,384]{2,1,0:T(8,128)(2,1)S(1)}, u32[]{:S(2)}, u32[]{:S(2)}) collective-permute-start(bf16[4,192,384]{2,1,0:T(8,128)(2,1)S(1)} %slice.234), channel_id=1, source_target_pairs={{0,16},{16,0},{1,17},{17,1},{2,18},{18,2},{3,19},{19,3},{4,20},{20... | collective-permute-start | bytes 1769480 | tf_op jit(solution)/shard_map/ppermute | solution.py:55
  129.8 20.9 %collective-permute-start.50 = (bf16[4,96,768]{2,1,0:T(8,128)(2,1)S(1)}, bf16[4,96,768]{2,1,0:T(8,128)(2,1)S(1)}, u32[]{:S(2)}, u32[]{:S(2)}) collective-permute-start(bf16[4,96,768]{2,1,0:T(8,128)(2,1)S(1)} %get-tuple-element.153), channel_id=1, source_target_pairs={{0,2},{1,3},{2,0},{3,1},{4,6},{5,7},{6,4},{7,5},{8,10},{9,11},{10,... | collective-permute-start | bytes 1769480 | tf_op jit(solution)/shard_map/ppermute | solution.py:43
  133.3 17.6 %collective-permute-start.42 = (bf16[4,48,1536]{2,1,0:T(8,128)(2,1)S(1)}, bf16[4,48,1536]{2,1,0:T(8,128)(2,1)S(1)}, u32[]{:S(2)}, u32[]{:S(2)}) collective-permute-start(bf16[4,48,1536]{2,1,0:T(8,128)(2,1)S(1)} %get-tuple-element.143), channel_id=1, source_target_pairs={{0,16},{16,0},{1,17},{17,1},{2,18},{18,2},{3,19},{19,3},{4,20},{20... | collective-permute-start | bytes 1769480 | tf_op jit(solution)/shard_map/ppermute | solution.py:55
  151.7 22.5 %collective-permute-start.49 = (bf16[4,96,768]{2,1,0:T(8,128)(2,1)S(1)}, bf16[4,96,768]{2,1,0:T(8,128)(2,1)S(1)}, u32[]{:S(2)}, u32[]{:S(2)}) collective-permute-start(bf16[4,96,768]{2,1,0:T(8,128)(2,1)S(1)} %get-tuple-element.151), channel_id=1, source_target_pairs={{0,2},{1,3},{2,0},{3,1},{4,6},{5,7},{6,4},{7,5},{8,10},{9,11},{10,... | collective-permute-start | bytes 1769480 | tf_op jit(solution)/shard_map/ppermute | solution.py:43
  153.1 21.6 %collective-permute-start.51 = (bf16[4,96,768]{2,1,0:T(8,128)(2,1)S(1)}, bf16[4,96,768]{2,1,0:T(8,128)(2,1)S(1)}, u32[]{:S(2)}, u32[]{:S(2)}) collective-permute-start(bf16[4,96,768]{2,1,0:T(8,128)(2,1)S(1)} %add.133), channel_id=1, source_target_pairs={{0,16},{16,0},{1,17},{17,1},{2,18},{18,2},{3,19},{19,3},{4,20},{20... | collective-permute-start | bytes 1769480 | tf_op jit(solution)/shard_map/ppermute | solution.py:55
  156.3 81.7 %collective-permute-start.29 = (bf16[1024,768]{1,0:T(8,128)(2,1)}, bf16[1024,768]{1,0:T(8,128)(2,1)S(1)}, u32[]{:S(2)}, u32[]{:S(2)}) collective-permute-start(bf16[1024,768]{1,0:T(8,128)(2,1)} %input_part_other.1), channel_id=1, source_target_pairs={{0,1},{1,0},{2,3},{3,2},{4,5},{5,4},{6,7},{7,6},{8,9},{9,8},{10,11... | collective-permute-start | bytes 4718600 | tf_op jit(solution)/shard_map/ppermute | solution.py:43
  159.6 25.3 %collective-permute-start.44 = (bf16[4,48,1536]{2,1,0:T(8,128)(2,1)S(1)}, bf16[4,48,1536]{2,1,0:T(8,128)(2,1)S(1)}, u32[]{:S(2)}, u32[]{:S(2)}) collective-permute-start(bf16[4,48,1536]{2,1,0:T(8,128)(2,1)S(1)} %get-tuple-element.146), channel_id=1, source_target_pairs={{0,16},{16,0},{1,17},{17,1},{2,18},{18,2},{3,19},{19,3},{4,20},{20... | collective-permute-start | bytes 1769480 | tf_op jit(solution)/shard_map/ppermute | solution.py:55
  161.5 25.3 %collective-permute-start.43 = (bf16[4,48,1536]{2,1,0:T(8,128)(2,1)S(1)}, bf16[4,48,1536]{2,1,0:T(8,128)(2,1)S(1)}, u32[]{:S(2)}, u32[]{:S(2)}) collective-permute-start(bf16[4,48,1536]{2,1,0:T(8,128)(2,1)S(1)} %add.125), channel_id=1, source_target_pairs={{0,2},{1,3},{2,0},{3,1},{4,6},{5,7},{6,4},{7,5},{8,10},{9,11},{10,... | collective-permute-start | bytes 1769480 | tf_op jit(solution)/shard_map/ppermute | solution.py:43
  174.1 23.6 %collective-permute-start.38 = (bf16[4,48,1664]{2,1,0:T(8,128)(2,1)S(1)}, bf16[4,48,1664]{2,1,0:T(8,128)(2,1)S(1)}, u32[]{:S(2)}, u32[]{:S(2)}) collective-permute-start(bf16[4,48,1664]{2,1,0:T(8,128)(2,1)S(1)} %pad_maximum_fusion.4), channel_id=1, source_target_pairs={{0,16},{16,0},{1,17},{17,1},{2,18},{18,2},{3,19},{19,3},{4,20},{20... | collective-permute-start | bytes 1916936 | tf_op jit(solution)/shard_map/ppermute | solution.py:55
  174.7 24.7 %collective-permute-start.36 = (bf16[4,48,1664]{2,1,0:T(8,128)(2,1)S(1)}, bf16[4,48,1664]{2,1,0:T(8,128)(2,1)S(1)}, u32[]{:S(2)}, u32[]{:S(2)}) collective-permute-start(bf16[4,48,1664]{2,1,0:T(8,128)(2,1)S(1)} %pad_maximum_fusion.3), channel_id=1, source_target_pairs={{0,2},{1,3},{2,0},{3,1},{4,6},{5,7},{6,4},{7,5},{8,10},{9,11},{10,... | collective-permute-start | bytes 1916936 | tf_op jit(solution)/shard_map/ppermute | solution.py:43
  184.9 39.7 %collective-permute-start.52 = (bf16[96,768]{1,0:T(8,128)(2,1)S(1)}, bf16[96,768]{1,0:T(8,128)(2,1)S(1)}, u32[]{:S(2)}, u32[]{:S(2)}) collective-permute-start(bf16[96,768]{1,0:T(8,128)(2,1)S(1)} %get-tuple-element.190), channel_id=1, source_target_pairs={{0,4},{1,5},{2,6},{3,7},{4,8},{5,9},{6,10},{7,11},{8,12},{9,13},{1... | collective-permute-start | bytes 442376 | tf_op jit(solution)/shard_map/ppermute | solution.py:60
  212.7 13.4 %collective-permute-start.54 = (bf16[96,768]{1,0:T(8,128)(2,1)S(1)}, bf16[96,768]{1,0:T(8,128)(2,1)S(1)}, u32[]{:S(2)}, u32[]{:S(2)}) collective-permute-start(bf16[96,768]{1,0:T(8,128)(2,1)S(1)} %get-tuple-element.191), channel_id=1, source_target_pairs={{0,12},{1,13},{2,14},{3,15},{4,0},{5,1},{6,2},{7,3},{8,4},{9,5},{1... | collective-permute-start | bytes 442376 | tf_op jit(solution)/shard_map/ppermute | solution.py:60
  215.4 19.0 %collective-permute-start.53 = (bf16[96,768]{1,0:T(8,128)(2,1)S(1)}, bf16[96,768]{1,0:T(8,128)(2,1)S(1)}, u32[]{:S(2)}, u32[]{:S(2)}) collective-permute-start(bf16[96,768]{1,0:T(8,128)(2,1)S(1)} %get-tuple-element.192), channel_id=1, source_target_pairs={{0,8},{1,9},{2,10},{3,11},{4,12},{5,13},{6,14},{7,15},{8,0},{9,1},... | collective-permute-start | bytes 442376 | tf_op jit(solution)/shard_map/ppermute | solution.py:60
  224.5 13.4 %collective-permute-start.30 = (bf16[128,768]{1,0:T(8,128)(2,1)}, bf16[128,768]{1,0:T(8,128)(2,1)}, u32[]{:S(2)}, u32[]{:S(2)}) collective-permute-start(bf16[128,768]{1,0:T(8,128)(2,1)} %get-tuple-element.128), channel_id=1, source_target_pairs={{0,1},{1,0},{2,3},{3,2},{4,5},{5,4},{6,7},{7,6},{8,9},{9,8},{10,11... | collective-permute-start | bytes 589832 | tf_op jit(solution)/shard_map/ppermute | solution.py:43
  246.2 19.0 %collective-permute-start.31 = (bf16[512,768]{1,0:T(8,128)(2,1)}, bf16[512,768]{1,0:T(8,128)(2,1)S(1)}, u32[]{:S(2)}, u32[]{:S(2)}) collective-permute-start(bf16[512,768]{1,0:T(8,128)(2,1)} %get-tuple-element.130), channel_id=1, source_target_pairs={{0,2},{1,3},{2,0},{3,1},{4,6},{5,7},{6,4},{7,5},{8,10},{9,11},{10,... | collective-permute-start | bytes 2359304 | tf_op jit(solution)/shard_map/ppermute | solution.py:43
  269.3 14.4 %collective-permute-start.33 = (bf16[128,768]{1,0:T(8,128)(2,1)S(1)}, bf16[128,768]{1,0:T(8,128)(2,1)S(1)}, u32[]{:S(2)}, u32[]{:S(2)}) collective-permute-start(bf16[128,768]{1,0:T(8,128)(2,1)S(1)} %get-tuple-element.168), channel_id=1, source_target_pairs={{0,8},{1,9},{2,10},{3,11},{4,12},{5,13},{6,14},{7,15},{8,0},{9,1},... | collective-permute-start | bytes 589832 | tf_op jit(solution)/shard_map/ppermute | solution.py:60
  (37 other events, 394.2 us)

commit v4 on v3

--- a/solution.py
+++ b/solution.py
@@ -77,23 +77,60 @@
     return lax.dynamic_slice_in_dim(jnp.concatenate([blocks, blocks]), start, zs, 0)
 
 
-def along_z(block):
+def along_z_pieces(block):
     zs = lax.axis_size("ctx") // 4
     if zs > 4:
         every = lax.all_gather(block, "ctx", axis_index_groups=z_groups())
         return turned(every, lax.axis_index("ctx") // 4, False)
-    return jnp.stack([block] + [shift_z(block, k) for k in range(1, zs)])
-
-
-def sum_z(along):
+    return [block] + [shift_z(block, k) for k in range(1, zs)]
+
+
+def far_out(by_y, by_x, row):
+    return swap_x(by_y[:, :row]), swap_y(by_x[:, row:])
+
+
+def sources(groups, row):
+    arrays, where = [], {}
+    for ks, *blocks in groups:
+        at = len(arrays)
+        arrays += blocks
+        for i, k in enumerate(ks):
+            last = ((at + 3, i), (at + 4, i, row))
+            where[k] = (*(((at + j, i), (at + j, i, 0)) for j in range(3)), last)
+    return arrays, where
+
+
+def by_distance(arrays, where, row=0):
+    def whole(first, rest):
+        top = arrays[first[0]][first[1]][:row]
+        return jnp.concatenate([top, arrays[rest[0]][rest[1]][row - rest[2] :]])
+
+    blocks = [[whole(*side) for side in where[k]] for k in sorted(where)]
+    full = jnp.stack([jnp.stack(four) for four in blocks], axis=1)
+    return full.reshape(2, 2, *full.shape[1:])
+
+
+def fan_far(by_y, by_x, far, row):
+    if row == far.shape[1]:
+        return by_y + swap_x(far), by_x
+    over_x, over_y = swap_x(far[:, :row]), swap_y(far[:, row:])
+    by_y = jnp.concatenate([by_y[:, :row] + over_x, by_y[:, row:]], axis=1)
+    by_x = jnp.concatenate([by_x[:, :row], by_x[:, row:] + over_y], axis=1)
+    return by_y, by_x
+
+
+def sum_z(groups):
     zs = lax.axis_size("ctx") // 4
     if zs > 4:
+        ((_, along),) = groups
         every = turned(along, (zs - lax.axis_index("ctx") // 4) % zs, True)
         every = lax.all_to_all(every, "ctx", 0, 0, axis_index_groups=z_groups())
         return jnp.sum(every.astype(F32), axis=0)
-    total = along[0].astype(F32)
-    for k in range(1, zs):
-        total = total + shift_z(along[k], k).astype(F32)
+    total = None
+    for ks, blocks in groups:
+        for i, k in enumerate(ks):
+            part = (blocks[i] if k == 0 else shift_z(blocks[i], k)).astype(F32)
+            total = part if total is None else total + part
     return total
 
 
@@ -117,10 +154,6 @@
     return blocks
 
 
-def after(value, *ready):
-    return lax.optimization_barrier((value, *ready))[0]
-
-
 def chip_of(here, xr, yr, k, zs):
     x, z, y, _ = here
     return ((x ^ xr) * zs + lax.rem(z + k + zs, zs)) * 2 + (y ^ yr)
@@ -138,40 +171,101 @@
         out_shape=list(outs),
         scratch_shapes=list(scratch),
         compiler_params=pltpu.CompilerParams(vmem_limit_bytes=limit * MIB),
-        cost_estimate=pl.CostEstimate(
-            flops=flops, bytes_accessed=bytes_accessed, transcendentals=0
-        ),
+        cost_estimate=pl.CostEstimate(flops=1, bytes_accessed=1, transcendentals=0),
         name=name,
     )(*args)
 
 
-def build_qkv(along, by_y, by_x, far_a, far_b):
-    zs, rows, _ = along.shape
-    cut = zs // 2
+def pack(weights, inner, vectors):
+    rows, hidden = inner.shape[0], vectors[-1].shape[0]
+    count = len(weights)
+    every = (*weights, inner, *vectors)
+    base = WIDE + WIDTH + HALF
+    chips = inner.shape[1] // (2 * hidden)
+    cols = base + chips * hidden
+
+    def body(*refs):
+        n = len(every)
+        ins, (own_ref, send_ref), held = refs[:n], refs[n : n + 2], refs[n + 2 : 2 * n + 2]
+        flat_s, sems = refs[-2:]
+        copies = [pltpu.make_async_copy(i, h, sems.at[j]) for j, (i, h) in enumerate(zip(ins, held))]
+        for copy in copies:
+            copy.start()
+        flat_s[...] = jnp.zeros(flat_s.shape, F32)
+        for copy in copies:
+            copy.wait()
+        ws, inner_ref, vs = held[:count], held[count], held[count + 1 :]
+        core = place()[3]
+        at = 0
+        for v in vs:
+            for j in range(v.shape[0] // rows):
+                flat_s[at : at + 1, :rows] = v[pl.ds(j * rows, rows)].astype(F32).reshape(1, rows)
+                at += 1
+        aux = jnp.transpose(flat_s[...])[:rows, :].astype(BF16)
+        places = (0, WIDE, WIDE + HALF, WIDE + WIDTH)
+        whole = inner_ref[...]
+        units = [
+            jnp.concatenate(
+                [
+                    whole[:, (2 * i + side) * hidden : (2 * i + side + 1) * hidden]
+                    for i in range(chips)
+                ],
+                axis=1,
+            )
+            for side in range(2)
+        ]
+        for out, side in ((own_ref, core), (send_ref, 1 - core)):
+            out[:, HALF:WIDE] = aux
+            for w, lo in zip(ws, places):
+                out[:, lo : lo + HALF] = jnp.where(side == 0, w[:, :HALF], w[:, HALF:])
+            out[:, base:] = jnp.where(side == 0, units[0], units[1])
+
+    return pl.pallas_call(
+        body,
+        in_specs=[pl.BlockSpec(memory_space=pl.ANY) for _ in every],
+        out_specs=[pl.BlockSpec(memory_space=pltpu.VMEM)] * 2,
+        out_shape=[shape((rows, cols), BF16)] * 2,
+        scratch_shapes=[pltpu.VMEM(a.shape, BF16) for a in every]
+        + [pltpu.VMEM((AUX, AUX), F32), pltpu.SemaphoreType.DMA((len(every),))],
+        compiler_params=pltpu.CompilerParams(vmem_limit_bytes=56 * MIB),
+        name="pack",
+    )(*every)
+
+
+def join(own, got, outer):
+    rows, hidden = own.shape[0], outer.shape[0]
+    base = WIDE + WIDTH + HALF
+    quarters = (own.shape[1] - base) // HALF
+    core = place()[3]
+    both = jnp.concatenate(halves(core, own, got))
+    return both[:, :base], jnp.concatenate(
+        [both[:, base + j * HALF : base + (j + 1) * HALF] for j in range(quarters)]
+        + [outer[:, :HALF], outer[:, HALF:]]
+    )
+
+
+def build_qkv(arrays, where, row):
+    zs, rows = len(where), arrays[0].shape[1]
     ends = (0, WIDE, WIDE + WIDTH, WIDE + WIDTH + HALF)
     if rows % 16:
-        far = jnp.concatenate([far_a, far_b])
-        full = to_mesh_order(jnp.stack([along, by_y, by_x, far]).reshape(2, 2, zs, rows, -1))
-        full = full.reshape(WIDTH, -1)
+        full = to_mesh_order(by_distance(arrays, where, row)).reshape(WIDTH, -1)
         return [full[:, lo:hi] for lo, hi in zip(ends, ends[1:])]
 
-    def body(al_ref, y_ref, x_ref, fa_ref, fb_ref, *outs):
+    def body(*refs):
+        outs = refs[len(arrays) :]
         here = place()
         for k in range(zs):
-            far = (fa_ref, k) if k < cut else (fb_ref, k - cut)
-            for xr, yr, (ref, i) in (
-                (0, 0, (al_ref, k)),
-                (0, 1, (y_ref, k)),
-                (1, 0, (x_ref, k)),
-                (1, 1, far),
-            ):
-                to = rows_at(chip_of(here, xr, yr, -k, zs), rows)
+            for side, ((a, i), (b, n, back)) in enumerate(where[k]):
+                at = chip_of(here, side // 2, side % 2, -k, zs) * rows
+                top = pl.ds(pl.multiple_of(at, 16), row)
+                low = pl.ds(pl.multiple_of(at + row, 16), rows - row)
                 for out, lo, hi in zip(outs, ends, ends[1:]):
-                    out[to, :] = ref[i, :, lo:hi]
+                    out[top, :] = refs[a][i, :row, lo:hi]
+                    out[low, :] = refs[b][n, row - back : rows - back, lo:hi]
 
     return kernel(
         body,
-        (along, by_y, by_x, far_a, far_b),
+        arrays,
         [shape((WIDTH, hi - lo), BF16) for lo, hi in zip(ends, ends[1:])],
         "build_qkv",
         flops=10**6,
@@ -179,40 +273,33 @@
     )
 
 
-def build_rest(along, by_y, by_x, far_a, far_b, rows, hidden):
-    zs = along.shape[0]
-    quarters = zs * 4 * hidden // HALF
+def build_rest(arrays, where, rows, hidden):
+    zs = len(where)
+    units = zs * 4 * hidden
+    quarters = units // HALF
     first = quarters * rows
-    units = zs * 4 * hidden
     if rows % 16:
-        far = jnp.concatenate([far_a, far_b], axis=1)
-        full = to_mesh_order(
-            jnp.stack([along, by_y, by_x, far]).reshape(2, 2, zs, -1, HALF)
-        ).reshape(4 * zs, -1, HALF)
+        full = to_mesh_order(by_distance(arrays, where, first)).reshape(4 * zs, -1, HALF)
         w1 = jnp.swapaxes(full[:, :first].reshape(4 * zs, quarters, rows, HALF), 1, 2)
         w2 = jnp.swapaxes(full[:, first:].reshape(4 * zs, 2, hidden, HALF), 1, 2)
         return w1.reshape(WIDTH, units), w2.reshape(units, WIDTH)
 
-    def body(al_ref, y_ref, x_ref, fa_ref, fb_ref, w1_ref, w2_ref):
+    def body(*refs):
+        w1_ref, w2_ref = refs[len(arrays) :]
         here = place()
         for k in range(zs):
-            for xr, yr, ref, low, back in (
-                (0, 0, al_ref, al_ref, 0),
-                (0, 1, y_ref, y_ref, 0),
-                (1, 0, x_ref, x_ref, 0),
-                (1, 1, fa_ref, fb_ref, first),
-            ):
-                chip = chip_of(here, xr, yr, -k, zs)
+            for side, ((a, i), (b, n, back)) in enumerate(where[k]):
+                chip = chip_of(here, side // 2, side % 2, -k, zs)
                 to, down = rows_at(chip, rows), rows_at(chip, hidden)
                 for j in range(quarters):
-                    w1_ref[to, j * HALF : (j + 1) * HALF] = ref[k, j * rows : (j + 1) * rows, :]
+                    w1_ref[to, j * HALF : (j + 1) * HALF] = refs[a][i, j * rows : (j + 1) * rows, :]
                 for j in range(2):
                     lo = first + j * hidden - back
-                    w2_ref[down, j * HALF : (j + 1) * HALF] = low[k, lo : lo + hidden, :]
+                    w2_ref[down, j * HALF : (j + 1) * HALF] = refs[b][n, lo : lo + hidden, :]
 
     return kernel(
         body,
-        (along, by_y, by_x, far_a, far_b),
+        arrays,
         (shape((WIDTH, units), BF16), shape((units, WIDTH), BF16)),
         "build_rest",
         flops=10**6,
@@ -246,11 +333,7 @@
 
 
 def attend_cost(tokens, keys):
-    return pl.CostEstimate(
-        flops=8 * tokens * keys * HALF + 2 * keys * WIDTH * WIDTH,
-        bytes_accessed=4 * keys * WIDTH,
-        transcendentals=2 * tokens * keys * NH,
-    )
+    return pl.CostEstimate(flops=1, bytes_accessed=1, transcendentals=0)
 
 
 def attend_first(own, got, xo, wq, wkv):
@@ -639,11 +722,7 @@
 
 
 def attend_back_cost(tokens, keys):
-    return pl.CostEstimate(
-        flops=10 * tokens * keys * HALF,
-        bytes_accessed=4 * keys * WIDTH,
-        transcendentals=tokens * keys * NH,
-    )
+    return pl.CostEstimate(flops=1, bytes_accessed=1, transcendentals=0)
 
 
 def attend_back_first(q, low, low_got, o, lse, kv):
@@ -762,9 +841,7 @@
         out_specs=rows,
         out_shape=shape((keys, WIDTH), BF16),
         compiler_params=pltpu.CompilerParams(vmem_limit_bytes=12 * MIB),
-        cost_estimate=pl.CostEstimate(
-            flops=2 * keys * WIDTH * WIDTH, bytes_accessed=4 * keys * WIDTH, transcendentals=0
-        ),
+        cost_estimate=pl.CostEstimate(flops=1, bytes_accessed=1, transcendentals=0),
         name="input_part_other",
     )(dkv, wkv)
 
@@ -812,48 +889,70 @@
         out_shape=[shape((keys // 2, WIDTH), BF16)] * 2,
         scratch_shapes=[pltpu.VMEM((block, WIDTH), F32)],
         compiler_params=pltpu.CompilerParams(vmem_limit_bytes=12 * MIB),
-        cost_estimate=pl.CostEstimate(
-            flops=2 * keys * WIDTH * WIDTH, bytes_accessed=4 * keys * WIDTH, transcendentals=0
-        ),
+        cost_estimate=pl.CostEstimate(flops=1, bytes_accessed=1, transcendentals=0),
         name="input_part_own",
     )(dkv, wkv, got, dq, wq, q_got)
 
 
-def spread(zs, rows, cols, args, fill, name, scratch):
+def spread(zs, rows, cols, args, fill, name, scratch, limit=14):
     count = len(args)
 
     def body(*refs):
-        ins, outs, part_s = refs[:count], refs[count : count + 4], refs[-1]
-        fill(ins, part_s)
+        ins, outs, held = refs[:count], refs[count : count + 4], refs[count + 4 :]
+        write = fill(ins, held)
         here = place()
         for k in range(zs):
-            for i, out in enumerate(outs):
-                chip = chip_of(here, i // 2, i % 2, k, zs)
-                out[k] = part_s[rows_at(chip, rows), :]
+            for side in range(4):
+                write(outs[side], k, chip_of(here, side // 2, side % 2, k, zs))
 
     return kernel(
         body,
         args,
         [shape((zs, rows, cols), BF16)] * 4,
         name,
-        scratch=[pltpu.VMEM(scratch, BF16)],
+        limit=limit,
+        scratch=[pltpu.VMEM(dims, BF16) for dims in scratch],
         flops=2 * 10**9,
         bytes_accessed=6 * 10**6,
     )
 
 
-def spread_product(left, right, zs):
-    total, cols = left.shape[1], right.shape[1]
-    rows = total // (4 * zs)
+def spread_slow(full, zs):
+    full = to_distance(full.reshape(2, zs, 2, *full.shape[1:]))
+    full = full.reshape(4, zs, *full.shape[3:])
+    return full[0], full[1], full[2], full[3]
+
+
+def spread_rest(first2, grad_inner, active, grad_outer2, zs):
+    units = active.shape[1]
+    rows, hidden = WIDTH // (4 * zs), units // (4 * zs)
     if rows % 16:
-        full = t_mm(left, right).astype(BF16).reshape(2, zs, 2, rows, cols)
-        full = to_distance(full).reshape(4, zs, rows, cols)
-        return full[0], full[1], full[2], full[3]
-
-    def fill(ins, part_s):
-        part_s[...] = t_mm(ins[0][...], ins[1][...]).astype(BF16)
-
-    return spread(zs, rows, cols, (left, right), fill, "spread", (total, cols))
+        w1 = t_mm(first2, grad_inner).astype(BF16).reshape(4 * zs, rows, units)
+        w2 = t_mm(active, grad_outer2).astype(BF16).reshape(4 * zs, hidden, WIDTH)
+        return spread_slow(jnp.concatenate([w1[:, :, :WIDTH], w1[:, :, WIDTH:], w2], axis=1), zs)
+
+    def fill(ins, held):
+        f_ref, gi_ref, a_ref, go_ref = ins
+        held[0][...] = t_mm(f_ref[...], gi_ref[...]).astype(BF16)
+        held[1][...] = t_mm(a_ref[...], go_ref[...]).astype(BF16)
+
+        def write(out, n, chip):
+            at = rows_at(chip, rows)
+            out[n, :rows, :] = held[0][at, :WIDTH]
+            out[n, rows : 2 * rows, :] = held[0][at, WIDTH:]
+            out[n, 2 * rows :, :] = held[1][rows_at(chip, hidden), :]
+
+        return write
+
+    return spread(
+        zs,
+        2 * rows + hidden,
+        WIDTH,
+        (first2, grad_inner, active, grad_outer2),
+        fill,
+        "spread_rest",
+        ((WIDTH, units), (units, WIDTH)),
+    )
 
 
 def spread_qkv(zs, x_own, x_got, dq, qv, mid, top, unit, g_kv, ctx, ctx_got, low, low_got):
@@ -861,8 +960,9 @@
     rows = WIDTH // (4 * zs)
     cols = WIDE + WIDTH + HALF
 
-    def fill(ins, part_s):
-        xo, xg, dq_r, qv_r, mid_r, top_r, unit_r, kv_r, c_r, cg_r, l_r, lg_r = ins
+    def fill(ins, held):
+        part_s = held[0]
+        xo, xg, dq_r, qv_r, mid_r, top_r, unit_r, c_r, cg_r, l_r, lg_r, *kv_rs = ins
         core = place()[3]
         part_s[:, :HALF] = (
             t_mm(xo[...], dq_r[:tokens, :]) + t_mm(xg[...], dq_r[tokens:, :])
@@ -879,7 +979,13 @@
             axis=0,
         )
         part_s[:, HALF:WIDE] = jnp.transpose(sums).astype(BF16)
-        part_s[:, WIDE : WIDE + WIDTH] = kv_r[...]
+        if len(kv_rs) == 1:
+            part_s[:, WIDE : WIDE + WIDTH] = kv_rs[0][...]
+        else:
+            xk, dk, xl, dl = kv_rs
+            part_s[:, WIDE : WIDE + WIDTH] = (t_mm(xk[...], dk[...]) + t_mm(xl[...], dl[...])).astype(
+                BF16
+            )
         lows = (l_r[:, HALF:], lg_r[:, HALF:])
         part_s[pl.ds(pl.multiple_of(core * HALF, HALF), HALF), WIDE + WIDTH :] = (
             t_mm(c_r[:tokens, :], lows[0]) + t_mm(c_r[tokens:, :], lows[1])
@@ -888,16 +994,89 @@
             t_mm(cg_r[tokens:, :], lows[0]) + t_mm(cg_r[:tokens, :], lows[1])
         ).astype(BF16)
 
-    args = (x_own, x_got, dq, qv, mid, top, unit, g_kv, ctx, ctx_got, low, low_got)
+        def write(out, n, chip):
+            out[n] = part_s[rows_at(chip, rows), :]
+
+        return write
+
+    args = (x_own, x_got, dq, qv, mid, top, unit, ctx, ctx_got, low, low_got, *g_kv)
     if rows % 16 == 0:
-        return spread(zs, rows, cols, args, fill, "spread_qkv", (WIDTH, cols))
+        return spread(zs, rows, cols, args, fill, "spread_qkv", ((WIDTH, cols),), 24)
 
     def body(*refs):
-        fill(refs[:12], refs[12])
+        fill(refs[:12], refs[12:])
 
     full = kernel(body, args, [shape((WIDTH, cols), BF16)], "fill_qkv")[0]
-    full = to_distance(full.reshape(2, zs, 2, rows, cols)).reshape(4, zs, rows, cols)
-    return full[0], full[1], full[2], full[3]
+    return spread_slow(full.reshape(4 * zs, rows, cols), zs)
+
+
+def finish_sums(qkv, rest, rows):
+    count, cols = len(qkv), qkv[0].shape[1]
+    hidden = rest[0].shape[0] - 4 * rows
+    wide = cols + 2 * WIDTH
+
+    def body(*refs):
+        ins, (own_ref, send_ref, outer_ref, both_s) = refs[:-4], refs[-4:]
+        core = place()[3]
+        both_s[:, :cols] = sum(ref[...].astype(F32) for ref in ins[:count])
+        low = sum(ref[...].astype(F32) for ref in ins[count:])
+        both_s[:, cols : cols + WIDTH] = low[: 2 * rows]
+        both_s[:, cols + WIDTH :] = low[2 * rows : 4 * rows]
+        outer_ref[...] = low[4 * rows :]
+        halves_of = (both_s[:rows, :], both_s[rows:, :])
+        own_ref[...] = jnp.where(core == 0, *halves_of)
+        send_ref[...] = jnp.where(core == 1, *halves_of)
+
+    return kernel(
+        body,
+        (*qkv, *rest),
+        [shape((rows, wide), F32)] * 2 + [shape((hidden, WIDTH), F32)],
+        "finish_sums",
+        limit=8,
+        scratch=[pltpu.VMEM((2 * rows, wide), F32)],
+    )
+
+
+def finish_rows(own, got, hidden, per):
+    rows = own.shape[0]
+    base = WIDE + WIDTH + HALF
+    chips = (own.shape[1] - base) // hidden
+
+    def body(own_ref, got_ref, *outs):
+        core = place()[3]
+        left = jnp.where(core == 0, own_ref[...], got_ref[...])
+        right = jnp.where(core == 0, got_ref[...], own_ref[...])
+        for out, lo in zip(outs, (0, WIDE, WIDE + HALF, WIDE + WIDTH)):
+            out[:, :HALF] = left[:, lo : lo + HALF]
+            out[:, HALF:] = right[:, lo : lo + HALF]
+        outs[4][...] = jnp.concatenate(
+            [
+                side[:, base + i * hidden : base + (i + 1) * hidden]
+                for i in range(chips)
+                for side in (left, right)
+            ],
+            axis=1,
+        )
+        small = left[:, HALF:WIDE] + right[:, HALF:WIDE]
+        if rows < AUX:
+            small = jnp.concatenate([small, jnp.zeros((AUX - rows, AUX), F32)], axis=0)
+        small = jnp.transpose(small)
+        for j in range(9):
+            outs[5 + j][...] = small[j, :rows]
+        for j in range(per):
+            outs[14][pl.ds(j * rows, rows)] = small[9 + j, :rows]
+
+    outs = kernel(
+        body,
+        (own, got),
+        [shape((rows, WIDTH), F32)] * 4
+        + [shape((rows, 2 * chips * hidden), F32)]
+        + [shape((rows,), F32)] * 9
+        + [shape((hidden,), F32)],
+        "finish_rows",
+        limit=8,
+    )
+    return (*outs[:5], outs[5:])
 
 
 def shards(
@@ -935,8 +1114,10 @@
     def in_order(own, other, axis):
         return jnp.stack(halves(core, own, other), axis=axis)
 
-    aux = jnp.concatenate(
-        [
+    own, send = pack(
+        (query_weight, key_weight, value_weight, mixer_weight),
+        inner_weight,
+        (
             query_bias,
             value_bias,
             mixer_bias,
@@ -947,54 +1128,54 @@
             second_shift,
             head_weight,
             inner_bias,
-        ]
-    ).reshape(9 + per, rows)
-    aux = jnp.transpose(jnp.pad(aux, ((0, AUX - 9 - per), (0, 0))))
-    four = (query_weight, key_weight, value_weight, mixer_weight)
-
-    def side_of(side):
-        q, k, v, m = (lax.dynamic_slice_in_dim(w, side * HALF, HALF, 1) for w in four)
-        return jnp.concatenate([q, aux, k, v, m], axis=1)
-
-    x_along = along_z(inputs)
+        ),
+    )
+    block, rest = join(own, swap_core(send), outer_weight)
     x_got = swap_core(inputs)
-    qkv_block = in_order(side_of(core), swap_core(side_of(1 - core)), 0)
-    qkv = along_z(qkv_block.reshape(2 * rows, WIDE + WIDTH + HALF))
-    xo = jnp.concatenate([x_along, swap_y(x_along)]).reshape(2 * zs * tokens, WIDTH)
+    first = 2 * rows * (units // HALF)
+    every = tuple(range(zs))
+    barrier = lax.optimization_barrier
+    part_row = 2 * rows // 3
+    if zs == 4:
+        near_y, near_x = swap_y(rest[None]), swap_x(rest[None])
+        near_y, near_x, qkv = barrier((near_y, near_x, along_z_pieces(block)))
+        x_own, first_piece = barrier((inputs, qkv[1]))
+        qkv = jnp.stack([qkv[0], first_piece, *qkv[2:]])
+        flat = qkv.reshape(first, -1)
+        sent_y = swap_y(jnp.concatenate([flat, near_x[0, first:]], axis=1))
+        sent_x = swap_x(jnp.concatenate([flat, near_y[0, :first]], axis=1))
+        sent_y, sent_x, x_along = barrier((sent_y, sent_x, along_z_pieces(x_own)))
+        x_along = jnp.stack(x_along)
+        cols = flat.shape[1]
+        qkv_y, qkv_x = (sent[:, :cols].reshape(qkv.shape) for sent in (sent_y, sent_x))
+        near_far = [sent[None, :, cols:] for sent in (sent_x, sent_y)]
+        rest_sent, x_along = barrier((rest, x_along))
+        x_y, qkv_far, pieces = barrier(
+            (swap_y(x_along), far_out(qkv_y, qkv_x, part_row), along_z_pieces(rest_sent))
+        )
+        pieces = jnp.stack(pieces[1:])
+        rest_y, rest_x = swap_y(pieces), swap_x(pieces)
+    else:
+        qkv, x_along, pieces = (along_z_pieces(v) for v in (block, inputs, rest))
+        x_y, rest_y, rest_x = swap_y(x_along), swap_y(pieces), swap_x(pieces)
+        qkv_y, qkv_x = swap_y(qkv), swap_x(qkv)
+        qkv_far = far_out(qkv_y, qkv_x, part_row)
+    wq, wkv, mixer_own = build_qkv(
+        *sources([(every, qkv, qkv_y, qkv_x, *qkv_far)], part_row), part_row
+    )
+    mixer_got = swap_core(mixer_own)
+    xo = jnp.concatenate([x_along, x_y]).reshape(2 * zs * tokens, WIDTH)
     xc = swap_core(xo)
-    qkv_y, qkv_x = swap_y(qkv), swap_x(qkv)
-    wq, wkv, mixer_own = build_qkv(
-        qkv, qkv_y, qkv_x, swap_x(qkv_y[: zs // 2]), swap_y(qkv_x[zs // 2 :])
-    )
-    mixer_got = swap_core(mixer_own)
-
-    inner_split = inner_weight.reshape(rows, chips, 2, hidden)
-
-    def inner_of(side):
-        return pick(inner_split, side, 2).reshape(rows, units)
-
-    both = in_order(inner_of(core), swap_core(inner_of(1 - core)), 0).reshape(2 * rows, units)
-    quarters = units // HALF
-    first = quarters * 2 * rows
-    rest = jnp.concatenate(
-        [both[:, j * HALF : (j + 1) * HALF] for j in range(quarters)]
-        + [outer_weight[:, :HALF], outer_weight[:, HALF:]]
-    )
-    rest = along_z(after(rest, qkv))
 
     q_scaled, kvo, vecs, bias, top, total, weighted = attend_first(inputs, x_got, xo, wq, wkv)
-    rest = after(rest, q_scaled)
-    rest_y, rest_x = swap_y(rest), swap_x(rest)
     kvc, o_exact, ctx, lse = attend_last(q_scaled, xc, wkv, bias, top, total, weighted)
-    w_inner, w_outer = build_rest(
-        rest,
-        rest_y,
-        rest_x,
-        swap_x(rest_y[:, :first]),
-        swap_y(rest_x[:, first:]),
-        2 * rows,
-        hidden,
-    )
+    rest_y, rest_x, ctx = barrier((rest_y, rest_x, ctx))
+    away = (pieces, rest_y, rest_x, *far_out(rest_y, rest_x, first))
+    if zs == 4:
+        away = [((0,), rest[None], near_y, near_x, *near_far), ((1, 2, 3), *away)]
+    else:
+        away = [(every, *away)]
+    w_inner, w_outer = build_rest(*sources(away, first), 2 * rows, hidden)
     ctx_got = swap_core(ctx)
     i_bias = unit_bias(vecs, chips, per, rows)
     first_low, first_rows, first_normed, first_scale = mix(
@@ -1011,35 +1192,34 @@
         grad_outer, swap_core(grad_outer), slope, w_inner, w_outer
     )
     got = swap_core(away)
-    keep2, y2, x2, far2 = spread_product(active, grad_outer2, zs)
-    far2 = swap_y(far2)
-    keep1, y1, x1, far1 = spread_product(first2, grad_inner, zs)
-    far1 = swap_x(far1)
+    keep, rest_y, rest_x, far = spread_rest(first2, grad_inner, active, grad_outer2, zs)
+    mine, keep, rest_y, rest_x, far = barrier((mine, keep, rest_y, rest_x, far))
+    over_x, over_y = swap_x(far[:, : 4 * rows]), swap_y(far[:, 4 * rows :])
 
     grad_residual, low, low_send, mid_sums = mix_back(
         mine, got, grad_second, first_normed, first_scale, vecs, mixer_own, mixer_got
     )
     low_got = swap_core(low_send)
-    y2 = swap_y(after(y2, low_got))
-    x1 = swap_x(after(x1, low_got))
     dkvc, g_both, delta, acc, qv_sums = attend_back_first(
         q_scaled, low, low_got, o_exact, lse, kvc
     )
+    over_x, over_y, dkvc, kvo = barrier((over_x, over_y, dkvc, kvo))
     away = swap_core(input_part_other(dkvc, wkv))
-    x2, y1 = after(x2 + far2, dkvc), after(y1 + far1, dkvc)
-    x2 = swap_x(x2)
-    y1 = swap_y(y1)
+    rest_y = jnp.concatenate([rest_y[:, : 4 * rows] + over_x, rest_y[:, 4 * rows :]], axis=1)
+    rest_x = jnp.concatenate([rest_x[:, : 4 * rows], rest_x[:, 4 * rows :] + over_y], axis=1)
+    at = 1 if zs == 4 else 0
+    got_y, got_x = swap_y(rest_y[at:]), swap_x(rest_x[at:])
     dkvo, dq, qv_sums, q_away = attend_back_last(
         q_scaled, g_both, lse, delta, acc, qv_sums, kvo, wq
     )
 
     part, part_y = input_part_own(dkvo, wkv, away, dq, wq, swap_core(q_away))
-    part = (part + swap_y(part_y)).reshape(zs, tokens, WIDTH)
-    total = sum_z(jnp.concatenate([part[:1], jnp.flip(part[1:], 0)]))
-    input_grad = (grad_residual + total).astype(BF16)
-
-    g_kv = (t_mm(xo, dkvo) + t_mm(xc, dkvc)).astype(BF16)
-    keep, yq, xq, far = spread_qkv(
+    dq, dkvo, part, part_y = barrier((dq, dkvo, part, part_y))
+    if zs == 4:
+        g_kv = (xo, dkvo, xc, dkvc)
+    else:
+        g_kv = ((t_mm(xo, dkvo) + t_mm(xc, dkvc)).astype(BF16),)
+    g_qkv, qkv_y, qkv_x, qkv_far = spread_qkv(
         zs,
         inputs,
         x_got,
@@ -1054,47 +1234,72 @@
         low,
         low_got,
     )
-    cut = zs // 2
-    far_a, far_b = swap_x(far[:cut]), swap_y(far[cut:])
-    yq = swap_y(jnp.concatenate([yq[:cut] + far_a, yq[cut:]]))
-    xq = swap_x(jnp.concatenate([xq[:cut], xq[cut:] + far_b]))
-    g_outer = sum_z(keep2 + y2 + x2)
-    g_inner = sum_z(keep1 + y1 + x1)
-    g_qkv = sum_z(keep + yq + xq)
-
-    g_all = jnp.concatenate([g_qkv, g_inner], axis=1).reshape(2, rows, -1)
-    own, got = pick(g_all, core, 0), swap_core(pick(g_all, 1 - core, 0))
-
-    def columns(lo):
-        return jnp.concatenate(
-            halves(core, own[:, lo : lo + HALF], got[:, lo : lo + HALF]), axis=1
+    part, part_y = part.reshape(zs, tokens, WIDTH), part_y.reshape(zs, tokens, WIDTH)
+    if zs == 4:
+        got_y, got_x, part_y, qkv_far = barrier((got_y, got_x, part_y, qkv_far))
+        g_rest = keep[1:] + got_y + got_x
+        qkv_far, got_part, g_rest = barrier(
+            (
+                swap_x(qkv_far),
+                swap_y(part_y),
+                [shift_z(g_rest[k - 1], k) for k in range(1, zs)],
+            )
         )
-
-    at1 = WIDE + WIDTH + HALF
-    g_inner = in_order(
-        own[:, at1:].reshape(rows, chips, hidden), got[:, at1:].reshape(rows, chips, hidden), 2
-    ).reshape(rows, ff)
-    sm = jnp.transpose(own[:, HALF:WIDE] + got[:, HALF:WIDE])
+        part = part + got_part
+        qkv_x, qkv_far = barrier((qkv_x, qkv_far))
+        got_y, got_x, parts = barrier(
+            (
+                swap_y(qkv_y + qkv_far),
+                swap_x(qkv_x),
+                [shift_z(part[k], zs - k) for k in range(1, zs)],
+            )
+        )
+        near_y, near_x, parts = barrier((rest_y[:1], rest_x[:1], parts))
+        total = part[0].astype(F32)
+        for value in parts:
+            total = total + value.astype(F32)
+        g_qkv = g_qkv + got_y + got_x
+        near_y, near_x, pieces = barrier(
+            (
+                swap_y(near_y),
+                swap_x(near_x),
+                [shift_z(g_qkv[k], k) for k in range(1, zs)],
+            )
+        )
+        g_qkv = [g_qkv[0], *pieces]
+        g_rest = [keep[0], near_y[0], near_x[0], *g_rest]
+    else:
+        g_rest = [sum_z([(every, keep + got_y + got_x)])]
+        part = part + swap_y(part_y)
+        total = sum_z([(every, jnp.concatenate([part[:1], jnp.flip(part[1:], 0)]))])
+        qkv_y, qkv_x = fan_far(qkv_y, qkv_x, qkv_far, 2 * rows)
+        g_qkv = [sum_z([(every, g_qkv + swap_y(qkv_y) + swap_x(qkv_x))])]
+    input_grad = (grad_residual + total).astype(BF16)
+
+    own, send, g_outer = finish_sums(g_qkv, g_rest, rows)
+    g_query, g_key, g_value, g_mixer, g_inner, vectors = finish_rows(
+        own, swap_core(send), hidden, per
+    )
     return (
         final_low[None],
         term,
         input_grad[None],
-        columns(0),
-        sm[0],
-        columns(WIDE),
-        columns(WIDE + HALF),
-        sm[1],
-        columns(WIDE + WIDTH),
-        sm[2],
-        sm[3],
-        sm[4],
+        g_query,
+        vectors[0],
+        g_key,
+        g_value,
+        vectors[1],
+        g_mixer,
+        vectors[2],
+        vectors[3],
+        vectors[4],
         g_inner,
-        sm[9 : 9 + per].reshape(hidden),
-        g_outer.reshape(hidden, WIDTH),
-        sm[5],
-        sm[6],
-        sm[7],
-        sm[8],
+        vectors[9],
+        g_outer,
+        vectors[5],
+        vectors[6],
+        vectors[7],
+        vectors[8],
     )
 
 

time: 289 us -> 239 us (0.83)
  local copies, waits for them, and re-layouts: 22.6 us -> 0.62 us
  waiting for transfers between devices: 154 us -> 135 us
  other arithmetic: 6.99 us -> 3.61 us
  matrix products: 2.9 us -> 0 us
    ppermute x9 -> x10, waiting for transfers between devices: 61.8 us -> 9.74 us  [swap_x(): return lax.ppermute(value, 'seq', [(0, 1), (1, 0)])]
    ppermute x21 -> x18, waiting for transfers between devices: 52 us -> 93.4 us  [shift_z(): return lax.ppermute(value, 'ctx', [(i, (i + 4 * k) % n) for i in range(n)])]
    ppermute x25 -> x24, waiting for transfers between devices: 40.4 us -> 31.5 us  [swap_ctx(): return lax.ppermute(value, 'ctx', [(i, i ^ bit) for i in range(n)])]
    concatenate x4 -> x1, local copies, waits for them, and re-layouts: 7.58 us -> 0.02 us  [join(): jnp.concatenate([both[:, base + j * HALF:base + (j + 1) * HALF] for j in...]
    unnamed x41 -> x9, local copies, waits for them, and re-layouts: 7.39 us -> 0.04 us
    ppermute x21 -> x18, starting transfers between devices: 31.6 us -> 26.5 us  [shift_z(): return lax.ppermute(value, 'ctx', [(i, (i + 4 * k) % n) for i in range(n)])]
    pallas_call x12 -> x13, Pallas kernels: 11 us -> 15.2 us  [kernel(): pl.pallas_call(body, in_specs=[pl.BlockSpec(memory_space=pltpu.VMEM) for...]
    ppermute x9 -> x10, starting transfers between devices: 9.6 us -> 13.6 us  [swap_x(): return lax.ppermute(value, 'seq', [(0, 1), (1, 0)])]
  transfers between devices with their start and end apart: 55 -> 52, of which waited for: 28 -> 28; matrix products, arithmetic and copies ran while one was open for 9% -> 1% of each run, Pallas kernels for 11% -> 14%
where the time goes in v4:
time: 239 us; the launch traced here: 237 us
  waiting for transfers between devices  135 us (56%)
  starting transfers between devices  53.7 us (22%)
  Pallas kernels  43 us (18%)
  other arithmetic  3.61 us (2%)
    ppermute x18, waiting for transfers between devices, shift_z(): return lax.ppermute(value, 'ctx', [(i, (i + 4 * k) % n) for i in range(n)])  93.4 us
    ppermute x24, waiting for transfers between devices, swap_ctx(): return lax.ppermute(value, 'ctx', [(i, i ^ bit) for i in range(n)])  31.5 us
    ppermute x18, starting transfers between devices, shift_z(): return lax.ppermute(value, 'ctx', [(i, (i + 4 * k) % n) for i in range(n)])  26.5 us
    pallas_call x13, Pallas kernels, kernel(): pl.pallas_call(body, in_specs=[pl.BlockSpec(memory_space=pltpu.VMEM) for...  15.2 us
    ppermute x24, starting transfers between devices, swap_ctx(): return lax.ppermute(value, 'ctx', [(i, i ^ bit) for i in range(n)])  13.6 us
    ppermute x10, starting transfers between devices, swap_x(): return lax.ppermute(value, 'seq', [(0, 1), (1, 0)])  13.6 us
    ppermute x10, waiting for transfers between devices, swap_x(): return lax.ppermute(value, 'seq', [(0, 1), (1, 0)])  9.74 us
    pallas_call x1, Pallas kernels, attend_first(): pl.pallas_call(body, grid=(keys // block,), in_specs=[whole_spec(tokens,...  6.44 us
  transfers between devices with their start and end apart: 52, of which 28 were waited for; matrix products, arithmetic and copies ran while one was open for 1% of the time, Pallas kernels for 14%

profile of v4, /device:TPU:0, one launch (start us, length us, event | category | flops | bytes accessed | tf_op | source)
XLA Modules:
  0.0 237.0 jit_solution(11750244736316547145)
XLA Ops:
  0.7 2.1 pack.1
  5.6 2.9 %collective-permute-start.2 = (bf16[1,384,384]{2,1,0:T(8,128)(2,1)S(1)}, bf16[1,384,384]{2,1,0:T(8,128)(2,1)S(1)}, u32[]{:S(2)}, u32[]{:S(2)}) collective-permute-start(bf16[1,384,384]{2,1,0:T(8,128)(2,1)S(1)} %bitcast.76), channel_id=1, source_target_pairs={{0,16},{16,0},{1,17},{17,1},{2,18},{18,2},{3,19},{19,3},{4,20},{20... | collective-permute-start | bytes 884744 | tf_op jit(solution)/shard_map/ppermute | solution.py:55
  10.0 3.7 %collective-permute-start.5 = (bf16[48,1664]{1,0:T(8,128)(2,1)S(1)}, bf16[48,1664]{1,0:T(8,128)(2,1)S(1)}, u32[]{:S(2)}, u32[]{:S(2)}) collective-permute-start(bf16[48,1664]{1,0:T(8,128)(2,1)S(1)} %pad_maximum_fusion.8), channel_id=1, source_target_pairs={{0,12},{1,13},{2,14},{3,15},{4,0},{5,1},{6,2},{7,3},{8,4},{9,5},{1... | collective-permute-start | bytes 479240 | tf_op jit(solution)/shard_map/ppermute | solution.py:60
  14.7 3.6 %collective-permute-done.5 = bf16[48,1664]{1,0:T(8,128)(2,1)S(1)} collective-permute-done((bf16[48,1664]{1,0:T(8,128)(2,1)S(1)}, bf16[48,1664]{1,0:T(8,128)(2,1)S(1)}, u32[]{:S(2)}, u32[]{:S(2)}) %collective-permute-start.5) | collective-permute-done | bytes 159776 | tf_op jit(solution)/shard_map/ppermute | solution.py:60
  18.3 8.7 %collective-permute-done.4 = bf16[48,1664]{1,0:T(8,128)(2,1)S(1)} collective-permute-done((bf16[48,1664]{1,0:T(8,128)(2,1)S(1)}, bf16[48,1664]{1,0:T(8,128)(2,1)S(1)}, u32[]{:S(2)}, u32[]{:S(2)}) %collective-permute-start.4) | collective-permute-done | bytes 159776 | tf_op jit(solution)/shard_map/ppermute | solution.py:60
  31.3 2.0 collective-permute-start.8
  33.3 1.8 collective-permute-done.10
  35.1 12.7 %collective-permute-done.9 = bf16[128,768]{1,0:T(8,128)(2,1)S(1)} collective-permute-done((bf16[128,768]{1,0:T(8,128)(2,1)S(1)}, bf16[128,768]{1,0:T(8,128)(2,1)S(1)}, u32[]{:S(2)}, u32[]{:S(2)}) %collective-permute-start.9) | collective-permute-done | bytes 196640 | tf_op jit(solution)/shard_map/ppermute | solution.py:60
  53.1 2.2 collective-permute-done.12.refs_3_
  55.5 4.0 %collective-permute-done.16 = bf16[384,384]{1,0:T(8,128)(2,1)S(1)} collective-permute-done((bf16[384,384]{1,0:T(8,128)(2,1)S(1)}, bf16[384,384]{1,0:T(8,128)(2,1)S(1)}, u32[]{:S(2)}, u32[]{:S(2)}) %collective-permute-start.16) | collective-permute-done | bytes 294944 | tf_op jit(solution)/shard_map/ppermute | solution.py:60
  59.4 18.0 %collective-permute-done.15 = bf16[384,384]{1,0:T(8,128)(2,1)S(1)} collective-permute-done((bf16[384,384]{1,0:T(8,128)(2,1)S(1)}, bf16[384,384]{1,0:T(8,128)(2,1)S(1)}, u32[]{:S(2)}, u32[]{:S(2)}) %collective-permute-start.15) | collective-permute-done | bytes 294944 | tf_op jit(solution)/shard_map/ppermute | solution.py:60
  82.5 6.4 %attend_first.1 = (bf16[256,384]{1,0:T(8,128)(2,1)S(1)}, bf16[1024,768]{1,0:T(8,128)(2,1)S(1)}, f32[16,768]{1,0:T(8,128)S(1)}, f32[8,384]{1,0:T(8,128)S(1)}, f32...) custom-call(bf16[128,768]{1,0:T(8,128)(2,1)S(1)} %bitcast.72, ...), custom_call_target="tpu_custom_call" | custom-call | flops 1 | bytes 1 | tf_op jit(solution)/shard_map/attend_first/pallas_call | solution.py:361
  89.0 6.2 %attend_last.1 = (bf16[1024,768]{1,0:T(8,128)(2,1)S(1)}, f32[384,256]{1,0:T(8,128)S(1)}, bf16[256,384]{1,0:T(8,128)(2,1)S(1)}, f32[8,256]{1,0:T(8,128)S(1)}) custom-call(bf16[256,384]{1,0:T(8,128)(2,1)S(1)} %get-tuple-element.187.q_ref, bf16[1024,768]{1,0:T(8,128)(2,1)S(1)} %collective-permute-done.20.x_ref.refs_13_, ...), custom_call_target="tpu_custom_call" | custom-call | flops 1 | bytes 1 | tf_op jit(solution)/shard_map/attend_last/pallas_call | solution.py:418
  95.2 4.8 %collective-permute-done.18.refs_7_ = bf16[3,384,384]{2,1,0:T(8,128)(2,1)S(1)} collective-permute-done((bf16[3,384,384]{2,1,0:T(8,128)(2,1)S(1)}, bf16[3,384,384]{2,1,0:T(8,128)(2,1)S(1)}, u32[]{:S(2)}, u32[]{:S(2)}) %collective-permute-start.18) | collective-permute-done | bytes 884768 | tf_op jit(solution)/shard_map/ppermute | solution.py:55
  104.7 8.5 %collective-permute-done.25.refs_9_ = bf16[3,192,384]{2,1,0:T(8,128)(2,1)S(1)} collective-permute-done((bf16[3,192,384]{2,1,0:T(8,128)(2,1)S(1)}, bf16[3,192,384]{2,1,0:T(8,128)(2,1)S(1)}, u32[]{:S(2)}, u32[]{:S(2)}) %collective-permute-start.25) | collective-permute-done | bytes 442400 | tf_op jit(solution)/shard_map/ppermute | solution.py:43
  115.1 1.8 feed.1
  129.2 4.7 %attend_back_first.1 = (bf16[1024,768]{1,0:T(8,128)(2,1)S(1)}, bf16[256,384]{1,0:T(8,128)(2,1)S(1)}, f32[8,256]{1,0:T(8,128)S(1)}, f32[384,256]{1,0:T(8,128)S(1)}, f32[8,384]{1,0:T(8,128)S(1)}) custom-call(bf16[256,384]{1,0:T(8,128)(2,1)S(1)} %get-tuple-element.187.q_ref, bf16[128,768]{1,0:T(8,128)(2,1)S(1)} %get-tuple-element.223.go_ref.refs_9_, ...), custom_call_target="tpu_custom_call" | custom-call | flops 1 | bytes 1 | tf_op jit(solution)/shard_map/attend_back_first/pallas_call | solution.py:746
  133.9 6.7 %collective-permute-done.31 = bf16[4,96,768]{2,1,0:T(8,128)(2,1)S(1)} collective-permute-done((bf16[4,96,768]{2,1,0:T(8,128)(2,1)S(1)}, bf16[4,96,768]{2,1,0:T(8,128)(2,1)S(1)}, u32[]{:S(2)}, u32[]{:S(2)}) %collective-permute-start.31) | collective-permute-done | bytes 589856 | tf_op jit(solution)/shard_map/ppermute | solution.py:43
  145.9 4.9 %attend_back_last.1 = (bf16[1024,768]{1,0:T(8,128)(2,1)S(1)}, bf16[256,384]{1,0:T(8,128)(2,1)S(1)}, f32[8,384]{1,0:T(8,128)S(1)}, bf16[128,768]{1,0:T(8,128)(2,1)S(1)}) custom-call(bf16[256,384]{1,0:T(8,128)(2,1)S(1)} %get-tuple-element.187.q_ref, bf16[256,384]{1,0:T(8,128)(2,1)S(1)} %get-tuple-element.228.g_ref, f32[8,256]{1,0:T(8,128)S(1)} %get-tuple-element.226.lse_ref, ...), custom_call_target="tpu_custom_call" | custom-call | flops 1 | bytes 1 | tf_op jit(solution)/shard_map/attend_back_last/pallas_call | solution.py:797
  152.3 2.1 input_part_own.1
  154.5 3.5 %spread_qkv.1 = (bf16[4,48,1664]{2,1,0:T(8,128)(2,1)S(1)}, bf16[4,48,1664]{2,1,0:T(8,128)(2,1)S(1)}, bf16[4,48,1664]{2,1,0:T(8,128)(2,1)S(1)}, bf16[4,48,1664]{2,1,0:T(8,128)(2,1)S(1)}) custom-call(bf16[128,768]{1,0:T(8,128)(2,1)S(1)} %bitcast.74, bf16[128,768]{1,0:T(8,128)(2,1)S(1)} %collective-permute-done.19.g_ref.refs_1_, ...), custom_call_target="tpu_custom_call" | custom-call | flops 1 | bytes 1 | tf_op jit(solution)/shard_map/spread_qkv/pallas_call | solution.py:167
  157.9 7.0 %collective-permute-done.34 = bf16[3,192,768]{2,1,0:T(8,128)(2,1)S(1)} collective-permute-done((bf16[3,192,768]{2,1,0:T(8,128)(2,1)S(1)}, bf16[3,192,768]{2,1,0:T(8,128)(2,1)S(1)}, u32[]{:S(2)}, u32[]{:S(2)}) %collective-permute-start.34) | collective-permute-done | bytes 884768 | tf_op jit(solution)/shard_map/ppermute | solution.py:43
  168.9 1.9 collective-permute-start.38
  170.9 6.7 %collective-permute-done.40.refs_9_ = bf16[192,768]{1,0:T(8,128)(2,1)S(1)} collective-permute-done((bf16[192,768]{1,0:T(8,128)(2,1)S(1)}, bf16[192,768]{1,0:T(8,128)(2,1)S(1)}, u32[]{:S(2)}, u32[]{:S(2)}) %collective-permute-start.40) | collective-permute-done | bytes 294944 | tf_op jit(solution)/shard_map/ppermute | solution.py:60
  177.6 16.2 %collective-permute-done.39.refs_8_ = bf16[192,768]{1,0:T(8,128)(2,1)S(1)} collective-permute-done((bf16[192,768]{1,0:T(8,128)(2,1)S(1)}, bf16[192,768]{1,0:T(8,128)(2,1)S(1)}, u32[]{:S(2)}, u32[]{:S(2)}) %collective-permute-start.39) | collective-permute-done | bytes 294944 | tf_op jit(solution)/shard_map/ppermute | solution.py:60
  197.1 2.0 collective-permute-start.44
  199.1 2.8 %collective-permute-start.43 = (bf16[128,768]{1,0:T(8,128)(2,1)S(1)}, bf16[128,768]{1,0:T(8,128)(2,1)S(1)}, u32[]{:S(2)}, u32[]{:S(2)}) collective-permute-start(bf16[128,768]{1,0:T(8,128)(2,1)S(1)} %get-tuple-element.314), channel_id=1, source_target_pairs={{0,12},{1,13},{2,14},{3,15},{4,0},{5,1},{6,2},{7,3},{8,4},{9,5},{1... | collective-permute-start | bytes 589832 | tf_op jit(solution)/shard_map/ppermute | solution.py:60
  202.0 4.1 %collective-permute-done.45 = bf16[128,768]{1,0:T(8,128)(2,1)S(1)} collective-permute-done((bf16[128,768]{1,0:T(8,128)(2,1)S(1)}, bf16[128,768]{1,0:T(8,128)(2,1)S(1)}, u32[]{:S(2)}, u32[]{:S(2)}) %collective-permute-start.45) | collective-permute-done | bytes 196640 | tf_op jit(solution)/shard_map/ppermute | solution.py:60
  206.1 6.1 %collective-permute-done.44 = bf16[128,768]{1,0:T(8,128)(2,1)S(1)} collective-permute-done((bf16[128,768]{1,0:T(8,128)(2,1)S(1)}, bf16[128,768]{1,0:T(8,128)(2,1)S(1)}, u32[]{:S(2)}, u32[]{:S(2)}) %collective-permute-start.44) | collective-permute-done | bytes 196640 | tf_op jit(solution)/shard_map/ppermute | solution.py:60
  214.4 6.7 %collective-permute-start.50 = (bf16[48,1664]{1,0:T(8,128)(2,1)S(1)}, bf16[48,1664]{1,0:T(8,128)(2,1)S(1)}, u32[]{:S(2)}, u32[]{:S(2)}) collective-permute-start(bf16[48,1664]{1,0:T(8,128)(2,1)S(1)} %get-tuple-element.315), channel_id=1, source_target_pairs={{0,12},{1,13},{2,14},{3,15},{4,0},{5,1},{6,2},{7,3},{8,4},{9,5},{1... | collective-permute-start | bytes 479240 | tf_op jit(solution)/shard_map/ppermute | solution.py:60
  221.8 3.9 %collective-permute-done.50.refs_3_ = bf16[48,1664]{1,0:T(8,128)(2,1)S(1)} collective-permute-done((bf16[48,1664]{1,0:T(8,128)(2,1)S(1)}, bf16[48,1664]{1,0:T(8,128)(2,1)S(1)}, u32[]{:S(2)}, u32[]{:S(2)}) %collective-permute-start.50) | collective-permute-done | bytes 159776 | tf_op jit(solution)/shard_map/ppermute | solution.py:60
  225.7 7.6 %collective-permute-done.49.refs_2_ = bf16[48,1664]{1,0:T(8,128)(2,1)S(1)} collective-permute-done((bf16[48,1664]{1,0:T(8,128)(2,1)S(1)}, bf16[48,1664]{1,0:T(8,128)(2,1)S(1)}, u32[]{:S(2)}, u32[]{:S(2)}) %collective-permute-start.49) | collective-permute-done | bytes 159776 | tf_op jit(solution)/shard_map/ppermute | solution.py:60
  (138 shorter events, 59.4 us)
Async XLA Ops:
  5.6 21.4 %collective-permute-start.2 = (bf16[1,384,384]{2,1,0:T(8,128)(2,1)S(1)}, bf16[1,384,384]{2,1,0:T(8,128)(2,1)S(1)}, u32[]{:S(2)}, u32[]{:S(2)}) collective-permute-start(bf16[1,384,384]{2,1,0:T(8,128)(2,1)S(1)} %bitcast.76), channel_id=1, source_target_pairs={{0,16},{16,0},{1,17},{17,1},{2,18},{18,2},{3,19},{19,3},{4,20},{20... | collective-permute-start | bytes 884744 | tf_op jit(solution)/shard_map/ppermute | solution.py:55
  8.5 18.5 %collective-permute-start.1 = (bf16[1,384,384]{2,1,0:T(8,128)(2,1)S(1)}, bf16[1,384,384]{2,1,0:T(8,128)(2,1)S(1)}, u32[]{:S(2)}, u32[]{:S(2)}) collective-permute-start(bf16[1,384,384]{2,1,0:T(8,128)(2,1)S(1)} %bitcast.77), channel_id=1, source_target_pairs={{0,2},{1,3},{2,0},{3,1},{4,6},{5,7},{6,4},{7,5},{8,10},{9,11},{10,... | collective-permute-start | bytes 884744 | tf_op jit(solution)/shard_map/ppermute | solution.py:43
  13.7 13.3 %collective-permute-start.4 = (bf16[48,1664]{1,0:T(8,128)(2,1)S(1)}, bf16[48,1664]{1,0:T(8,128)(2,1)S(1)}, u32[]{:S(2)}, u32[]{:S(2)}) collective-permute-start(bf16[48,1664]{1,0:T(8,128)(2,1)S(1)} %pad_maximum_fusion.8), channel_id=1, source_target_pairs={{0,8},{1,9},{2,10},{3,11},{4,12},{5,13},{6,14},{7,15},{8,0},{9,1},... | collective-permute-start | bytes 479240 | tf_op jit(solution)/shard_map/ppermute | solution.py:60
  13.7 13.3 %collective-permute-start.3 = (bf16[48,1664]{1,0:T(8,128)(2,1)S(1)}, bf16[48,1664]{1,0:T(8,128)(2,1)S(1)}, u32[]{:S(2)}, u32[]{:S(2)}) collective-permute-start(bf16[48,1664]{1,0:T(8,128)(2,1)S(1)} %pad_maximum_fusion.8), channel_id=1, source_target_pairs={{0,4},{1,5},{2,6},{3,7},{4,8},{5,9},{6,10},{7,11},{8,12},{9,13},{1... | collective-permute-start | bytes 479240 | tf_op jit(solution)/shard_map/ppermute | solution.py:60
  27.3 20.4 %collective-permute-start.7 = (bf16[192,2048]{1,0:T(8,128)(2,1)S(1)}, bf16[192,2048]{1,0:T(8,128)(2,1)S(1)}, u32[]{:S(2)}, u32[]{:S(2)}) collective-permute-start(bf16[192,2048]{1,0:T(8,128)(2,1)S(1)} %get-tuple-element.319), channel_id=1, source_target_pairs={{0,16},{16,0},{1,17},{17,1},{2,18},{18,2},{3,19},{19,3},{4,20},{20... | collective-permute-start | bytes 2359304 | tf_op jit(solution)/shard_map/ppermute | solution.py:55
  27.9 19.8 %collective-permute-start.6 = (bf16[192,2048]{1,0:T(8,128)(2,1)S(1)}, bf16[192,2048]{1,0:T(8,128)(2,1)S(1)}, u32[]{:S(2)}, u32[]{:S(2)}) collective-permute-start(bf16[192,2048]{1,0:T(8,128)(2,1)S(1)} %get-tuple-element.320), channel_id=1, source_target_pairs={{0,2},{1,3},{2,0},{3,1},{4,6},{5,7},{6,4},{7,5},{8,10},{9,11},{10,... | collective-permute-start | bytes 2359304 | tf_op jit(solution)/shard_map/ppermute | solution.py:43
  29.6 18.2 %collective-permute-start.9 = (bf16[128,768]{1,0:T(8,128)(2,1)S(1)}, bf16[128,768]{1,0:T(8,128)(2,1)S(1)}, u32[]{:S(2)}, u32[]{:S(2)}) collective-permute-start(bf16[128,768]{1,0:T(8,128)(2,1)S(1)} %bitcast.69), channel_id=1, source_target_pairs={{0,8},{1,9},{2,10},{3,11},{4,12},{5,13},{6,14},{7,15},{8,0},{9,1},... | collective-permute-start | bytes 589832 | tf_op jit(solution)/shard_map/ppermute | solution.py:60
  31.3 16.5 %collective-permute-start.8 = (bf16[128,768]{1,0:T(8,128)(2,1)S(1)}, bf16[128,768]{1,0:T(8,128)(2,1)S(1)}, u32[]{:S(2)}, u32[]{:S(2)}) collective-permute-start(bf16[128,768]{1,0:T(8,128)(2,1)S(1)} %bitcast.70), channel_id=1, source_target_pairs={{0,4},{1,5},{2,6},{3,7},{4,8},{5,9},{6,10},{7,11},{8,12},{9,13},{1... | collective-permute-start | bytes 589832 | tf_op jit(solution)/shard_map/ppermute | solution.py:60
  47.9 29.6 %collective-permute-start.11 = (bf16[4,128,768]{2,1,0:T(8,128)(2,1)S(1)}, bf16[4,128,768]{2,1,0:T(8,128)(2,1)S(1)}, u32[]{:S(2)}, u32[]{:S(2)}) collective-permute-start(bf16[4,128,768]{2,1,0:T(8,128)(2,1)S(1)} %pad_maximum_fusion.4), channel_id=1, source_target_pairs={{0,2},{1,3},{2,0},{3,1},{4,6},{5,7},{6,4},{7,5},{8,10},{9,11},{10,... | collective-permute-start | bytes 2359304 | tf_op jit(solution)/shard_map/ppermute | solution.py:43
  51.1 26.4 %collective-permute-start.13 = (bf16[4,32,1664]{2,1,0:T(8,128)(2,1)S(1)}, bf16[4,32,1664]{2,1,0:T(8,128)(2,1)S(1)}, u32[]{:S(2)}, u32[]{:S(2)}) collective-permute-start(bf16[4,32,1664]{2,1,0:T(8,128)(2,1)S(1)} %slice.161), channel_id=1, source_target_pairs={{0,2},{1,3},{2,0},{3,1},{4,6},{5,7},{6,4},{7,5},{8,10},{9,11},{10,... | collective-permute-start | bytes 1277960 | tf_op jit(solution)/shard_map/ppermute | solution.py:43
  51.6 25.8 %collective-permute-start.15 = (bf16[384,384]{1,0:T(8,128)(2,1)S(1)}, bf16[384,384]{1,0:T(8,128)(2,1)S(1)}, u32[]{:S(2)}, u32[]{:S(2)}) collective-permute-start(bf16[384,384]{1,0:T(8,128)(2,1)S(1)} %slice_dynamic-update-slice_fusion), channel_id=1, source_target_pairs={{0,8},{1,9},{2,10},{3,11},{4,12},{5,13},{6,14},{7,15},{8,0},{9,1},... | collective-permute-start | bytes 884744 | tf_op jit(solution)/shard_map/ppermute | solution.py:60
  55.3 22.2 %collective-permute-start.14 = (bf16[384,384]{1,0:T(8,128)(2,1)S(1)}, bf16[384,384]{1,0:T(8,128)(2,1)S(1)}, u32[]{:S(2)}, u32[]{:S(2)}) collective-permute-start(bf16[384,384]{1,0:T(8,128)(2,1)S(1)} %slice_dynamic-update-slice_fusion), channel_id=1, source_target_pairs={{0,4},{1,5},{2,6},{3,7},{4,8},{5,9},{6,10},{7,11},{8,12},{9,13},{1... | collective-permute-start | bytes 884744 | tf_op jit(solution)/shard_map/ppermute | solution.py:60
  77.8 22.1 %collective-permute-start.18 = (bf16[3,384,384]{2,1,0:T(8,128)(2,1)S(1)}, bf16[3,384,384]{2,1,0:T(8,128)(2,1)S(1)}, u32[]{:S(2)}, u32[]{:S(2)}) collective-permute-start(bf16[3,384,384]{2,1,0:T(8,128)(2,1)S(1)} %pad_maximum_fusion.1.refs_5_), channel_id=1, source_target_pairs={{0,16},{16,0},{1,17},{17,1},{2,18},{18,2},{3,19},{19,3},{4,20},{20... | collective-permute-start | bytes 2654216 | tf_op jit(solution)/shard_map/ppermute | solution.py:55
  78.6 21.8 %collective-permute-start.17 = (bf16[3,384,384]{2,1,0:T(8,128)(2,1)S(1)}, bf16[3,384,384]{2,1,0:T(8,128)(2,1)S(1)}, u32[]{:S(2)}, u32[]{:S(2)}) collective-permute-start(bf16[3,384,384]{2,1,0:T(8,128)(2,1)S(1)} %pad_maximum_fusion.1.refs_5_), channel_id=1, source_target_pairs={{0,2},{1,3},{2,0},{3,1},{4,6},{5,7},{6,4},{7,5},{8,10},{9,11},{10,... | collective-permute-start | bytes 2654216 | tf_op jit(solution)/shard_map/ppermute | solution.py:43
  80.2 23.2 %collective-permute-start.22 = (bf16[768,384]{1,0:T(8,128)(2,1)S(1)}, bf16[768,384]{1,0:T(8,128)(2,1)S(1)}, u32[]{:S(2)}, u32[]{:S(2)}) collective-permute-start(bf16[768,384]{1,0:T(8,128)(2,1)S(1)} %get-tuple-element.194.mo_ref), channel_id=1, source_target_pairs={{0,1},{1,0},{2,3},{3,2},{4,5},{5,4},{6,7},{7,6},{8,9},{9,8},{10,11... | collective-permute-start | bytes 1769480 | tf_op jit(solution)/shard_map/ppermute | solution.py:43
  100.5 12.6 %collective-permute-start.25 = (bf16[3,192,384]{2,1,0:T(8,128)(2,1)S(1)}, bf16[3,192,384]{2,1,0:T(8,128)(2,1)S(1)}, u32[]{:S(2)}, u32[]{:S(2)}) collective-permute-start(bf16[3,192,384]{2,1,0:T(8,128)(2,1)S(1)} %slice.136), channel_id=1, source_target_pairs={{0,2},{1,3},{2,0},{3,1},{4,6},{5,7},{6,4},{7,5},{8,10},{9,11},{10,... | collective-permute-start | bytes 1327112 | tf_op jit(solution)/shard_map/ppermute | solution.py:43
  101.9 12.3 %collective-permute-start.24 = (bf16[3,192,384]{2,1,0:T(8,128)(2,1)S(1)}, bf16[3,192,384]{2,1,0:T(8,128)(2,1)S(1)}, u32[]{:S(2)}, u32[]{:S(2)}) collective-permute-start(bf16[3,192,384]{2,1,0:T(8,128)(2,1)S(1)} %slice.135), channel_id=1, source_target_pairs={{0,16},{16,0},{1,17},{17,1},{2,18},{18,2},{3,19},{19,3},{4,20},{20... | collective-permute-start | bytes 1327112 | tf_op jit(solution)/shard_map/ppermute | solution.py:55
  124.9 15.7 %collective-permute-start.31 = (bf16[4,96,768]{2,1,0:T(8,128)(2,1)S(1)}, bf16[4,96,768]{2,1,0:T(8,128)(2,1)S(1)}, u32[]{:S(2)}, u32[]{:S(2)}) collective-permute-start(bf16[4,96,768]{2,1,0:T(8,128)(2,1)S(1)} %get-tuple-element.307), channel_id=1, source_target_pairs={{0,2},{1,3},{2,0},{3,1},{4,6},{5,7},{6,4},{7,5},{8,10},{9,11},{10,... | collective-permute-start | bytes 1769480 | tf_op jit(solution)/shard_map/ppermute | solution.py:43
  125.6 15.3 %collective-permute-start.30 = (bf16[4,96,768]{2,1,0:T(8,128)(2,1)S(1)}, bf16[4,96,768]{2,1,0:T(8,128)(2,1)S(1)}, u32[]{:S(2)}, u32[]{:S(2)}) collective-permute-start(bf16[4,96,768]{2,1,0:T(8,128)(2,1)S(1)} %get-tuple-element.308), channel_id=1, source_target_pairs={{0,16},{16,0},{1,17},{17,1},{2,18},{18,2},{3,19},{19,3},{4,20},{20... | collective-permute-start | bytes 1769480 | tf_op jit(solution)/shard_map/ppermute | solution.py:55
  142.8 22.1 %collective-permute-start.34 = (bf16[3,192,768]{2,1,0:T(8,128)(2,1)S(1)}, bf16[3,192,768]{2,1,0:T(8,128)(2,1)S(1)}, u32[]{:S(2)}, u32[]{:S(2)}) collective-permute-start(bf16[3,192,768]{2,1,0:T(8,128)(2,1)S(1)} %fusion.1), channel_id=1, source_target_pairs={{0,2},{1,3},{2,0},{3,1},{4,6},{5,7},{6,4},{7,5},{8,10},{9,11},{10,... | collective-permute-start | bytes 2654216 | tf_op jit(solution)/shard_map/ppermute | solution.py:43
  144.4 21.8 %collective-permute-start.35 = (bf16[3,192,768]{2,1,0:T(8,128)(2,1)S(1)}, bf16[3,192,768]{2,1,0:T(8,128)(2,1)S(1)}, u32[]{:S(2)}, u32[]{:S(2)}) collective-permute-start(bf16[3,192,768]{2,1,0:T(8,128)(2,1)S(1)} %fusion), channel_id=1, source_target_pairs={{0,16},{16,0},{1,17},{17,1},{2,18},{18,2},{3,19},{19,3},{4,20},{20... | collective-permute-start | bytes 2654216 | tf_op jit(solution)/shard_map/ppermute | solution.py:55
  166.2 27.6 %collective-permute-start.36 = (bf16[4,48,1664]{2,1,0:T(8,128)(2,1)S(1)}, bf16[4,48,1664]{2,1,0:T(8,128)(2,1)S(1)}, u32[]{:S(2)}, u32[]{:S(2)}) collective-permute-start(bf16[4,48,1664]{2,1,0:T(8,128)(2,1)S(1)} %get-tuple-element.255), channel_id=1, source_target_pairs={{0,16},{16,0},{1,17},{17,1},{2,18},{18,2},{3,19},{19,3},{4,20},{20... | collective-permute-start | bytes 1916936 | tf_op jit(solution)/shard_map/ppermute | solution.py:55
  167.7 26.1 %collective-permute-start.37 = (bf16[4,128,768]{2,1,0:T(8,128)(2,1)S(1)}, bf16[4,128,768]{2,1,0:T(8,128)(2,1)S(1)}, u32[]{:S(2)}, u32[]{:S(2)}) collective-permute-start(bf16[4,128,768]{2,1,0:T(8,128)(2,1)S(1)} %bitcast.82), channel_id=1, source_target_pairs={{0,2},{1,3},{2,0},{3,1},{4,6},{5,7},{6,4},{7,5},{8,10},{9,11},{10,... | collective-permute-start | bytes 2359304 | tf_op jit(solution)/shard_map/ppermute | solution.py:43
  168.5 25.3 %collective-permute-start.39 = (bf16[192,768]{1,0:T(8,128)(2,1)S(1)}, bf16[192,768]{1,0:T(8,128)(2,1)S(1)}, u32[]{:S(2)}, u32[]{:S(2)}) collective-permute-start(bf16[192,768]{1,0:T(8,128)(2,1)S(1)} %get-tuple-element.310), channel_id=1, source_target_pairs={{0,8},{1,9},{2,10},{3,11},{4,12},{5,13},{6,14},{7,15},{8,0},{9,1},... | collective-permute-start | bytes 884744 | tf_op jit(solution)/shard_map/ppermute | solution.py:60
  168.9 24.9 %collective-permute-start.38 = (bf16[192,768]{1,0:T(8,128)(2,1)S(1)}, bf16[192,768]{1,0:T(8,128)(2,1)S(1)}, u32[]{:S(2)}, u32[]{:S(2)}) collective-permute-start(bf16[192,768]{1,0:T(8,128)(2,1)S(1)} %get-tuple-element.311), channel_id=1, source_target_pairs={{0,4},{1,5},{2,6},{3,7},{4,8},{5,9},{6,10},{7,11},{8,12},{9,13},{1... | collective-permute-start | bytes 884744 | tf_op jit(solution)/shard_map/ppermute | solution.py:60
  194.0 18.1 %collective-permute-start.41 = (bf16[4,48,1664]{2,1,0:T(8,128)(2,1)S(1)}, bf16[4,48,1664]{2,1,0:T(8,128)(2,1)S(1)}, u32[]{:S(2)}, u32[]{:S(2)}) collective-permute-start(bf16[4,48,1664]{2,1,0:T(8,128)(2,1)S(1)} %add.46), channel_id=1, source_target_pairs={{0,2},{1,3},{2,0},{3,1},{4,6},{5,7},{6,4},{7,5},{8,10},{9,11},{10,... | collective-permute-start | bytes 1916936 | tf_op jit(solution)/shard_map/ppermute | solution.py:43
  195.6 16.6 %collective-permute-start.42 = (bf16[4,48,1664]{2,1,0:T(8,128)(2,1)S(1)}, bf16[4,48,1664]{2,1,0:T(8,128)(2,1)S(1)}, u32[]{:S(2)}, u32[]{:S(2)}) collective-permute-start(bf16[4,48,1664]{2,1,0:T(8,128)(2,1)S(1)} %get-tuple-element.265), channel_id=1, source_target_pairs={{0,16},{16,0},{1,17},{17,1},{2,18},{18,2},{3,19},{19,3},{4,20},{20... | collective-permute-start | bytes 1916936 | tf_op jit(solution)/shard_map/ppermute | solution.py:55
  197.1 15.1 %collective-permute-start.44 = (bf16[128,768]{1,0:T(8,128)(2,1)S(1)}, bf16[128,768]{1,0:T(8,128)(2,1)S(1)}, u32[]{:S(2)}, u32[]{:S(2)}) collective-permute-start(bf16[128,768]{1,0:T(8,128)(2,1)S(1)} %get-tuple-element.313), channel_id=1, source_target_pairs={{0,8},{1,9},{2,10},{3,11},{4,12},{5,13},{6,14},{7,15},{8,0},{9,1},... | collective-permute-start | bytes 589832 | tf_op jit(solution)/shard_map/ppermute | solution.py:60
  199.1 13.1 %collective-permute-start.43 = (bf16[128,768]{1,0:T(8,128)(2,1)S(1)}, bf16[128,768]{1,0:T(8,128)(2,1)S(1)}, u32[]{:S(2)}, u32[]{:S(2)}) collective-permute-start(bf16[128,768]{1,0:T(8,128)(2,1)S(1)} %get-tuple-element.314), channel_id=1, source_target_pairs={{0,12},{1,13},{2,14},{3,15},{4,0},{5,1},{6,2},{7,3},{8,4},{9,5},{1... | collective-permute-start | bytes 589832 | tf_op jit(solution)/shard_map/ppermute | solution.py:60
  212.2 21.1 %collective-permute-start.46 = (bf16[1,192,768]{2,1,0:T(8,128)(2,1)S(1)}, bf16[1,192,768]{2,1,0:T(8,128)(2,1)S(1)}, u32[]{:S(2)}, u32[]{:S(2)}) collective-permute-start(bf16[1,192,768]{2,1,0:T(8,128)(2,1)S(1)} %pad_maximum_fusion.7), channel_id=1, source_target_pairs={{0,2},{1,3},{2,0},{3,1},{4,6},{5,7},{6,4},{7,5},{8,10},{9,11},{10,... | collective-permute-start | bytes 884744 | tf_op jit(solution)/shard_map/ppermute | solution.py:43
  212.9 20.4 %collective-permute-start.47 = (bf16[1,192,768]{2,1,0:T(8,128)(2,1)S(1)}, bf16[1,192,768]{2,1,0:T(8,128)(2,1)S(1)}, u32[]{:S(2)}, u32[]{:S(2)}) collective-permute-start(bf16[1,192,768]{2,1,0:T(8,128)(2,1)S(1)} %pad_maximum_fusion.6), channel_id=1, source_target_pairs={{0,16},{16,0},{1,17},{17,1},{2,18},{18,2},{3,19},{19,3},{4,20},{20... | collective-permute-start | bytes 884744 | tf_op jit(solution)/shard_map/ppermute | solution.py:55
  221.1 12.2 %collective-permute-start.49 = (bf16[48,1664]{1,0:T(8,128)(2,1)S(1)}, bf16[48,1664]{1,0:T(8,128)(2,1)S(1)}, u32[]{:S(2)}, u32[]{:S(2)}) collective-permute-start(bf16[48,1664]{1,0:T(8,128)(2,1)S(1)} %get-tuple-element.316), channel_id=1, source_target_pairs={{0,8},{1,9},{2,10},{3,11},{4,12},{5,13},{6,14},{7,15},{8,0},{9,1},... | collective-permute-start | bytes 479240 | tf_op jit(solution)/shard_map/ppermute | solution.py:60
  (24 other events, 135.6 us)
